TPU v7x, 32 devices: a whole 2x2x4 slice. The times are simulated.
32 devices in a mesh: expert: 4 (over z), tensor: 4 (over y, x), rep: 2 (over core).
Axes of the slice: x: 2, y: 2, z: 4, core: 2. Of those that a mesh axis runs over, the one named last changes fastest.
Arguments:
- tokens: bfloat16 [8, 1024, 768], P(('expert', 'rep'), 'tensor'), may hold values from -16 to 16
- segments: int32 [8, 1024], P(('expert', 'rep')), may hold values from 0 to 2, as said below
- routes: int32 [8, 1024, 2], P(('expert', 'rep'), 'tensor'), may hold values from 0 to 63, all different within a row
- capacity: int32 [64], replicated, may hold values from 6 to 12, as said below
- cotangent: bfloat16 [8, 1024, 768], P(('expert', 'rep'), 'tensor'), may hold values from -6 to 6
- rel_table: bfloat16 [32, 12], P('expert', 'tensor'), may hold values from -4 to 4
- w_query: bfloat16 [768, 768], P('expert', 'tensor'), may hold values from -0.21875 to 0.21875
- w_key: bfloat16 [768, 768], P('expert', 'tensor'), may hold values from -0.21875 to 0.21875
- w_value: bfloat16 [768, 768], P('expert', 'tensor'), may hold values from -0.21875 to 0.21875
- w_attn_out: bfloat16 [768, 768], P('expert', 'tensor'), may hold values from -0.875 to 0.875
- gain_attn: bfloat16 [768], P('expert'), may hold values from 0.5 to 1.5
- gain_moe: bfloat16 [768], P('expert'), may hold values from 0.5 to 1.5
- w_router: bfloat16 [768, 64], P('expert'), may hold values from -0.15625 to 0.15625
- w_in: bfloat16 [64, 768, 3072], P('expert', None, 'tensor'), may hold values from -0.21875 to 0.21875
- w_out: bfloat16 [64, 3072, 768], P('expert', 'tensor'), may hold values from -0.109375 to 0.109375
Outputs:
- output: bfloat16 [8, 1024, 768], P(('expert', 'rep'), 'tensor')
- grad_tokens: float32 [8, 1024, 768], P(('expert', 'rep'), 'tensor')
- grad_table: float32 [32, 12], P('expert', 'tensor')
- grad_query: float32 [768, 768], P('expert', 'tensor')
- grad_key: float32 [768, 768], P('expert', 'tensor')
- grad_value: float32 [768, 768], P('expert', 'tensor')
- grad_attn_out: float32 [768, 768], P('expert', 'tensor')
- grad_gain_attn: float32 [768], P('expert')
- grad_gain_moe: float32 [768], P('expert')
- grad_router: float32 [768, 64], P('expert')
- grad_w_in: float32 [64, 768, 3072], P('expert', None, 'tensor')
- grad_w_out: float32 [64, 3072, 768], P('expert', 'tensor')
Inputs may be any that keep to these rules, and one draw needn't show every extreme that they name: `segments`: segment numbers never fall along a sequence. Each sequence holds the tail of a document (fewer than 128 positions), one whole document that begins before position 128 and ends within the last 256 positions, and the head of another document. `routes`: the two experts of a token differ. `capacity`: some expert has all 12 slots.
All inputs are finite; a program needn't handle non-finite values.
Results may differ from a plain program's by a relative error of at most 0.025.
Values may be sent and summed in bfloat16 or wider, within the bound.
No kernel may reach another device: no remote copies, remote signals or barrier semaphores. Data moves between devices by JAX's collectives and lax.ppermute only.
A program may use at most 384 MiB of HBM per device.

v0:
```python
import functools
import math

import jax
import jax.numpy as jnp
from jax import lax
from jax.experimental import pallas as pl
from jax.experimental.pallas import tpu as pltpu
from jax.sharding import PartitionSpec as P

HEAD = 64
CAP = 12
QB = 128
epsilon = 1e-06
masked_value = -1e30
thresholds = (16, 19, 21, 24, 27, 31, 35, 40, 46, 52, 59, 67, 77, 87, 99, 113)
lowest = tuple(range(16)) + thresholds
f32 = jnp.float32
bf16 = jnp.bfloat16
i32 = jnp.int32
NN = (((1,), (0,)), ((), ()))
NT = (((1,), (1,)), ((), ()))
TN = (((0,), (0,)), ((), ()))
VM = pl.BlockSpec(memory_space=pltpu.VMEM)
SM = pl.BlockSpec(memory_space=pltpu.SMEM)
sd = jax.ShapeDtypeStruct


def dot(a, b, dims=NN):
    return lax.dot_general(a, b, dims, preferred_element_type=f32)


def call(kernel, name, outs, operands, scratch=(), smem=0, flops=0, moved=4_000_000, alias=None):
    return pl.pallas_call(
        kernel,
        out_shape=tuple(outs),
        in_specs=[SM] * smem + [VM] * (len(operands) - smem),
        out_specs=tuple(VM for _ in outs),
        scratch_shapes=list(scratch),
        compiler_params=pltpu.CompilerParams(vmem_limit_bytes=56 << 20),
        cost_estimate=pl.CostEstimate(flops=flops, bytes_accessed=moved, transcendentals=0),
        name=name,
    )(*operands)


def to_tensor(a, flip):
    return lax.ppermute(a, "tensor", [(i, i ^ flip) for i in range(4)])


def to_expert(a, shift, size):
    return lax.ppermute(a, "expert", [(i, (i + shift) % size) for i in range(size)])


def to_core(a):
    return lax.ppermute(a, "rep", [(0, 1), (1, 0)])


def shifted(blocks):
    size = len(blocks)
    return [blocks[0]] + [to_expert(blocks[k], k, size) for k in range(1, size)]


def gather_pieces(own, half):
    px = to_tensor(own, 1)
    py = to_tensor(own, 2)
    d0 = to_tensor(px[:half], 2)
    d1 = to_tensor(py[half:], 1)
    return own, px, py, d0, d1


def scatter_pieces(pack_x, pack_y, x_late, y_late):
    got_x = to_tensor(pack_x, 1)
    got_y = to_tensor(pack_y, 2)
    late_x = to_tensor((x_late.astype(f32) + got_y[0].astype(f32)).astype(bf16), 1)
    late_y = to_tensor((y_late.astype(f32) + got_x[0].astype(f32)).astype(bf16), 2)
    return got_x, late_y, got_y, late_x


def add_parts(own, got_x, late_y, got_y, late_x):
    half = late_y.shape[0]
    first = own[0:half, :].astype(f32) + got_x[1].astype(f32) + late_y[...].astype(f32)
    second = own[half:, :].astype(f32) + got_y[1].astype(f32) + late_x[...].astype(f32)
    return first, second


def onehot(index, width):
    return lax.broadcasted_iota(i32, (index.shape[0], width), 1) == index


def as_bf16(mask):
    return jnp.where(mask, 1.0, 0.0).astype(bf16)


def prepare_kernel(size, chunks, me_ref, routes_ref, capacity_ref, cot_ref, idx_ref, *g_refs):
    count = routes_ref.shape[0]
    experts = capacity_ref.shape[1]
    local = experts // size
    part = local // chunks
    me = me_ref[0]
    first, second = routes_ref[:, 0:1], routes_ref[:, 1:2]
    both = as_bf16(onehot(first, experts)) + as_bf16(onehot(second, experts))
    rows = lax.broadcasted_iota(i32, (count, count), 0)
    cols = lax.broadcasted_iota(i32, (count, count), 1)
    before = dot(as_bf16(cols < rows), both)
    capacity = capacity_ref[...].astype(f32)
    shift = int(math.log2(local))
    columns = []
    for route in (first, second):
        mine = onehot(route, experts)
        position = jnp.sum(jnp.where(mine, before, 0.0), axis=1, keepdims=True)
        limit = jnp.sum(jnp.where(mine, jnp.broadcast_to(capacity, mine.shape), 0.0), axis=1, keepdims=True)
        keep = position < limit
        position = position.astype(i32)
        owner = lax.shift_right_logical(route, jnp.full_like(route, shift))
        inner = route & (local - 1)
        away = (owner - me + size) & (size - 1)
        chunk = lax.shift_right_logical(inner, jnp.full_like(route, int(math.log2(part))))
        slot = ((chunk * size + away) * part + (inner & (part - 1))) * CAP + position
        columns += [route, jnp.where(keep, slot, -1), jnp.where(keep, away * local + inner, -1), away * CAP + position]
    for n, column in enumerate(columns):
        idx_ref[:, n:n + 1] = column
    width = experts * CAP
    spread = as_bf16(onehot(columns[1], width)) + as_bf16(onehot(columns[5], width))
    slots = dot(spread, cot_ref[...], TN).astype(bf16)
    rows_of = part * CAP
    for k in range(size):
        for c in range(chunks):
            g_refs[k][c * rows_of:(c + 1) * rows_of, :] = slots[(c * size + k) * rows_of:(c * size + k + 1) * rows_of]


def order_matrix(size, part, block, extra, out_extra):
    rows = part * size * CAP
    m = [[0.0] * (size * block) for _ in range(rows + out_extra)]
    for e in range(part):
        for k in range(size):
            for c in range(CAP):
                m[(e * size + k) * CAP + c][k * block + e * CAP + c] = 1.0
    for r in range(extra):
        for k in range(size):
            m[rows + r][k * block + part * CAP + r] = 1.0
    return jnp.array(m, dtype=bf16)


def reorder_kernel(count, m_ref, *refs):
    blocks, out_ref = refs[:count], refs[count]
    out_ref[...] = dot(m_ref[...], jnp.concatenate([b[...] for b in blocks], axis=0)).astype(bf16)


def reorder(matrix, blocks, name):
    rows = matrix.shape[0]
    width = blocks[0].shape[1]
    return call(functools.partial(reorder_kernel, len(blocks)), name, [sd((rows, width), bf16)], (matrix, *blocks),
                flops=2 * matrix.size * width, moved=2 * rows * width * 2)[0]


def give_back_kernel(count, extra, m_ref, *refs):
    if extra:
        extra_ref, refs = refs[0], refs[1:]
    own, got_x, late_y, got_y, late_x = refs[:5]
    outs = refs[5:]
    first, second = add_parts(own, got_x, late_y, got_y, late_x)
    rows = jnp.concatenate([first.astype(bf16), second.astype(bf16)], axis=0)
    back = dot(m_ref[...], rows, TN).astype(bf16)
    block = back.shape[0] // count
    for k in range(count):
        outs[k][0:block, :] = back[k * block:(k + 1) * block]
        if extra:
            outs[k][block:, :] = extra_ref[...]


def plain_back_kernel(count, m_ref, rows_ref, *outs):
    back = dot(m_ref[...], rows_ref[...], TN).astype(bf16)
    block = back.shape[0] // count
    for k in range(count):
        outs[k][...] = back[k * block:(k + 1) * block]


def unpack_kernel(size, at_ref, *refs):
    mine, other = refs[:size], refs[size:2 * size]
    full, qkv_ref, wo_ref, router_ref, gains_ref, table_ref = refs[2 * size:]
    me, rep = at_ref[0], at_ref[1]
    half = mine[0].shape[0]
    for k in range(size):
        z = (me - k + size) & (size - 1)
        full[2 * z + rep] = mine[k][...].astype(f32)
        full[2 * z + 1 - rep] = other[k][...].astype(f32)
    full = jnp.concatenate([full[n] for n in range(2 * size)], axis=0)
    qkv_ref[...] = full[:, 0:576].astype(bf16)
    router_ref[...] = full[:, 576:640].astype(bf16)
    wo_ref[...] = full[:, 640:832].astype(bf16)
    tail = full[:, 768:896]
    turned = tail.T
    gains_ref[...] = turned[64:72, :]
    rows = table_ref.shape[0] // size
    for z in range(size):
        table_ref[z * rows:(z + 1) * rows, :] = tail[z * 2 * half: z * 2 * half + rows, :]


def unpack(at, mine, other, buckets):
    size = len(mine)
    half, cols = mine[0].shape
    width = 2 * half * size

    def kernel(at_ref, *refs):
        unpack_kernel(size, at_ref, *refs[:2 * size], refs[-1], *refs[2 * size:-1])

    outs = [sd((width, 576), bf16), sd((width, 192), bf16), sd((width, 64), bf16), sd((8, width), f32), sd((buckets, 128), f32)]
    return call(kernel, "unpack", outs, (at, *mine, *other), scratch=[pltpu.VMEM((2 * size, half, cols), f32)], smem=1)


def put_pieces(part, tok, own, pack_x, pack_y, x_late, y_late):
    half = tok // 2
    own[...] = part(0, 0, tok)
    pack_x[0] = part(3, 0, half)
    pack_x[1] = part(1, 0, half)
    pack_y[0] = part(3, half, half)
    pack_y[1] = part(2, half, half)
    x_late[...] = part(1, half, half)
    y_late[...] = part(2, 0, half)


def piece_shapes(rows, width):
    half = rows // 2
    return [sd((rows, width), bf16), sd((2, half, width), bf16), sd((2, half, width), bf16), sd((half, width), bf16), sd((half, width), bf16)]


def near_offset():
    rows = lax.broadcasted_iota(jnp.int32, (QB, 2 * QB), 0)
    cols = lax.broadcasted_iota(jnp.int32, (QB, 2 * QB), 1)
    return QB + rows - cols


def near_bias(table_ref, head, buckets):
    off = near_offset()
    bias = jnp.where(off < 0, masked_value, table_ref[0, head])
    for b in range(1, buckets):
        bias = jnp.where(off >= lowest[b], table_ref[b, head], bias)
    return bias


def scores_of(q, k_ref, head, i, near, far, seg_col, seg_row_ref):
    lo = max(i - 1, 0) * QB
    hi = (i + 1) * QB
    s = dot(q, k_ref[head, 0:hi], NT)
    bias = near[:, QB:] if i == 0 else near
    same_near = seg_col == seg_row_ref[:, lo:hi]
    s_near = jnp.where(same_near, s[:, lo:hi] + bias, masked_value)
    if lo == 0:
        return s_near
    same_far = seg_col == seg_row_ref[:, 0:lo]
    s_far = jnp.where(same_far, s[:, 0:lo] + far, masked_value)
    return jnp.concatenate([s_far, s_near], axis=1)


def attn_fwd_kernel(heads, at_ref, table_ref, own_ref, px_ref, py_ref, pd0_ref, pd1_ref, segc_ref, segr_ref, w_ref, wo_ref, gain_ref,
                    xn_ref, qkv_ref, o_ref, lse_ref, out_own, out_px, out_py, out_x, out_y, qs, ks, vs):
    pos = at_ref[2]
    tok = own_ref.shape[0]
    half = tok // 2
    buckets = table_ref.shape[0]
    gain = gain_ref[0:1, :]

    def norm(rows):
        x = rows.astype(f32)
        r = lax.rsqrt(jnp.mean(x * x, axis=-1, keepdims=True) + epsilon)
        return (x * r * gain).astype(bf16)

    def at(flip, start=0, size=tok):
        return pl.ds(pl.multiple_of((pos ^ flip) * tok + start, half), size)

    xn_ref[at(0), :] = norm(own_ref[...])
    xn_ref[at(1), :] = norm(px_ref[...])
    xn_ref[at(2), :] = norm(py_ref[...])
    xn_ref[at(3, 0, half), :] = norm(pd0_ref[...])
    xn_ref[at(3, half, half), :] = norm(pd1_ref[...])
    qkv = dot(xn_ref[...], w_ref[...]).astype(bf16)
    qkv_ref[...] = qkv
    width = heads * HEAD
    for h in range(heads):
        qs[h] = qkv[:, h * HEAD:(h + 1) * HEAD] * bf16(0.125)
        ks[h] = qkv[:, width + h * HEAD: width + (h + 1) * HEAD]
        vs[h] = qkv[:, 2 * width + h * HEAD: 2 * width + (h + 1) * HEAD]
    blocks = xn_ref.shape[0] // QB
    for h in range(heads):
        near = near_bias(table_ref, h, buckets)
        far = table_ref[buckets - 1, h]
        for i in range(blocks):
            rows = slice(i * QB, (i + 1) * QB)
            s = scores_of(qs[h, rows], ks, h, i, near, far, segc_ref[rows, :], segr_ref)
            top = jnp.max(s, axis=-1, keepdims=True)
            e = jnp.exp(s - top)
            total = jnp.sum(e, axis=-1, keepdims=True)
            p = (e * (1.0 / total)).astype(bf16)
            o_ref[rows, h * HEAD:(h + 1) * HEAD] = dot(p, vs[h, 0:(i + 1) * QB]).astype(bf16)
            lse_ref[rows, h:h + 1] = top + jnp.log(total)
    wo = wo_ref[...]
    put_pieces(lambda flip, start, size: dot(o_ref[at(flip, start, size), :], wo, NT).astype(bf16), tok, out_own, out_px, out_py, out_x, out_y)


def attn_bwd_kernel(heads, size, at_ref, table_ref, own_ref, px_ref, py_ref, pd0_ref, pd1_ref, segc_ref, segr_ref, w_ref, wo_ref,
                    xn_ref, qkv_ref, o_ref, lse_ref, keep_ref, send_ref, gain_ref, gtab_ref, out_own, out_px, out_py, out_x, out_y,
                    dh, qs, ks, vs, do, dk, dv, dqkv, acc, full):
    pos = at_ref[2]
    rep = at_ref[1]
    tok = own_ref.shape[0]
    half = tok // 2
    buckets = table_ref.shape[0]
    width = heads * HEAD

    def at(flip, start=0, size=tok):
        return pl.ds(pl.multiple_of((pos ^ flip) * tok + start, half), size)

    dh[at(0), :] = own_ref[...]
    dh[at(1), :] = px_ref[...]
    dh[at(2), :] = py_ref[...]
    dh[at(3, 0, half), :] = pd0_ref[...]
    dh[at(3, half, half), :] = pd1_ref[...]
    dall = dot(dh[...], wo_ref[...]).astype(bf16)
    for h in range(heads):
        do[h] = dall[:, h * HEAD:(h + 1) * HEAD]
        qs[h] = qkv_ref[:, h * HEAD:(h + 1) * HEAD] * bf16(0.125)
        ks[h] = qkv_ref[:, width + h * HEAD: width + (h + 1) * HEAD]
        vs[h] = qkv_ref[:, 2 * width + h * HEAD: 2 * width + (h + 1) * HEAD]
    blocks = xn_ref.shape[0] // QB
    off = near_offset()
    for h in range(heads):
        near = near_bias(table_ref, h, buckets)
        far = table_ref[buckets - 1, h]
        acc[...] = jnp.zeros_like(acc)
        dk[...] = jnp.zeros_like(dk)
        dv[...] = jnp.zeros_like(dv)
        far_sum = jnp.zeros((QB, 1), f32)
        for i in range(blocks):
            rows = slice(i * QB, (i + 1) * QB)
            lo = max(i - 1, 0) * QB
            hi = (i + 1) * QB
            q = qs[h, rows]
            s = scores_of(q, ks, h, i, near, far, segc_ref[rows, :], segr_ref)
            p = jnp.exp(s - lse_ref[rows, h:h + 1])
            g = do[h, rows]
            dv[0:hi] += dot(p.astype(bf16), g, TN)
            dp = dot(g, vs[h, 0:hi], NT)
            pd = p * dp
            ds = (pd - p * jnp.sum(pd, axis=-1, keepdims=True)).astype(bf16)
            dq = dot(ds, ks[h, 0:hi]) * 0.125
            dqkv[rows, h * HEAD:(h + 1) * HEAD] = dq.astype(bf16)
            dk[0:hi] += dot(ds, q, TN)
            dsf = ds.astype(f32)
            if i == 0:
                acc[:, QB:] += dsf
            else:
                acc[...] += dsf[:, lo:hi]
            if lo > 0:
                far_sum = far_sum + jnp.sum(dsf[:, 0:lo], axis=-1, keepdims=True)
        dqkv[:, width + h * HEAD: width + (h + 1) * HEAD] = dk[...].astype(bf16)
        dqkv[:, 2 * width + h * HEAD: 2 * width + (h + 1) * HEAD] = dv[...].astype(bf16)
        total = acc[...]
        rest = jnp.sum(far_sum, axis=0, keepdims=True)
        for b in range(buckets):
            if b == buckets - 1:
                inside = off >= lowest[b]
            else:
                inside = (off >= lowest[b]) & (off < lowest[b + 1])
            part = jnp.sum(jnp.where(inside, total, 0.0), axis=0, keepdims=True)
            one = jnp.sum(part, axis=1, keepdims=True)
            gtab_ref[b:b + 1, h:h + 1] = one + rest if b == buckets - 1 else one
    w = w_ref[...]
    def part(flip, start, size):
        return dot(dqkv[at(flip, start, size), :], w, NT).astype(bf16)

    put_pieces(part, tok, out_own, out_px, out_py, out_x, out_y)
    grad = dot(xn_ref[...], dqkv[...], TN)
    gain_sum = jnp.sum(grad * w.astype(f32), axis=1, keepdims=True)
    gain_ref[...] = jnp.broadcast_to(gain_sum, (gain_sum.shape[0], 128)).T[0:8, :]
    grad_out = dot(dh[...], o_ref[...], TN)
    part_rows = keep_ref.shape[1]
    for n in range(2 * size):
        full[n, :, 0:3 * width] = grad[n * part_rows:(n + 1) * part_rows].astype(bf16)
        full[n, :, 3 * width:] = grad_out[n * part_rows:(n + 1) * part_rows].astype(bf16)
    for z in range(size):
        keep_ref[z] = full[2 * z + rep]
        send_ref[z] = full[2 * z + 1 - rep]


def attn_fwd(at, table, pieces, segc, segr, w, wo, gains):
    tok, width = pieces[0].shape
    length = segc.shape[0]
    heads = wo.shape[1] // HEAD
    outs = [sd((length, width), bf16), sd((length, 3 * heads * HEAD), bf16), sd((length, heads * HEAD), bf16), sd((length, heads), f32)]
    return call(functools.partial(attn_fwd_kernel, heads), "attn_fwd", outs + piece_shapes(tok, width),
                (at, table, *pieces, segc, segr, w, wo, gains),
                scratch=[pltpu.VMEM((heads, length, HEAD), bf16)] * 3, smem=2, flops=8_000_000_000, moved=10_000_000)


def attn_bwd(at, size, table, pieces, segc, segr, w, wo, xn, qkv, o, lse):
    tok, width = pieces[0].shape
    length = segc.shape[0]
    heads = wo.shape[1] // HEAD
    outs = [sd((size, width // (2 * size), 4 * heads * HEAD), bf16)] * 2 + [sd((8, width), f32), sd((table.shape[0], heads), f32)]
    scratch = [pltpu.VMEM((length, width), bf16)] + [pltpu.VMEM((heads, length, HEAD), bf16)] * 4 + [pltpu.VMEM((length, HEAD), f32)] * 2
    scratch += [pltpu.VMEM((length, 3 * heads * HEAD), bf16), pltpu.VMEM((QB, 2 * QB), f32), pltpu.VMEM((2 * size, width // (2 * size), 4 * heads * HEAD), bf16)]
    return call(functools.partial(attn_bwd_kernel, heads, size), "attn_bwd", outs + piece_shapes(tok, width),
                (at, table, *pieces, segc, segr, w, wo, xn, qkv, o, lse), scratch=scratch, smem=2, flops=16_000_000_000, moved=12_000_000)


def route_kernel(size, chunks, idx_ref, tokens_ref, own, got_x, late_y, got_y, late_x, router_ref, gains_ref, h_ref, xn_ref, probs_ref, gate_ref, *blocks):
    count, width = tokens_ref.shape
    experts = router_ref.shape[1]
    local = experts // size
    rows_of = local // chunks * CAP
    lanes = lanes_of(size)
    first, second = add_parts(own, got_x, late_y, got_y, late_x)
    h = tokens_ref[...].astype(f32) + jnp.concatenate([first, second], axis=0)
    r = lax.rsqrt(jnp.mean(h * h, axis=-1, keepdims=True) + epsilon)
    xn = (h * r * gains_ref[1:2, :]).astype(bf16)
    h_ref[...] = h
    xn_ref[...] = xn
    logits = dot(xn, router_ref[...])
    e = jnp.exp(logits - jnp.max(logits, axis=-1, keepdims=True))
    probs = e / jnp.sum(e, axis=-1, keepdims=True)
    probs_ref[...] = probs
    picked = [jnp.sum(jnp.where(onehot(idx_ref[:, 4 * j:4 * j + 1], experts), probs, 0.0), axis=-1, keepdims=True) for j in (0, 1)]
    total = picked[0] + picked[1]
    gates = [p / total for p in picked]
    gate_ref[:, 0:1], gate_ref[:, 1:2], gate_ref[:, 2:3] = gates[0], gates[1], total
    spread = as_bf16(onehot(idx_ref[:, 1:2], experts * CAP)) + as_bf16(onehot(idx_ref[:, 5:6], experts * CAP))
    slots = dot(spread, xn, TN).astype(bf16)
    held = jnp.zeros((experts, lanes), f32)
    for j in (0, 1):
        to = as_bf16(onehot(idx_ref[:, 4 * j + 2:4 * j + 3], experts))
        at = jnp.where(onehot(idx_ref[:, 4 * j + 3:4 * j + 4], lanes), gates[j], 0.0).astype(bf16)
        held = held + dot(to, at, TN)
    for c in range(chunks):
        for k in range(size):
            ref = blocks[c * size + k]
            ref[0:rows_of, :] = slots[(c * size + k) * rows_of:(c * size + k + 1) * rows_of]
            if c == 0:
                ref[rows_of:, :] = jnp.zeros((16, width), bf16)
                ref[rows_of:rows_of + local, 0:lanes] = held[k * local:(k + 1) * local].astype(bf16)


def lanes_of(size):
    return -(-size * CAP // 128) * 128


def route(idx, tokens, parts, router, gains, size, chunks):
    count, width = tokens.shape
    experts = router.shape[1]
    rows_of = experts // size // chunks * CAP
    outs = [sd((count, width), f32), sd((count, width), bf16), sd((count, experts), f32), sd((count, 8), f32)]
    for c in range(chunks):
        outs += [sd((rows_of + (16 if c == 0 else 0), width), bf16)] * size
    return call(functools.partial(route_kernel, size, chunks), "route", outs, (idx, tokens, *parts, router, gains),
                flops=400_000_000, moved=5_000_000)


def moe_kernel(rows, part, offset, more, at_ref, own, px, py, d0, d1, e_own, e_px, e_py, e_d, g_ref, win_ref, wout_ref, *refs):
    if more:
        refs = refs[2:]
    o_own, o_px, o_py, o_x, o_y, y_ref, dg_ref, acts = refs
    pos = at_ref[2]
    e, j = pl.program_id(0), pl.program_id(1)
    early = e < part // 2
    wide = e_own.shape[1]

    pick = lax.broadcasted_iota(i32, (16, wide), 0) == e + offset
    square = lax.broadcasted_iota(i32, (rows, wide), 0) + j * rows == lax.broadcasted_iota(i32, (rows, wide), 1)

    def gate_of(ref):
        row = jnp.sum(jnp.where(pick, ref[...].astype(f32), 0.0), axis=0, keepdims=True)
        return jnp.sum(jnp.where(square, jnp.broadcast_to(row, square.shape), 0.0), axis=1, keepdims=True)

    gate = jnp.concatenate([gate_of(r) for r in (e_own, e_px, e_py, e_d)], axis=0)
    far = jnp.where(early, d0[...].astype(f32), d1[...].astype(f32)).astype(bf16)
    s = jnp.concatenate([own[...], px[...], py[...], far], axis=0)

    def keep(n, value):
        for flip in range(4):
            acts[n, 0, flip] = value[flip * rows:(flip + 1) * rows]

    keep(0, s)
    g = jnp.concatenate([g_ref[pos ^ flip] for flip in range(4)], axis=0).astype(f32)
    win, wout = win_ref[0], wout_ref[0]
    dy = (g * gate).astype(bf16)
    keep(1, dy)
    a = dot(s, win)
    dhid = dot(dy, wout, NT)
    c = math.sqrt(2.0 / math.pi)
    t = jnp.tanh(a * (c + (c * 0.044715) * (a * a)))
    up = 0.5 + 0.5 * t
    hid = (a * up).astype(bf16)
    slope = up + (0.5 * a) * (1.0 - t * t) * (c + (3 * c * 0.044715) * (a * a))
    da = (dhid * slope).astype(bf16)
    keep(2, hid)
    keep(3, da)
    y = dot(hid, wout)
    ones = jnp.ones((8, y.shape[1]), bf16)
    sums = dot(ones, (y * g).astype(bf16), NT)
    yb = y.astype(bf16)
    dg_ref[...] = jnp.zeros_like(dg_ref)
    for flip in range(4):
        y_ref[pos ^ flip] = yb[flip * rows:(flip + 1) * rows]
        dg_ref[0, flip:flip + 1, 0:rows] = sums[0:1, flip * rows:(flip + 1) * rows]
    ds = dot(da, win, NT).astype(bf16)
    o_own[...] = ds[0:rows]

    @pl.when(early)
    def _():
        o_px[0] = ds[3 * rows:]
        o_px[1] = ds[rows:2 * rows]
        o_y[...] = ds[2 * rows:3 * rows]

    @pl.when(jnp.logical_not(early))
    def _():
        o_py[0] = ds[3 * rows:]
        o_py[1] = ds[2 * rows:3 * rows]
        o_x[...] = ds[rows:2 * rows]


def moe(at, size, chunk, part, pieces, extras, g, w_in, w_out, before):
    all_rows = size * CAP
    rows = 128 if all_rows % 128 == 0 else all_rows
    steps = all_rows // rows
    local, width, hidden = w_in.shape
    half = part // 2
    lanes = -(-all_rows // 128) * 128
    lo = lambda e, j: jnp.where(e < half, e * steps + j, half * steps - 1)
    hi = lambda e, j: jnp.where(e < half, 0, (e - half) * steps + j)
    whole = lambda e, j: e * steps + j
    flat = lambda f: pl.BlockSpec((rows, width), lambda e, j: (f(e, j), 0))
    two = lambda f: pl.BlockSpec((2, rows, width), lambda e, j: (0, f(e, j), 0))
    first = chunk * part
    ext = lambda n: pl.BlockSpec((16, lanes), lambda e, j: (n // 16, 0))
    four = pl.BlockSpec((4, rows, width), lambda e, j: (0, (first + e) * steps + j, 0))
    in_specs = [SM, flat(whole), flat(whole), flat(whole), flat(lo), flat(hi)]
    in_specs += [ext(part * all_rows)] * 3 + [ext(half * all_rows), four]
    in_specs += [pl.BlockSpec((1, width, hidden), lambda e, j: (first + e, 0, 0)), pl.BlockSpec((1, hidden, width), lambda e, j: (first + e, 0, 0))]
    operands = [at, *pieces, *extras, g, w_in, w_out]
    alias = {}
    if before:
        alias = {len(operands): 5, len(operands) + 1: 6}
        operands += list(before)
        in_specs += [pl.BlockSpec(memory_space=pl.ANY)] * 2
    total, late = part * all_rows, half * all_rows
    outs = [sd((total, width), bf16), sd((2, late, width), bf16), sd((2, late, width), bf16), sd((late, width), bf16), sd((late, width), bf16),
            sd((4, local * all_rows, width), bf16), sd((local, 8, lanes), f32), sd((4, part, 4, all_rows, width), bf16)]
    out_specs = [flat(whole), two(lo), two(hi), flat(hi), flat(lo), four,
                 pl.BlockSpec((1, 8, lanes // steps), lambda e, j: (first + e, 0, j)),
                 pl.BlockSpec((4, 1, 4, rows, width), lambda e, j: (0, e, 0, j, 0))]
    return pl.pallas_call(
        functools.partial(moe_kernel, rows, part, first, bool(before)),
        grid=(part, steps),
        out_shape=tuple(outs), in_specs=in_specs, out_specs=tuple(out_specs),
        input_output_aliases=alias,
        compiler_params=pltpu.CompilerParams(vmem_limit_bytes=56 << 20),
        cost_estimate=pl.CostEstimate(flops=8 * part * 4 * all_rows * width * hidden, bytes_accessed=30_000_000, transcendentals=part * 4 * all_rows * hidden),
        name="moe",
    )(*operands)


def expert_grad_kernel(steps, at_ref, mine, other, *refs):
    gin, gout = refs[-2:]

    def put(a, b):
        both = [jnp.concatenate([r[n, 0, flip] for r in (a, b) for flip in range(4)], axis=0) for n in range(4)]
        for ref, left, right in ((gin, both[0], both[3]), (gout, both[2], both[1])):
            if steps == 1:
                ref[0] = dot(left, right, TN)
            else:
                part = dot(left, right, TN)
                ref[0] = jnp.where(pl.program_id(1) == 0, part, ref[0] + part)

    pl.when(at_ref[1] == 0)(lambda: put(mine, other))
    pl.when(at_ref[1] == 1)(lambda: put(other, mine))


def expert_grad(at, chunk, local, mine, other, before):
    part, four, all_rows, width = mine.shape[1:]
    rows = 128 if all_rows % 128 == 0 else all_rows
    steps = all_rows // rows
    spec = pl.BlockSpec((4, 1, 4, rows, width), lambda e, j: (0, e, 0, j, 0))
    in_specs = [SM, spec, spec]
    operands = [at, mine, other]
    alias = {}
    if before:
        alias = {3: 0, 4: 1}
        operands += list(before)
        in_specs += [pl.BlockSpec(memory_space=pl.ANY)] * 2
    out = pl.BlockSpec((1, width, width), lambda e, j: (chunk * part + e, 0, 0))
    return pl.pallas_call(
        functools.partial(expert_grad_kernel, steps),
        grid=(part, steps),
        out_shape=(sd((local, width, width), f32),) * 2, in_specs=in_specs, out_specs=(out, out),
        input_output_aliases=alias,
        compiler_params=pltpu.CompilerParams(vmem_limit_bytes=56 << 20),
        cost_estimate=pl.CostEstimate(flops=32 * part * all_rows * width * width,
                                      bytes_accessed=part * (64 * all_rows * width + 8 * width * width), transcendentals=0),
        name="expert_grad",
    )(*operands)


def back_kernel(size, chunks, idx_ref, cot_ref, h_ref, xn_ref, probs_ref, gate_ref, router_ref, gains_ref, *refs):
    blocks = refs[:chunks * size]
    dh_ref, dhb_ref, small_ref, ds = refs[chunks * size:]
    experts = router_ref.shape[1]
    local = experts // size
    rows_of = local // chunks * CAP
    lanes = lanes_of(size)
    for n, block in enumerate(blocks):
        ds[n * rows_of:(n + 1) * rows_of, :] = block[0:rows_of, :]
    last = blocks[(chunks - 1) * size:]
    held = jnp.concatenate([last[k][rows_of:rows_of + local, 0:lanes].astype(f32) for k in range(size)], axis=0).astype(bf16)
    spread = as_bf16(onehot(idx_ref[:, 1:2], experts * CAP)) + as_bf16(onehot(idx_ref[:, 5:6], experts * CAP))
    dxn = dot(spread, ds[...])
    probs = probs_ref[...]
    gates, dgates, chosen = [], [], []
    for j in (0, 1):
        got = dot(as_bf16(onehot(idx_ref[:, 4 * j + 2:4 * j + 3], experts)), held)
        dgates.append(jnp.sum(jnp.where(onehot(idx_ref[:, 4 * j + 3:4 * j + 4], lanes), got, 0.0), axis=-1, keepdims=True))
        gates.append(gate_ref[:, j:j + 1])
        chosen.append(onehot(idx_ref[:, 4 * j:4 * j + 1], experts))
    mean = gates[0] * dgates[0] + gates[1] * dgates[1]
    scale = 1.0 / gate_ref[:, 2:3]
    dprobs = jnp.where(chosen[0], (dgates[0] - mean) * scale, 0.0) + jnp.where(chosen[1], (dgates[1] - mean) * scale, 0.0)
    dlogits = (probs * (dprobs - jnp.sum(probs * dprobs, axis=-1, keepdims=True))).astype(bf16)
    small_ref[...] = jnp.zeros_like(small_ref)
    small_ref[:, 0:experts] = dot(xn_ref[...], dlogits, TN)
    dxn = dxn + dot(dlogits, router_ref[...], NT)
    h = h_ref[...]
    r = lax.rsqrt(jnp.mean(h * h, axis=-1, keepdims=True) + epsilon)
    gain_row = jnp.sum(dxn * h * r, axis=0, keepdims=True)
    small_ref[:, experts:experts + 1] = jnp.broadcast_to(gain_row, (8, gain_row.shape[1])).T[:, 0:1]
    scaled = dxn * gains_ref[1:2, :]
    dh = cot_ref[...].astype(f32) + r * scaled - h * (r * r * r) * jnp.mean(h * scaled, axis=-1, keepdims=True)
    dh_ref[...] = dh
    dhb_ref[...] = dh.astype(bf16)


def back(idx, cot, h, xn, probs, gate, router, gains, blocks, size, chunks):
    count, width = h.shape
    experts = router.shape[1]
    outs = [sd((count, width), f32), sd((count, width), bf16), sd((width, 128), f32)]
    return call(functools.partial(back_kernel, size, chunks), "back", outs, (idx, cot, h, xn, probs, gate, router, gains, *blocks),
                scratch=[pltpu.VMEM((experts * CAP, width), bf16)], flops=400_000_000, moved=6_000_000)


def mix_kernel(size, local, idx_ref, h_ref, gate_ref, *refs):
    blocks, out_ref, ys = refs[:size], refs[size], refs[size + 1]
    rows_of = local * CAP
    for k in range(size):
        ys[k * rows_of:(k + 1) * rows_of, :] = blocks[k][...]
    out = h_ref[...]
    for j in (0, 1):
        expert, lane = idx_ref[:, 4 * j + 2:4 * j + 3], idx_ref[:, 4 * j + 3:4 * j + 4]
        away = lax.shift_right_logical(expert, jnp.full_like(expert, int(math.log2(local))))
        slot = jnp.where(expert < 0, -1, expert * CAP + lane - away * CAP)
        out = out + gate_ref[:, j:j + 1] * dot(as_bf16(onehot(slot, rows_of * size)), ys[...])
    out_ref[...] = out.astype(bf16)


def mix(idx, h, gate, blocks, local):
    size = len(blocks)
    count, width = h.shape
    return call(functools.partial(mix_kernel, size, local), "mix", [sd((count, width), bf16)], (idx, h, gate, *blocks),
                scratch=[pltpu.VMEM((size * local * CAP, width), bf16)], flops=600_000_000, moved=3_000_000)[0]


def last_kernel(tokens_ref, dh_ref, own, got_x, late_y, got_y, late_x, gains_ref, out_ref):
    first, second = add_parts(own, got_x, late_y, got_y, late_x)
    x = tokens_ref[...].astype(f32)
    r = lax.rsqrt(jnp.mean(x * x, axis=-1, keepdims=True) + epsilon)
    scaled = jnp.concatenate([first, second], axis=0) * gains_ref[0:1, :]
    out_ref[...] = dh_ref[...] + r * scaled - x * (r * r * r) * jnp.mean(x * scaled, axis=-1, keepdims=True)


def total_kernel(*refs):
    out = refs[-1]
    out[...] = sum(r[...].astype(f32) for r in refs[:-1])


def finish_kernel(at_ref, mine_ref, other_ref, q_ref, k_ref, v_ref, o_ref, small_ref):
    half = mine_ref.shape[0]
    width = q_ref.shape[1]

    def put(first, second):
        for n, ref in enumerate((q_ref, k_ref, v_ref, o_ref)):
            ref[0:half, :] = first[:, n * width:(n + 1) * width]
            ref[half:, :] = second[:, n * width:(n + 1) * width]
        a, b = first[:, 4 * width:], second[:, 4 * width:]
        lane = lax.broadcasted_iota(i32, a.shape, 1)
        small_ref[0:half, :] = jnp.where(lane == 65, a + shift_lane(b), jnp.where(lane > 66, a + b, a))
        small_ref[half:, :] = jnp.where(lane == 65, b + shift_lane(a), b)

    def shift_lane(x):
        return jnp.broadcast_to(x[:, 66:67], x.shape)

    pl.when(at_ref[1] == 0)(lambda: put(mine_ref, other_ref))
    pl.when(at_ref[1] == 1)(lambda: put(other_ref, mine_ref))


def on_device(size, tokens, segments, routes, capacity, cotangent, rel_table, w_query, w_key, w_value, w_attn_out, gain_attn, gain_moe, w_router, w_in, w_out):
    z = lax.axis_index("expert").astype(i32)
    rep = lax.axis_index("rep").astype(i32)
    pos = lax.axis_index("tensor").astype(i32)
    at = jnp.stack([z, rep, pos])
    tok = tokens[0]
    cot = cotangent[0]
    count, width = tok.shape
    local = w_in.shape[0]
    experts = w_router.shape[1]
    chunks = 2 if local >= 4 else 1
    part = local // chunks
    rows_dev = w_query.shape[0]
    half = rows_dev // 2
    buckets = rel_table.shape[0] * size

    pieces = gather_pieces(tok, count // 2)
    table_rows = jnp.pad(rel_table, ((0, rows_dev - rel_table.shape[0]), (0, 59)))
    packed = jnp.concatenate([w_query, w_key, w_value, w_router, w_attn_out, gain_attn[:, None], gain_moe[:, None], table_rows], axis=1)
    mine = [lax.dynamic_slice_in_dim(packed, rep * half, half, axis=0)]
    mine += [to_expert(mine[0], k, size) for k in range(1, size)]
    other = [to_core(m) for m in mine]
    qkv_w, wo, router, gains, table_full = unpack(at, mine, other, buckets)
    table = table_full[:, 66:69]

    idx, *g_blocks = call(functools.partial(prepare_kernel, size, chunks), "prepare",
                          [sd((count, 8), i32)] + [sd((local * CAP, width), bf16)] * size,
                          (z[None], routes[0], capacity[None], cot), smem=1, flops=400_000_000)
    whole = order_matrix(size, local, local * CAP, 0, 0)
    g_own = reorder(whole, shifted(g_blocks), "order_g")
    g_all = lax.all_gather(g_own, "tensor", axis=0)

    segc, segr = segments[0][:, None], segments
    xn, qkv, o, lse, own, pack_x, pack_y, x_late, y_late = attn_fwd(at, table, pieces, segc, segr, qkv_w, wo, gains)
    parts = scatter_pieces(pack_x, pack_y, x_late, y_late)
    h, xn2, probs, gate, *blocks = route(idx, tok, (own, *parts), router, gains, size, chunks)

    extras = None
    before = ()
    acts, sums = [], []
    for c in range(chunks):
        extra = 16 if c == 0 else 0
        matrix = order_matrix(size, part, part * CAP + extra, extra, extra)
        ordered = reorder(matrix, shifted(blocks[c * size:(c + 1) * size]), "order")
        got = gather_pieces(ordered, part * CAP * size // 2)
        if c == 0:
            extras = (got[0], got[1], got[2], got[4])
        *scattered, y_full, dg_full, act = moe(at, size, c, part, got, extras, g_all, w_in, w_out, before)
        before = (y_full, dg_full)
        acts.append(act)
        sums.append((scattered[0], *scatter_pieces(*scattered[1:])))
    other_acts = [to_core(a) for a in acts]
    dg_x = to_tensor(dg_full, 1)
    dg_two = dg_full[:, 2] + dg_x[:, 3]
    dg = dg_full[:, 0] + dg_x[:, 1] + to_tensor(dg_two, 2)
    dg = jnp.pad(dg.astype(bf16), ((0, 16 - local), (0, width - dg.shape[1])))
    back_blocks = []
    for c in range(chunks):
        extra = c == chunks - 1
        matrix = order_matrix(size, part, part * CAP, 0, 0)
        outs = [sd((part * CAP + 16 * extra, width), bf16)] * size
        given = call(functools.partial(give_back_kernel, size, extra), "give_back", outs,
                     (matrix,) + ((dg,) if extra else ()) + sums[c], flops=300_000_000, moved=3_000_000)
        back_blocks += [given[0]] + [to_expert(given[k], size - k, size) for k in range(1, size)]
    dh, dhb, small = back(idx, cot, h, xn2, probs, gate, router, gains, back_blocks, size, chunks)

    y_own = lax.psum_scatter(y_full, "tensor", scatter_dimension=0)
    given = call(functools.partial(plain_back_kernel, size), "give_back_y", [sd((local * CAP, width), bf16)] * size,
                 (whole, y_own), flops=900_000_000, moved=3_000_000)
    y_blocks = [given[0]] + [to_expert(given[k], size - k, size) for k in range(1, size)]
    output = mix(idx, h, gate, y_blocks, local)

    grads = ()
    for c in range(chunks):
        grads = expert_grad(at, c, local, acts[c], other_acts[c], grads)

    dh_pieces = gather_pieces(dhb, count // 2)
    keep, send, gain_row, gtab, own, pack_x, pack_y, x_late, y_late = attn_bwd(at, size, table, dh_pieces, segc, segr, qkv_w, wo, xn, qkv, o, lse)
    parts = scatter_pieces(pack_x, pack_y, x_late, y_late)
    grad_tokens = call(last_kernel, "last", [sd((count, width), f32)], (tok, dh, own, *parts, gains), moved=3_000_000)[0]

    small = small + to_tensor(small, 1)
    small = small + to_tensor(small, 2)
    small = small + to_core(small)
    gain_row = gain_row + to_tensor(gain_row, 1)
    gain_row = gain_row + to_tensor(gain_row, 2)
    gain_col = gain_row[0].reshape(size, 2, half)
    got = to_core(send)
    out_blocks = []
    small_rows = small.reshape(size, 2, half, 128)
    gtab_rows = gtab.reshape(size, buckets // size, gtab.shape[1])
    for k in range(size):
        to = (z + k) & (size - 1)
        both = lax.dynamic_index_in_dim(keep, to, keepdims=False).astype(f32) + lax.dynamic_index_in_dim(got, to, keepdims=False).astype(f32)
        few = lax.dynamic_slice(small_rows, (to, rep, 0, 0), (1, 1, half, 128))[0, 0]
        gain_a = lax.dynamic_slice(gain_col, (to, rep, 0), (1, 1, half))[0, 0][:, None]
        gain_b = lax.dynamic_slice(gain_col, (to, 1 - rep, 0), (1, 1, half))[0, 0][:, None]
        rows = lax.dynamic_slice(gtab_rows, (to, 0, 0), (1, *gtab_rows.shape[1:]))[0]
        rows = jnp.pad(rows, ((0, half - rows.shape[0]), (0, 0)))
        tail = jnp.concatenate([few[:, :experts + 1], gain_a, gain_b, rows, few[:, experts + 6:]], axis=1)
        out_blocks.append(jnp.concatenate([both, tail], axis=1).astype(bf16))
    arrived = shifted(out_blocks)
    total = call(total_kernel, "total", [sd(out_blocks[0].shape, f32)], tuple(arrived))[0]
    swapped = to_core(total)
    lw = w_query.shape[1]
    grad_q, grad_k, grad_v, grad_o, few = call(finish_kernel, "finish", [sd((rows_dev, lw), f32)] * 4 + [sd((rows_dev, 128), f32)],
                                               (at, total, swapped), smem=1)
    grad_router = few[:, :experts]
    grad_gain_moe = few[:, experts]
    grad_gain_attn = few[:, experts + 1] / gain_attn.astype(f32)
    grad_table = few[:rel_table.shape[0], experts + 3:experts + 3 + rel_table.shape[1]]
    return (output[None], grad_tokens[None], grad_table, grad_q, grad_k, grad_v, grad_o, grad_gain_attn, grad_gain_moe, grad_router, grads[0], grads[1])


def solution(mesh):
    by_token = P(("expert", "rep"), "tensor", None)
    both = P("expert", "tensor")
    return jax.shard_map(
        functools.partial(on_device, mesh.shape["expert"]),
        mesh=mesh,
        in_specs=(by_token, P(("expert", "rep"), None), by_token, P(), by_token, both, both, both, both, both, P("expert"), P("expert"),
                  P("expert", None), P("expert", None, "tensor"), P("expert", "tensor", None)),
        out_specs=(by_token, by_token, both, both, both, both, both, P("expert"), P("expert"), P("expert", None),
                   P("expert", None, "tensor"), P("expert", "tensor", None)),
        check_vma=False,
    )
```

profile of v0, /device:TPU:1, one launch (start us, length us, event | category | flops | bytes accessed | tf_op | source)
XLA Modules:
  0.0 500.9 jit_solution(238560529782521711)
XLA Ops:
  17.3 5.7 %collective-permute-done.28.refs_1_ = bf16[192,768]{1,0:T(8,128)(2,1)S(1)} collective-permute-done((bf16[192,768]{1,0:T(8,128)(2,1)}, bf16[192,768]{1,0:T(8,128)(2,1)S(1)}, u32[]{:S(2)}, u32[]{:S(2)}) %collective-permute-start.28) | collective-permute-done | bytes 294944 | tf_op jit(solution)/shard_map/ppermute | solution.py:51
  23.0 13.3 %collective-permute-done.29.refs_2_ = bf16[192,768]{1,0:T(8,128)(2,1)S(1)} collective-permute-done((bf16[192,768]{1,0:T(8,128)(2,1)}, bf16[192,768]{1,0:T(8,128)(2,1)S(1)}, u32[]{:S(2)}, u32[]{:S(2)}) %collective-permute-start.29) | collective-permute-done | bytes 294944 | tf_op jit(solution)/shard_map/ppermute | solution.py:51
  49.1 7.5 %collective-permute-start.2 = (bf16[96,896]{1,0:T(8,128)(2,1)S(1)}, bf16[96,896]{1,0:T(8,128)(2,1)S(1)}, u32[]{:S(2)}, u32[]{:S(2)}) collective-permute-start(bf16[96,896]{1,0:T(8,128)(2,1)S(1)} %constant_dynamic-slice_fusion.12.refs_0_), channel_id=1, source_target_pairs={{0,24},{8,0},{16,8},{24,16},{1,25},{9,1},{17,9},{25,17},{2,26},{10... | collective-permute-start | bytes 516104 | tf_op jit(solution)/shard_map/ppermute | solution.py:51
  64.3 8.0 %collective-permute-done.1.refs_2_ = bf16[96,896]{1,0:T(8,128)(2,1)S(1)} collective-permute-done((bf16[96,896]{1,0:T(8,128)(2,1)S(1)}, bf16[96,896]{1,0:T(8,128)(2,1)S(1)}, u32[]{:S(2)}, u32[]{:S(2)}) %collective-permute-start.1) | collective-permute-done | bytes 172064 | tf_op jit(solution)/shard_map/ppermute | solution.py:51
  82.0 15.4 %attn_fwd.1 = (bf16[1024,768]{1,0:T(8,128)(2,1)}, bf16[1024,576]{1,0:T(8,128)(2,1)}, bf16[1024,192]{1,0:T(8,128)(2,1)}, f32[1024,3]{1,0:T(8,128)}, bf16[256,768]...) custom-call(s32[3]{0:T(128)} %pad_add_fusion.at_ref, ...), custom_call_target="tpu_custom_call" | custom-call | flops 8000000000 | bytes 10000000 | tf_op jit(solution)/shard_map/attn_fwd/pallas_call | solution.py:34
  98.5 17.2 %collective-permute-done.11.got_x = bf16[2,128,768]{2,1,0:T(8,128)(2,1)S(1)} collective-permute-done((bf16[2,128,768]{2,1,0:T(8,128)(2,1)}, bf16[2,128,768]{2,1,0:T(8,128)(2,1)S(1)}, u32[]{:S(2)}, u32[]{:S(2)}) %collective-permute-start.11) | collective-permute-done | bytes 393248 | tf_op jit(solution)/shard_map/ppermute | solution.py:47
  136.2 7.8 %collective-permute-done.23.refs_2_ = bf16[112,768]{1,0:T(8,128)(2,1)S(1)} collective-permute-done((bf16[112,768]{1,0:T(8,128)(2,1)}, bf16[112,768]{1,0:T(8,128)(2,1)S(1)}, u32[]{:S(2)}, u32[]{:S(2)}) %collective-permute-start.23) | collective-permute-done | bytes 172064 | tf_op jit(solution)/shard_map/ppermute | solution.py:51
  155.5 8.7 %collective-permute-done.16.refs_2_ = bf16[96,768]{1,0:T(8,128)(2,1)S(1)} collective-permute-done((bf16[96,768]{1,0:T(8,128)(2,1)}, bf16[96,768]{1,0:T(8,128)(2,1)S(1)}, u32[]{:S(2)}, u32[]{:S(2)}) %collective-permute-start.16) | collective-permute-done | bytes 147488 | tf_op jit(solution)/shard_map/ppermute | solution.py:51
  170.5 11.4 %collective-permute-done.19.py = bf16[384,768]{1,0:T(8,128)(2,1)S(1)} collective-permute-done((bf16[384,768]{1,0:T(8,128)(2,1)}, bf16[384,768]{1,0:T(8,128)(2,1)S(1)}, u32[]{:S(2)}, u32[]{:S(2)}) %collective-permute-start.19) | collective-permute-done | bytes 589856 | tf_op jit(solution)/shard_map/ppermute | solution.py:47
  189.7 18.7 %moe.2 = (bf16[384,768]{1,0:T(8,128)(2,1)}, bf16[2,192,768]{2,1,0:T(8,128)(2,1)}, bf16[2,192,768]{2,1,0:T(8,128)(2,1)}, bf16[192,768]{1,0:T(8,128)(2,1)}, bf16[1...) custom-call(s32[3]{0:T(128)} %pad_add_fusion.at_ref, ...), custom_call_target="tpu_custom_call" | custom-call | flops 7247757312 | bytes 30000000 | tf_op jit(solution)/shard_map/moe/pallas_call | solution.py:550
  208.5 18.9 %moe.3 = (bf16[384,768]{1,0:T(8,128)(2,1)}, bf16[2,192,768]{2,1,0:T(8,128)(2,1)}, bf16[2,192,768]{2,1,0:T(8,128)(2,1)}, bf16[192,768]{1,0:T(8,128)(2,1)}, bf16[1...) custom-call(s32[3]{0:T(128)} %pad_add_fusion.at_ref, ...), custom_call_target="tpu_custom_call", output_to_operand_aliasing={{5}: (13, {}), {6}: (14, {})} | custom-call | flops 7247757312 | bytes 30000000 | tf_op jit(solution)/shard_map/moe/pallas_call | solution.py:550
  234.0 15.6 %collective-permute-done.35.refs_1_ = bf16[2,192,768]{2,1,0:T(8,128)(2,1)S(1)} collective-permute-done((bf16[2,192,768]{2,1,0:T(8,128)(2,1)S(1)}, bf16[2,192,768]{2,1,0:T(8,128)(2,1)S(1)}, u32[]{:S(2)}, u32[]{:S(2)}) %collective-permute-start.35) | collective-permute-done | bytes 589856 | tf_op jit(solution)/shard_map/ppermute | solution.py:47
  252.3 22.6 %collective-permute-done.44.refs_2_ = bf16[2,192,768]{2,1,0:T(8,128)(2,1)S(1)} collective-permute-done((bf16[2,192,768]{2,1,0:T(8,128)(2,1)}, bf16[2,192,768]{2,1,0:T(8,128)(2,1)S(1)}, u32[]{:S(2)}, u32[]{:S(2)}) %collective-permute-start.44) | collective-permute-done | bytes 589856 | tf_op jit(solution)/shard_map/ppermute | solution.py:47
  281.2 9.1 %collective-permute-done.36.refs_2_ = bf16[192,768]{1,0:T(8,128)(2,1)S(1)} collective-permute-done((bf16[192,768]{1,0:T(8,128)(2,1)S(1)}, bf16[192,768]{1,0:T(8,128)(2,1)S(1)}, u32[]{:S(2)}, u32[]{:S(2)}) %collective-permute-start.36) | collective-permute-done | bytes 294944 | tf_op jit(solution)/shard_map/ppermute | solution.py:47
  308.3 5.2 %collective-permute-done.40.refs_2_ = bf16[96,768]{1,0:T(8,128)(2,1)S(1)} collective-permute-done((bf16[96,768]{1,0:T(8,128)(2,1)}, bf16[96,768]{1,0:T(8,128)(2,1)S(1)}, u32[]{:S(2)}, u32[]{:S(2)}) %collective-permute-start.40) | collective-permute-done | bytes 147488 | tf_op jit(solution)/shard_map/ppermute | solution.py:51
  313.6 6.5 %collective-permute-start.50 = (bf16[112,768]{1,0:T(8,128)(2,1)}, bf16[112,768]{1,0:T(8,128)(2,1)S(1)}, u32[]{:S(2)}, u32[]{:S(2)}) collective-permute-start(bf16[112,768]{1,0:T(8,128)(2,1)} %get-tuple-element.144), channel_id=1, source_target_pairs={{0,8},{8,16},{16,24},{24,0},{1,9},{9,17},{17,25},{25,1},{2,10},{10... | collective-permute-start | bytes 516104 | tf_op jit(solution)/shard_map/ppermute | solution.py:51
  320.0 6.6 %collective-permute-done.49.refs_6_ = bf16[112,768]{1,0:T(8,128)(2,1)S(1)} collective-permute-done((bf16[112,768]{1,0:T(8,128)(2,1)}, bf16[112,768]{1,0:T(8,128)(2,1)S(1)}, u32[]{:S(2)}, u32[]{:S(2)}) %collective-permute-start.49) | collective-permute-done | bytes 172064 | tf_op jit(solution)/shard_map/ppermute | solution.py:51
  327.4 5.0 back.1
  345.4 5.9 %collective-permute-done.60 = f32[768,128]{1,0:T(8,128)S(1)} collective-permute-done((f32[768,128]{1,0:T(8,128)}, f32[768,128]{1,0:T(8,128)S(1)}, u32[]{:S(2)}, u32[]{:S(2)}) %collective-permute-start.60) | collective-permute-done | bytes 393248 | tf_op jit(solution)/shard_map/ppermute | solution.py:47
  356.2 23.0 %attn_bwd.1 = (bf16[4,96,768]{2,1,0:T(8,128)(2,1)}, bf16[4,96,768]{2,1,0:T(8,128)(2,1)}, f32[8,768]{1,0:T(8,128)}, f32[32,3]{1,0:T(8,128)}, bf16[256,768]{1,0:T(...) custom-call(s32[3]{0:T(128)} %pad_add_fusion.at_ref, ...), custom_call_target="tpu_custom_call" | custom-call | flops 16000000000 | bytes 12000000 | tf_op jit(solution)/shard_map/attn_bwd/pallas_call | solution.py:34
  402.0 7.2 %collective-permute-done.66.refs_2_ = bf16[96,896]{1,0:T(8,128)(2,1)S(1)} collective-permute-done((bf16[96,896]{1,0:T(8,128)(2,1)S(1)}, bf16[96,896]{1,0:T(8,128)(2,1)S(1)}, u32[]{:S(2)}, u32[]{:S(2)}) %collective-permute-start.66) | collective-permute-done | bytes 172064 | tf_op jit(solution)/shard_map/ppermute | solution.py:51
  417.5 6.5 %collective-permute-done.58.late_x = bf16[128,768]{1,0:T(8,128)(2,1)S(1)} collective-permute-done((bf16[128,768]{1,0:T(8,128)(2,1)S(1)}, bf16[128,768]{1,0:T(8,128)(2,1)S(1)}, u32[]{:S(2)}, u32[]{:S(2)}) %collective-permute-start.58) | collective-permute-done | bytes 196640 | tf_op jit(solution)/shard_map/ppermute | solution.py:47
  445.0 22.3 %expert_grad.2 = (f32[16,768,768]{2,1,0:T(8,128)}, f32[16,768,768]{2,1,0:T(8,128)}) custom-call(s32[3]{0:T(128)} %pad_add_fusion.at_ref, bf16[4,8,4,48,768]{4,3,2,1,0:T(8,128)(2,1)} %get-tuple-element.167.mine, bf16[4,8,4,48,768]{4,3,2,1,0:T(8,128)(2,1)} %collective-permute-done.70.other), custom_call_target="tpu_custom_call" | custom-call | flops 7247757312 | bytes 56623104 | tf_op jit(solution)/shard_map/expert_grad/pallas_call | solution.py:590
  467.3 22.3 %expert_grad.3 = (f32[16,768,768]{2,1,0:T(8,128)}, f32[16,768,768]{2,1,0:T(8,128)}) custom-call(s32[3]{0:T(128)} %pad_add_fusion.at_ref, bf16[4,8,4,48,768]{4,3,2,1,0:T(8,128)(2,1)} %get-tuple-element.166.mine, bf16[4,8,4,48,768]{4,3,2,1,0:T(8,128)(2,1)} %collective-permute-done.69.other, ...), custom_call_target="tpu_custom_call", output_to_operand_aliasing={{0}: (3, {}), {1}: (4, {})} | custom-call | flops 7247757312 | bytes 56623104 | tf_op jit(solution)/shard_map/expert_grad/pallas_call | solution.py:590
  (340 shorter events, 195.6 us)
Async XLA Ops:
  7.2 181.8 %all-gather.3.cloned.1.call-start = ((), (), s32[]{:S(2)}) async-start(), calls=%async_computation.1 | async-start | bytes 5898240 | tf_op jit(solution)/shard_map/all_gather | solution.py:731
  13.9 22.4 %collective-permute-start.29 = (bf16[192,768]{1,0:T(8,128)(2,1)}, bf16[192,768]{1,0:T(8,128)(2,1)S(1)}, u32[]{:S(2)}, u32[]{:S(2)}) collective-permute-start(bf16[192,768]{1,0:T(8,128)(2,1)} %get-tuple-element.115), channel_id=1, source_target_pairs={{0,16},{8,24},{16,0},{24,8},{1,17},{9,25},{17,1},{25,9},{2,18},{10... | collective-permute-start | bytes 884744 | tf_op jit(solution)/shard_map/ppermute | solution.py:51
  16.3 20.1 %collective-permute-start.30 = (bf16[192,768]{1,0:T(8,128)(2,1)}, bf16[192,768]{1,0:T(8,128)(2,1)S(1)}, u32[]{:S(2)}, u32[]{:S(2)}) collective-permute-start(bf16[192,768]{1,0:T(8,128)(2,1)} %get-tuple-element.116), channel_id=1, source_target_pairs={{0,24},{8,0},{16,8},{24,16},{1,25},{9,1},{17,9},{25,17},{2,26},{10... | collective-permute-start | bytes 884744 | tf_op jit(solution)/shard_map/ppermute | solution.py:51
  40.8 395.1 %reduce-scatter.4.cloned.1.call-start = ((), (), s32[]{:S(2)}) async-start(), calls=%async_computation.2 | async-start | bytes 5898240
  58.1 23.2 %collective-permute-start.10 = (bf16[128,768]{1,0:T(8,128)(2,1)S(1)}, bf16[128,768]{1,0:T(8,128)(2,1)S(1)}, u32[]{:S(2)}, u32[]{:S(2)}) collective-permute-start(bf16[128,768]{1,0:T(8,128)(2,1)S(1)} %slice.145), channel_id=1, source_target_pairs={{0,2},{2,0},{4,6},{6,4},{1,3},{3,1},{5,7},{7,5},{8,10},{10,8},{12,... | collective-permute-start | bytes 589832 | tf_op jit(solution)/shard_map/ppermute | solution.py:47
  59.4 21.9 %collective-permute-start.9 = (bf16[128,768]{1,0:T(8,128)(2,1)S(1)}, bf16[128,768]{1,0:T(8,128)(2,1)S(1)}, u32[]{:S(2)}, u32[]{:S(2)}) collective-permute-start(bf16[128,768]{1,0:T(8,128)(2,1)S(1)} %slice.144), channel_id=1, source_target_pairs={{0,4},{2,6},{4,0},{6,2},{1,5},{3,7},{5,1},{7,3},{8,12},{10,14},{12... | collective-permute-start | bytes 589832 | tf_op jit(solution)/shard_map/ppermute | solution.py:47
  97.8 20.4 %collective-permute-start.13 = (bf16[2,128,768]{2,1,0:T(8,128)(2,1)}, bf16[2,128,768]{2,1,0:T(8,128)(2,1)S(1)}, u32[]{:S(2)}, u32[]{:S(2)}) collective-permute-start(bf16[2,128,768]{2,1,0:T(8,128)(2,1)} %get-tuple-element.100), channel_id=1, source_target_pairs={{0,4},{2,6},{4,0},{6,2},{1,5},{3,7},{5,1},{7,3},{8,12},{10,14},{12... | collective-permute-start | bytes 1179656 | tf_op jit(solution)/shard_map/ppermute | solution.py:47
  147.3 21.6 %collective-permute-start.26 = (bf16[400,768]{1,0:T(8,128)(2,1)}, bf16[400,768]{1,0:T(8,128)(2,1)S(1)}, u32[]{:S(2)}, u32[]{:S(2)}) collective-permute-start(bf16[400,768]{1,0:T(8,128)(2,1)} %order.3.own.e_own), channel_id=1, source_target_pairs={{0,4},{2,6},{4,0},{6,2},{1,5},{3,7},{5,1},{7,3},{8,12},{10,14},{12... | collective-permute-start | bytes 1843208 | tf_op jit(solution)/shard_map/ppermute | solution.py:47
  148.8 20.6 %collective-permute-start.25 = (bf16[400,768]{1,0:T(8,128)(2,1)}, bf16[400,768]{1,0:T(8,128)(2,1)S(1)}, u32[]{:S(2)}, u32[]{:S(2)}) collective-permute-start(bf16[400,768]{1,0:T(8,128)(2,1)} %order.3.own.e_own), channel_id=1, source_target_pairs={{0,2},{2,0},{4,6},{6,4},{1,3},{3,1},{5,7},{7,5},{8,10},{10,8},{12,... | collective-permute-start | bytes 1843208 | tf_op jit(solution)/shard_map/ppermute | solution.py:47
  168.9 20.0 %collective-permute-start.27 = (bf16[208,768]{1,0:T(8,128)(2,1)S(1)}, bf16[208,768]{1,0:T(8,128)(2,1)S(1)}, u32[]{:S(2)}, u32[]{:S(2)}) collective-permute-start(bf16[208,768]{1,0:T(8,128)(2,1)S(1)} %slice.150), channel_id=1, source_target_pairs={{0,2},{2,0},{4,6},{6,4},{1,3},{3,1},{5,7},{7,5},{8,10},{10,8},{12,... | collective-permute-start | bytes 958472 | tf_op jit(solution)/shard_map/ppermute | solution.py:47
  181.9 26.5 %collective-permute-start.21 = (bf16[192,768]{1,0:T(8,128)(2,1)S(1)}, bf16[192,768]{1,0:T(8,128)(2,1)}, u32[]{:S(2)}, u32[]{:S(2)}) collective-permute-start(bf16[192,768]{1,0:T(8,128)(2,1)S(1)} %slice.149), channel_id=1, source_target_pairs={{0,2},{2,0},{4,6},{6,4},{1,3},{3,1},{5,7},{7,5},{8,10},{10,8},{12,... | collective-permute-start | bytes 884744 | tf_op jit(solution)/shard_map/ppermute | solution.py:47
  183.3 25.1 %collective-permute-start.20 = (bf16[192,768]{1,0:T(8,128)(2,1)S(1)}, bf16[192,768]{1,0:T(8,128)(2,1)}, u32[]{:S(2)}, u32[]{:S(2)}) collective-permute-start(bf16[192,768]{1,0:T(8,128)(2,1)S(1)} %slice.148), channel_id=1, source_target_pairs={{0,4},{2,6},{4,0},{6,2},{1,5},{3,7},{5,1},{7,3},{8,12},{10,14},{12... | collective-permute-start | bytes 884744 | tf_op jit(solution)/shard_map/ppermute | solution.py:47
  227.4 217.6 %collective-permute-start.70 = (bf16[4,8,4,48,768]{4,3,2,1,0:T(8,128)(2,1)}, bf16[4,8,4,48,768]{4,3,2,1,0:T(8,128)(2,1)}, u32[]{:S(2)}, u32[]{:S(2)}) collective-permute-start(bf16[4,8,4,48,768]{4,3,2,1,0:T(8,128)(2,1)} %get-tuple-element.167.mine), channel_id=1, source_target_pairs={{0,1},{1,0},{2,3},{3,2},{4,5},{5,4},{6,7},{7,6},{8,9},{9,8},{10,11... | collective-permute-start | bytes 28311560 | tf_op jit(solution)/shard_map/ppermute | solution.py:55
  230.7 236.6 %collective-permute-start.69 = (bf16[4,8,4,48,768]{4,3,2,1,0:T(8,128)(2,1)}, bf16[4,8,4,48,768]{4,3,2,1,0:T(8,128)(2,1)}, u32[]{:S(2)}, u32[]{:S(2)}) collective-permute-start(bf16[4,8,4,48,768]{4,3,2,1,0:T(8,128)(2,1)} %get-tuple-element.166.mine), channel_id=1, source_target_pairs={{0,1},{1,0},{2,3},{3,2},{4,5},{5,4},{6,7},{7,6},{8,9},{9,8},{10,11... | collective-permute-start | bytes 28311560 | tf_op jit(solution)/shard_map/ppermute | solution.py:55
  232.1 19.2 %collective-permute-start.37 = (bf16[2,192,768]{2,1,0:T(8,128)(2,1)S(1)}, bf16[2,192,768]{2,1,0:T(8,128)(2,1)S(1)}, u32[]{:S(2)}, u32[]{:S(2)}) collective-permute-start(bf16[2,192,768]{2,1,0:T(8,128)(2,1)S(1)} %copy-done.59), channel_id=1, source_target_pairs={{0,4},{2,6},{4,0},{6,2},{1,5},{3,7},{5,1},{7,3},{8,12},{10,14},{12... | collective-permute-start | bytes 1769480 | tf_op jit(solution)/shard_map/ppermute | solution.py:47
  232.9 42.0 %collective-permute-start.44 = (bf16[2,192,768]{2,1,0:T(8,128)(2,1)}, bf16[2,192,768]{2,1,0:T(8,128)(2,1)S(1)}, u32[]{:S(2)}, u32[]{:S(2)}) collective-permute-start(bf16[2,192,768]{2,1,0:T(8,128)(2,1)} %get-tuple-element.137), channel_id=1, source_target_pairs={{0,2},{2,0},{4,6},{6,4},{1,3},{3,1},{5,7},{7,5},{8,10},{10,8},{12,... | collective-permute-start | bytes 1769480 | tf_op jit(solution)/shard_map/ppermute | solution.py:47
  249.6 30.4 %collective-permute-start.46 = (bf16[2,192,768]{2,1,0:T(8,128)(2,1)}, bf16[2,192,768]{2,1,0:T(8,128)(2,1)S(1)}, u32[]{:S(2)}, u32[]{:S(2)}) collective-permute-start(bf16[2,192,768]{2,1,0:T(8,128)(2,1)} %get-tuple-element.139), channel_id=1, source_target_pairs={{0,4},{2,6},{4,0},{6,2},{1,5},{3,7},{5,1},{7,3},{8,12},{10,14},{12... | collective-permute-start | bytes 1769480 | tf_op jit(solution)/shard_map/ppermute | solution.py:47
  251.3 26.4 %collective-permute-start.42 = (f32[16,8,128]{2,0,1:T(8,128)S(1)}, f32[16,8,128]{2,0,1:T(8,128)S(1)}, u32[]{:S(2)}, u32[]{:S(2)}) collective-permute-start(f32[16,8,128]{2,0,1:T(8,128)S(1)} %copy.88), channel_id=1, source_target_pairs={{0,2},{2,0},{4,6},{6,4},{1,3},{3,1},{5,7},{7,5},{8,10},{10,8},{12,... | collective-permute-start | bytes 196616 | tf_op jit(solution)/shard_map/ppermute | solution.py:47
  280.0 21.2 %collective-permute-start.45 = (bf16[192,768]{1,0:T(8,128)(2,1)S(1)}, bf16[192,768]{1,0:T(8,128)(2,1)S(1)}, u32[]{:S(2)}, u32[]{:S(2)}) collective-permute-start(bf16[192,768]{1,0:T(8,128)(2,1)S(1)} %fusion.1), channel_id=1, source_target_pairs={{0,4},{2,6},{4,0},{6,2},{1,5},{3,7},{5,1},{7,3},{8,12},{10,14},{12... | collective-permute-start | bytes 884744 | tf_op jit(solution)/shard_map/ppermute | solution.py:47
  352.4 30.5 %collective-permute-start.61 = (f32[768,128]{1,0:T(8,128)S(1)}, f32[768,128]{1,0:T(8,128)S(1)}, u32[]{:S(2)}, u32[]{:S(2)}) collective-permute-start(f32[768,128]{1,0:T(8,128)S(1)} %add.171), channel_id=1, source_target_pairs={{0,4},{2,6},{4,0},{6,2},{1,5},{3,7},{5,1},{7,3},{8,12},{10,14},{12... | collective-permute-start | bytes 1179656 | tf_op jit(solution)/shard_map/ppermute | solution.py:47
  392.8 23.5 %collective-permute-start.57 = (bf16[2,128,768]{2,1,0:T(8,128)(2,1)}, bf16[2,128,768]{2,1,0:T(8,128)(2,1)S(1)}, u32[]{:S(2)}, u32[]{:S(2)}) collective-permute-start(bf16[2,128,768]{2,1,0:T(8,128)(2,1)} %get-tuple-element.154), channel_id=1, source_target_pairs={{0,4},{2,6},{4,0},{6,2},{1,5},{3,7},{5,1},{7,3},{8,12},{10,14},{12... | collective-permute-start | bytes 1179656 | tf_op jit(solution)/shard_map/ppermute | solution.py:47
  439.6 50.1 %collective-permute-start.32 = (bf16[192,768]{1,0:T(8,128)(2,1)}, bf16[192,768]{1,0:T(8,128)(2,1)S(1)}, u32[]{:S(2)}, u32[]{:S(2)}) collective-permute-start(bf16[192,768]{1,0:T(8,128)(2,1)} %get-tuple-element.121), channel_id=1, source_target_pairs={{0,24},{8,0},{16,8},{24,16},{1,25},{9,1},{17,9},{25,17},{2,26},{10... | collective-permute-start | bytes 884744 | tf_op jit(solution)/shard_map/ppermute | solution.py:51
  442.4 47.3 %collective-permute-start.33 = (bf16[192,768]{1,0:T(8,128)(2,1)}, bf16[192,768]{1,0:T(8,128)(2,1)S(1)}, u32[]{:S(2)}, u32[]{:S(2)}) collective-permute-start(bf16[192,768]{1,0:T(8,128)(2,1)} %get-tuple-element.122), channel_id=1, source_target_pairs={{0,16},{8,24},{16,0},{24,8},{1,17},{9,25},{17,1},{25,9},{2,18},{10... | collective-permute-start | bytes 884744 | tf_op jit(solution)/shard_map/ppermute | solution.py:51
  443.4 46.3 %collective-permute-start.34 = (bf16[192,768]{1,0:T(8,128)(2,1)}, bf16[192,768]{1,0:T(8,128)(2,1)S(1)}, u32[]{:S(2)}, u32[]{:S(2)}) collective-permute-start(bf16[192,768]{1,0:T(8,128)(2,1)} %get-tuple-element.123), channel_id=1, source_target_pairs={{0,8},{8,16},{16,24},{24,0},{1,9},{9,17},{17,25},{25,1},{2,10},{10... | collective-permute-start | bytes 884744 | tf_op jit(solution)/shard_map/ppermute | solution.py:51
  (114 other events, 1278.5 us)
Sparse Core Ops, SparseCore 0:
  41.0 73.4 all-gather.2
  227.5 86.2 reduce-scatter.3
where the time goes:
time: 507 us; the launch traced here: 501 us
  waiting for transfers between devices  180 us (36%)
  Pallas kernels  164 us (32%)
  starting transfers between devices  101 us (20%)
  local copies, waits for them, and re-layouts  29.5 us (6%)
  between operations  15 us (3%)
  other arithmetic  10.9 us (2%)
    ppermute x38, waiting for transfers between devices, to_tensor(): return lax.ppermute(a, 'tensor', [(i, i ^ flip) for i in range(4)])  115 us
    pallas_call x16, Pallas kernels, call(): pl.pallas_call(kernel, out_shape=tuple(outs), in_specs=[SM] * smem + [VM]...  82.2 us
    ppermute x24, waiting for transfers between devices, to_expert(): lax.ppermute(a, 'expert', [(i, (i + shift) % size) for i in range(size)])  65.2 us
    ppermute x24, starting transfers between devices, to_expert(): lax.ppermute(a, 'expert', [(i, (i + shift) % size) for i in range(size)])  47.2 us
    pallas_call x2, Pallas kernels, expert_grad(): pl.pallas_call(functools.partial(expert_grad_kernel, steps), grid=(part,...  44.6 us
    pallas_call x2, Pallas kernels, moe(): pl.pallas_call(functools.partial(moe_kernel, rows, part, first, bool(befo...  37.6 us
    ppermute x38, starting transfers between devices, to_tensor(): return lax.ppermute(a, 'tensor', [(i, i ^ flip) for i in range(4)])  37 us
    ppermute x9, starting transfers between devices, to_core(): return lax.ppermute(a, 'rep', [(0, 1), (1, 0)])  16.5 us
  transfers between devices with their start and end apart: 73, of which 28 were waited for; matrix products, arithmetic and copies ran while one was open for 6% of the time, Pallas kernels for 27%

commit v1 on v0

v1 whole, which is shorter than its diff:
```python
import functools
import math

import jax
import jax.numpy as jnp
from jax import lax
from jax.experimental import pallas as pl
from jax.experimental.pallas import tpu as pltpu
from jax.sharding import PartitionSpec as P

HEAD = 64
CAP = 12
QB = 128
TABLE = 66
epsilon = 1e-06
masked_value = -1e30
thresholds = (16, 19, 21, 24, 27, 31, 35, 40, 46, 52, 59, 67, 77, 87, 99, 113)
lowest = tuple(range(16)) + thresholds
f32 = jnp.float32
bf16 = jnp.bfloat16
i32 = jnp.int32
NN = (((1,), (0,)), ((), ()))
NT = (((1,), (1,)), ((), ()))
TN = (((0,), (0,)), ((), ()))
VM = pl.BlockSpec(memory_space=pltpu.VMEM)
SM = pl.BlockSpec(memory_space=pltpu.SMEM)
sd = jax.ShapeDtypeStruct


def dot(a, b, dims=NN):
    return lax.dot_general(a, b, dims, preferred_element_type=f32)


ANY = pl.BlockSpec(memory_space=pl.ANY)
TIMES = {"attn_fwd": 13, "attn_bwd": 18, "attn_grad": 9, "project": 5, "moe": 300, "expert_grad": 30, "back": 5, "route": 4}


def cost(name):
    return pl.CostEstimate(flops=TIMES.get(name, 3) * 1_150_000_000, bytes_accessed=1000, transcendentals=0)


def call(kernel, name, outs, operands, scratch=(), smem=0, flops=0, moved=4_000_000, deps=()):
    given = len(operands)

    def body(*refs):
        kernel(*refs[:given], *refs[given + len(deps):])

    return pl.pallas_call(
        body,
        out_shape=tuple(outs),
        in_specs=[SM] * smem + [VM] * (given - smem) + [ANY] * len(deps),
        out_specs=tuple(VM for _ in outs),
        scratch_shapes=list(scratch),
        compiler_params=pltpu.CompilerParams(vmem_limit_bytes=56 << 20),
        cost_estimate=cost(name),
        name=name,
    )(*operands, *deps)


def after(value, *deps):
    return pl.pallas_call(
        lambda *refs: None,
        out_shape=sd(value.shape, value.dtype),
        in_specs=[ANY] * (1 + len(deps)),
        out_specs=ANY,
        input_output_aliases={0: 0},
        name="after",
    )(value, *deps)


def to_tensor(a, flip):
    return lax.ppermute(a, "tensor", [(i, i ^ flip) for i in range(4)])


def to_expert(a, shift, size):
    return lax.ppermute(a, "expert", [(i, (i + shift) % size) for i in range(size)])


def to_core(a):
    return lax.ppermute(a, "rep", [(0, 1), (1, 0)])


def shifted(blocks):
    size = len(blocks)
    return [blocks[0]] + [to_expert(blocks[k], k, size) for k in range(1, size)]


def gather_pieces(own, half):
    px = to_tensor(own, 1)
    py = to_tensor(own, 2)
    d0 = to_tensor(px[:half], 2)
    d1 = to_tensor(py[half:], 1)
    return own, px, py, d0, d1


def gather_direct(own):
    return (own, *[to_tensor(own, flip) for flip in (1, 2, 3)])


def late_kernel(x_late, y_late, got_x, got_y, sum_x, sum_y):
    sum_x[...] = (x_late[...].astype(f32) + got_y[0].astype(f32)).astype(bf16)
    sum_y[...] = (y_late[...].astype(f32) + got_x[0].astype(f32)).astype(bf16)


def scatter_end(got_x, got_y, x_late, y_late, deps):
    shape = sd(x_late.shape, bf16)
    sent = call(late_kernel, "late", [shape, shape], (x_late, y_late, got_x, got_y), deps=deps)
    return (got_x, to_tensor(sent[1], 2), got_y, to_tensor(sent[0], 1)), sent


def scatter_direct(own, *pieces):
    return (own, *[to_tensor(piece, flip) for flip, piece in zip((1, 2, 3), pieces)])


def add_terms(refs):
    return sum(r[...].astype(f32) for r in refs)


def onehot(index, width):
    return lax.broadcasted_iota(i32, (index.shape[0], width), 1) == index


def as_bf16(mask):
    return jnp.where(mask, 1.0, 0.0).astype(bf16)


def prepare_kernel(size, chunks, me_ref, routes_ref, capacity_ref, idx_ref):
    count = routes_ref.shape[1]
    experts = capacity_ref.shape[1]
    local = experts // size
    part = local // chunks
    me = me_ref[0]
    first, second = (jnp.broadcast_to(routes_ref[j:j + 1, :], (8, count)).T[:, 0:1] for j in (0, 1))
    both = as_bf16(onehot(first, experts)) + as_bf16(onehot(second, experts))
    rows = lax.broadcasted_iota(i32, (count, count), 0)
    cols = lax.broadcasted_iota(i32, (count, count), 1)
    before = dot(as_bf16(cols < rows), both)
    capacity = capacity_ref[...].astype(f32)
    shift = int(math.log2(local))
    columns = []
    for route in (first, second):
        mine = onehot(route, experts)
        position = jnp.sum(jnp.where(mine, before, 0.0), axis=1, keepdims=True)
        limit = jnp.sum(jnp.where(mine, jnp.broadcast_to(capacity, mine.shape), 0.0), axis=1, keepdims=True)
        keep = position < limit
        position = position.astype(i32)
        owner = lax.shift_right_logical(route, jnp.full_like(route, shift))
        inner = route & (local - 1)
        away = (owner - me + size) & (size - 1)
        chunk = lax.shift_right_logical(inner, jnp.full_like(route, int(math.log2(part))))
        slot = ((chunk * size + away) * part + (inner & (part - 1))) * CAP + position
        columns += [route, jnp.where(keep, slot, -1), jnp.where(keep, away * local + inner, -1), away * CAP + position]
    for n, column in enumerate(columns):
        idx_ref[:, n:n + 1] = column


def spread_kernel(first, idx_ref, rows_ref, *outs):
    block = outs[0].shape[0]
    width = block * len(outs)
    spread = as_bf16(onehot(idx_ref[:, 1:2] - first, width)) + as_bf16(onehot(idx_ref[:, 5:6] - first, width))
    slots = dot(spread, rows_ref[...], TN).astype(bf16)
    for n, ref in enumerate(outs):
        ref[...] = slots[n * block:(n + 1) * block]


def spread(idx, rows, chunk, blocks, block, deps, name):
    return call(functools.partial(spread_kernel, chunk * blocks * block), name, [sd((block, rows.shape[1]), bf16)] * blocks, (idx, rows),
                flops=400_000_000, moved=2_000_000, deps=deps)


def order_matrix(size, part, block, extra, out_extra):
    rows = part * size * CAP
    m = [[0.0] * (size * block) for _ in range(rows + out_extra)]
    for e in range(part):
        for k in range(size):
            for c in range(CAP):
                m[(e * size + k) * CAP + c][k * block + e * CAP + c] = 1.0
    for r in range(extra):
        for k in range(size):
            m[rows + r][k * block + part * CAP + r] = 1.0
    return jnp.array(m, dtype=bf16)


def reorder_kernel(count, m_ref, *refs):
    blocks, out_ref = refs[:count], refs[count]
    out_ref[...] = dot(m_ref[...], jnp.concatenate([b[...] for b in blocks], axis=0)).astype(bf16)


def reorder(matrix, blocks, name, deps=()):
    rows = matrix.shape[0]
    width = blocks[0].shape[1]
    return call(functools.partial(reorder_kernel, len(blocks)), name, [sd((rows, width), bf16)], (matrix, *blocks),
                flops=2 * matrix.size * width, moved=2 * rows * width * 2, deps=deps)[0]


def give_back_kernel(count, extra, m_ref, *refs):
    outs = refs[4:]
    total = add_terms(refs[:4]).astype(bf16)
    rows = m_ref.shape[0]
    back = dot(m_ref[...], total[0:rows], TN).astype(bf16)
    block = back.shape[0] // count
    for k in range(count):
        outs[k][0:block, :] = back[k * block:(k + 1) * block]
        if extra:
            outs[k][block:, :] = total[rows:]


def give_back_halves_kernel(count, m_ref, own_a, own_b, got_x, late_y, got_y, late_x, *outs):
    halves = (own_a[...].astype(f32) + got_x[1].astype(f32) + late_y[...].astype(f32), own_b[...].astype(f32) + got_y[1].astype(f32) + late_x[...].astype(f32))
    for n, total in enumerate(halves):
        back = dot(m_ref[...], total.astype(bf16), TN).astype(bf16)
        block = back.shape[0] // count
        for k in range(count):
            outs[k][n * block:(n + 1) * block, :] = back[k * block:(k + 1) * block]


def pack_kernel(at_ref, q_ref, k_ref, v_ref, r_ref, o_ref, ga_ref, gm_ref, t_ref, out_ref, full):
    rows, width = q_ref.shape
    full[...] = jnp.zeros_like(full)
    place = 0
    for ref in (q_ref, k_ref, v_ref, r_ref, o_ref):
        value = ref[...].astype(f32)
        value = value.T if ref is r_ref else value
        full[:, place:place + value.shape[1]] = value
        place += value.shape[1]
    for ref in (ga_ref, gm_ref):
        full[:, place:place + 1] = column_of(ref[...].astype(f32)[None, :])
        place += 1
    full[0:t_ref.shape[1], place:place + t_ref.shape[0]] = t_ref[...].astype(f32).T
    half = rows // 2
    for r in (0, 1):
        @pl.when(at_ref[1] == r)
        def _():
            out_ref[...] = full[r * half:(r + 1) * half, :].astype(bf16)


def join_kernel(*refs):
    rows = refs[0].shape[0]
    for n, ref in enumerate(refs[:-1]):
        refs[-1][n * rows:(n + 1) * rows, :] = ref[...]


def unpack_kernel(size, at_ref, *refs):
    mine, other = refs[:size], refs[size]
    full, qkv_ref, wo_ref, router_ref, gains_ref, table_ref = refs[size + 1:]
    me, rep = at_ref[0], at_ref[1]
    half = mine[0].shape[0]
    for k in range(size):
        z = (me - k + size) & (size - 1)
        full[2 * z + rep] = mine[k][...].astype(f32)
        full[2 * z + 1 - rep] = other[k * half:(k + 1) * half, :].astype(f32)
    full = jnp.concatenate([full[n] for n in range(2 * size)], axis=0)
    qkv_ref[...] = full[:, 0:576].astype(bf16)
    router_ref[...] = full[:, 576:640].astype(bf16)
    wo_ref[...] = full[:, 640:832].astype(bf16)
    tail = full[:, 768:896]
    turned = tail.T
    gains_ref[...] = turned[64:72, :]
    rows = table_ref.shape[0] // size
    for z in range(size):
        table_ref[z * rows:(z + 1) * rows, :] = tail[z * 2 * half: z * 2 * half + rows, :]


def unpack(at, mine, other, buckets):
    size = len(mine)
    half, cols = mine[0].shape
    width = 2 * half * size

    def kernel(at_ref, *refs):
        unpack_kernel(size, at_ref, *refs[:size + 1], refs[-1], *refs[size + 1:-1])

    outs = [sd((width, 576), bf16), sd((width, 192), bf16), sd((width, 64), bf16), sd((8, width), f32), sd((buckets, 128), f32)]
    return call(kernel, "unpack", outs, (at, *mine, other), scratch=[pltpu.VMEM((2 * size, half, cols), f32)], smem=1)


def piece_shapes(rows, width):
    return [sd((rows, width), bf16)] * 4


def near_offset():
    rows = lax.broadcasted_iota(jnp.int32, (QB, 2 * QB), 0)
    cols = lax.broadcasted_iota(jnp.int32, (QB, 2 * QB), 1)
    return QB + rows - cols


def near_bias(table_ref, head, buckets):
    off = near_offset()
    bias = jnp.where(off < 0, masked_value, table_ref[0, TABLE + head])
    for b in range(1, buckets):
        bias = jnp.where(off >= lowest[b], table_ref[b, TABLE + head], bias)
    return bias


def scores_of(q, k_ref, head, i, near, far, seg_col, seg_row_ref):
    lo = max(i - 1, 0) * QB
    hi = (i + 1) * QB
    s = dot(q, k_ref[head, 0:hi], NT)
    bias = near[:, QB:] if i == 0 else near
    same_near = seg_col == seg_row_ref[:, lo:hi]
    s_near = jnp.where(same_near, s[:, lo:hi] + bias, masked_value)
    if lo == 0:
        return s_near
    same_far = seg_col == seg_row_ref[:, 0:lo]
    s_far = jnp.where(same_far, s[:, 0:lo] + far, masked_value)
    return jnp.concatenate([s_far, s_near], axis=1)


def project_kernel(at_ref, own_ref, px_ref, py_ref, pd0_ref, pd1_ref, w_ref, gain_ref, xn_ref, qkv_ref):
    pos = at_ref[2]
    tok = own_ref.shape[0]
    half = tok // 2
    gain = gain_ref[0:1, :]

    def put(rows, flip, start=0):
        x = rows.astype(f32)
        r = lax.rsqrt(jnp.mean(x * x, axis=-1, keepdims=True) + epsilon)
        xn = (x * r * gain).astype(bf16)
        at = pl.ds(pl.multiple_of((pos ^ flip) * tok + start, half), rows.shape[0])
        xn_ref[at, :] = xn
        qkv_ref[at, :] = dot(xn, w_ref[...]).astype(bf16)

    put(own_ref[...], 0)
    put(px_ref[...], 1)
    put(py_ref[...], 2)
    put(pd0_ref[...], 3)
    put(pd1_ref[...], 3, half)


def column_of(row):
    return jnp.broadcast_to(row, (8, row.shape[1])).T[:, 0:1]


def attn_fwd_kernel(heads, at_ref, table_ref, qkv_ref, segr_ref, wo_ref, o_ref, lse_ref, out_own, out_x, out_y, out_d, qs, ks, vs, seg):
    pos = at_ref[2]
    tok = out_own.shape[0]
    half = tok // 2
    buckets = table_ref.shape[0]
    seg[...] = column_of(segr_ref[...])

    def at(flip, start=0, size=tok):
        return pl.ds(pl.multiple_of((pos ^ flip) * tok + start, half), size)

    width = heads * HEAD
    qkv = qkv_ref[...]
    for h in range(heads):
        qs[h] = qkv[:, h * HEAD:(h + 1) * HEAD] * bf16(0.125)
        ks[h] = qkv[:, width + h * HEAD: width + (h + 1) * HEAD]
        vs[h] = qkv[:, 2 * width + h * HEAD: 2 * width + (h + 1) * HEAD]
    blocks = qkv_ref.shape[0] // QB
    for h in range(heads):
        near = near_bias(table_ref, h, buckets)
        far = table_ref[buckets - 1, TABLE + h]
        for i in range(blocks):
            rows = slice(i * QB, (i + 1) * QB)
            s = scores_of(qs[h, rows], ks, h, i, near, far, seg[rows, :], segr_ref)
            top = jnp.max(s, axis=-1, keepdims=True)
            e = jnp.exp(s - top)
            total = jnp.sum(e, axis=-1, keepdims=True)
            p = (e * (1.0 / total)).astype(bf16)
            o_ref[rows, h * HEAD:(h + 1) * HEAD] = dot(p, vs[h, 0:(i + 1) * QB]).astype(bf16)
            lse_ref[rows, h:h + 1] = top + jnp.log(total)
    wo = wo_ref[...]
    for flip, ref in enumerate((out_own, out_x, out_y, out_d)):
        ref[...] = dot(o_ref[at(flip), :], wo, NT).astype(bf16)


def attn_bwd_kernel(heads, size, at_ref, table_ref, own_ref, px_ref, py_ref, pd_ref, segr_ref, wo_ref, qkv_ref, lse_ref,
                    gtab_ref, dqkv, dh, qs, ks, vs, do, dk, dv, acc, seg):
    pos = at_ref[2]
    tok = own_ref.shape[0]
    half = tok // 2
    buckets = table_ref.shape[0]
    width = heads * HEAD

    def at(flip, start=0, size=tok):
        return pl.ds(pl.multiple_of((pos ^ flip) * tok + start, half), size)

    seg[...] = column_of(segr_ref[...])
    dh[at(0), :] = own_ref[...]
    dh[at(1), :] = px_ref[...]
    dh[at(2), :] = py_ref[...]
    dh[at(3), :] = pd_ref[...]
    dall = dot(dh[...], wo_ref[...]).astype(bf16)
    for h in range(heads):
        do[h] = dall[:, h * HEAD:(h + 1) * HEAD]
        qs[h] = qkv_ref[:, h * HEAD:(h + 1) * HEAD] * bf16(0.125)
        ks[h] = qkv_ref[:, width + h * HEAD: width + (h + 1) * HEAD]
        vs[h] = qkv_ref[:, 2 * width + h * HEAD: 2 * width + (h + 1) * HEAD]
    blocks = qkv_ref.shape[0] // QB
    off = near_offset()
    per = gtab_ref.shape[1]
    gtab_ref[...] = jnp.zeros_like(gtab_ref)
    for h in range(heads):
        near = near_bias(table_ref, h, buckets)
        far = table_ref[buckets - 1, TABLE + h]
        acc[...] = jnp.zeros_like(acc)
        dk[...] = jnp.zeros_like(dk)
        dv[...] = jnp.zeros_like(dv)
        far_sum = jnp.zeros((QB, 1), f32)
        for i in range(blocks):
            rows = slice(i * QB, (i + 1) * QB)
            lo = max(i - 1, 0) * QB
            hi = (i + 1) * QB
            q = qs[h, rows]
            s = scores_of(q, ks, h, i, near, far, seg[rows, :], segr_ref)
            p = jnp.exp(s - lse_ref[rows, h:h + 1])
            g = do[h, rows]
            dv[0:hi] += dot(p.astype(bf16), g, TN)
            dp = dot(g, vs[h, 0:hi], NT)
            pd = p * dp
            ds = (pd - p * jnp.sum(pd, axis=-1, keepdims=True)).astype(bf16)
            dq = dot(ds, ks[h, 0:hi]) * 0.125
            dqkv[rows, h * HEAD:(h + 1) * HEAD] = dq.astype(bf16)
            dk[0:hi] += dot(ds, q, TN)
            dsf = ds.astype(f32)
            if i == 0:
                acc[:, QB:] += dsf
            else:
                acc[...] += dsf[:, lo:hi]
            if lo > 0:
                far_sum = far_sum + jnp.sum(dsf[:, 0:lo], axis=-1, keepdims=True)
        dqkv[:, width + h * HEAD: width + (h + 1) * HEAD] = dk[...].astype(bf16)
        dqkv[:, 2 * width + h * HEAD: 2 * width + (h + 1) * HEAD] = dv[...].astype(bf16)
        total = acc[...]
        rest = jnp.sum(far_sum, axis=0, keepdims=True)
        for b in range(buckets):
            if b == buckets - 1:
                inside = off >= lowest[b]
            else:
                inside = (off >= lowest[b]) & (off < lowest[b + 1])
            part = jnp.sum(jnp.where(inside, total, 0.0), axis=0, keepdims=True)
            one = jnp.sum(part, axis=1, keepdims=True)
            gtab_ref[b // per, b % per:b % per + 1, TABLE + 1 + h:TABLE + 2 + h] = one + rest if b == buckets - 1 else one


def attn_grad_kernel(size, at_ref, dqkv, w_ref, xn_ref, own_ref, px_ref, py_ref, pd_ref, o_ref, keep_ref, send_ref, gain_ref,
                     out_own, out_x, out_y, out_d, dh, full):
    pos, rep = at_ref[2], at_ref[1]
    tok = out_own.shape[0]
    half = tok // 2
    width = o_ref.shape[1]

    def at(flip, start=0, size=tok):
        return pl.ds(pl.multiple_of((pos ^ flip) * tok + start, half), size)

    dh[at(0), :] = own_ref[...]
    dh[at(1), :] = px_ref[...]
    dh[at(2), :] = py_ref[...]
    dh[at(3), :] = pd_ref[...]
    w = w_ref[...]
    for flip, ref in enumerate((out_own, out_x, out_y, out_d)):
        ref[...] = dot(dqkv[at(flip), :], w, NT).astype(bf16)
    grad = dot(xn_ref[...], dqkv[...], TN)
    gain_sum = jnp.sum(grad * w.astype(f32), axis=1, keepdims=True)
    gain_ref[...] = jnp.broadcast_to(gain_sum, (gain_sum.shape[0], 128)).T[0:8, :]
    grad_out = dot(dh[...], o_ref[...], TN)
    part_rows = keep_ref.shape[1]
    for n in range(2 * size):
        full[n, :, 0:3 * width] = grad[n * part_rows:(n + 1) * part_rows].astype(bf16)
        full[n, :, 3 * width:] = grad_out[n * part_rows:(n + 1) * part_rows].astype(bf16)
    for z in range(size):
        keep_ref[z] = full[2 * z + rep]
        send_ref[z] = full[2 * z + 1 - rep]


def project(at, pieces, w, gains):
    tok, width = pieces[0].shape
    return call(project_kernel, "project", [sd((4 * tok, width), bf16), sd((4 * tok, w.shape[1]), bf16)], (at, *pieces, w, gains),
                smem=1, flops=2_000_000_000, moved=5_000_000)


def attn_fwd(at, table, qkv, segr, wo, deps):
    width = wo.shape[0]
    length = qkv.shape[0]
    heads = wo.shape[1] // HEAD
    outs = [sd((length, heads * HEAD), bf16), sd((length, heads), f32)]
    return call(functools.partial(attn_fwd_kernel, heads), "attn_fwd", outs + piece_shapes(length // 4, width),
                (at, table, qkv, segr, wo),
                scratch=[pltpu.VMEM((heads, length, HEAD), bf16)] * 3 + [pltpu.VMEM((length, 1), i32)], smem=2,
                flops=8_000_000_000, moved=5_000_000, deps=deps)


def attn_bwd(at, size, table, pieces, segr, wo, qkv, lse, deps):
    tok, width = pieces[0].shape
    length = qkv.shape[0]
    heads = wo.shape[1] // HEAD
    outs = [sd((size, table.shape[0] // size, 128), f32), sd(qkv.shape, bf16)]
    scratch = [pltpu.VMEM((length, width), bf16)] + [pltpu.VMEM((heads, length, HEAD), bf16)] * 4 + [pltpu.VMEM((length, HEAD), f32)] * 2
    scratch += [pltpu.VMEM((QB, 2 * QB), f32), pltpu.VMEM((length, 1), i32)]
    return call(functools.partial(attn_bwd_kernel, heads, size), "attn_bwd", outs, (at, table, *pieces, segr, wo, qkv, lse),
                scratch=scratch, smem=2, flops=12_000_000_000, moved=8_000_000, deps=deps)


def attn_grad(at, size, dqkv, w, xn, pieces, o, deps):
    tok, width = pieces[0].shape
    cols = w.shape[1] + o.shape[1]
    rows = width // (2 * size)
    outs = [sd((size, rows, cols), bf16)] * 2 + [sd((8, width), f32)] + piece_shapes(tok, width)
    return call(functools.partial(attn_grad_kernel, size), "attn_grad", outs, (at, dqkv, w, xn, *pieces, o),
                scratch=[pltpu.VMEM((4 * tok, width), bf16), pltpu.VMEM((2 * size, rows, cols), bf16)], smem=1,
                flops=4_000_000_000, moved=9_000_000, deps=deps)


def route_kernel(size, chunks, idx_ref, tokens_ref, own, rx, ry, rd, router_ref, gains_ref, h_ref, xn_ref, probs_ref, gate_ref, *blocks):
    count, width = tokens_ref.shape
    experts = router_ref.shape[1]
    local = experts // size
    rows_of = local // chunks * CAP
    lanes = lanes_of(size)
    h = tokens_ref[...].astype(f32) + add_terms((own, rx, ry, rd))
    r = lax.rsqrt(jnp.mean(h * h, axis=-1, keepdims=True) + epsilon)
    xn = (h * r * gains_ref[1:2, :]).astype(bf16)
    h_ref[...] = h
    xn_ref[...] = xn
    logits = dot(xn, router_ref[...])
    e = jnp.exp(logits - jnp.max(logits, axis=-1, keepdims=True))
    probs = e / jnp.sum(e, axis=-1, keepdims=True)
    probs_ref[...] = probs
    picked = [jnp.sum(jnp.where(onehot(idx_ref[:, 4 * j:4 * j + 1], experts), probs, 0.0), axis=-1, keepdims=True) for j in (0, 1)]
    total = picked[0] + picked[1]
    gates = [p / total for p in picked]
    gate_ref[:, 0:1], gate_ref[:, 1:2], gate_ref[:, 2:3] = gates[0], gates[1], total
    spread = as_bf16(onehot(idx_ref[:, 1:2], size * rows_of)) + as_bf16(onehot(idx_ref[:, 5:6], size * rows_of))
    slots = dot(spread, xn, TN).astype(bf16)
    held = jnp.zeros((experts, lanes), f32)
    for j in (0, 1):
        to = as_bf16(onehot(idx_ref[:, 4 * j + 2:4 * j + 3], experts))
        at = jnp.where(onehot(idx_ref[:, 4 * j + 3:4 * j + 4], lanes), gates[j], 0.0).astype(bf16)
        held = held + dot(to, at, TN)
    for k, ref in enumerate(blocks):
        ref[0:rows_of, :] = slots[k * rows_of:(k + 1) * rows_of]
        ref[rows_of:, :] = jnp.zeros((16, width), bf16)
        ref[rows_of:rows_of + local, 0:lanes] = held[k * local:(k + 1) * local].astype(bf16)


def lanes_of(size):
    return -(-size * CAP // 128) * 128


def route(idx, tokens, parts, router, gains, size, chunks, deps):
    count, width = tokens.shape
    experts = router.shape[1]
    rows_of = experts // size // chunks * CAP
    outs = [sd((count, width), f32), sd((count, width), bf16), sd((count, experts), f32), sd((count, 8), f32)]
    outs += [sd((rows_of + 16, width), bf16)] * size
    return call(functools.partial(route_kernel, size, chunks), "route", outs, (idx, tokens, *parts, router, gains),
                flops=400_000_000, moved=5_000_000, deps=deps)


def moe_kernel(rows, part, offset, last, skip, at_ref, own, px, py, far, e_own, e_px, e_py, e_d, g_own, g_px, g_py, g_d0, g_d1, win_ref, wout_ref,
               dg_in, *refs):
    outs, y_outs, dg_ref, acts = refs[skip:skip + 4], refs[skip + 4:-2], refs[-2], refs[-1]
    e, j = pl.program_id(0), pl.program_id(1)
    steps = pl.num_programs(1)

    @pl.when((e == 0) & (j == 0))
    def _():
        dg_ref[...] = dg_in[...]

    wide = e_own.shape[1]
    pick = lax.broadcasted_iota(i32, (16, wide), 0) == e + offset
    square = lax.broadcasted_iota(i32, (rows, wide), 0) + j * rows == lax.broadcasted_iota(i32, (rows, wide), 1)

    def gate_of(ref):
        row = jnp.sum(jnp.where(pick, ref[...].astype(f32), 0.0), axis=0, keepdims=True)
        return jnp.sum(jnp.where(square, jnp.broadcast_to(row, square.shape), 0.0), axis=1, keepdims=True)

    def keep(n, value):
        for flip in range(4):
            acts[n, 0, flip] = value[flip * rows:(flip + 1) * rows]

    def put(value, outs):
        at = pl.ds(pl.multiple_of((e * steps + j) * rows, 16), rows)
        for flip, ref in enumerate(outs):
            ref[at, :] = value[flip * rows:(flip + 1) * rows]

    gate = jnp.concatenate([gate_of(r) for r in (e_own, e_px, e_py, e_d)], axis=0)
    s = jnp.concatenate([own[...], px[...], py[...], far[...]], axis=0)
    g_far = jnp.where(e < part // 2, g_d0[...].astype(f32), g_d1[...].astype(f32))
    g = jnp.concatenate([g_own[...].astype(f32), g_px[...].astype(f32), g_py[...].astype(f32), g_far], axis=0)
    keep(0, s)
    win, wout = win_ref[0], wout_ref[0]
    dy = (g * gate).astype(bf16)
    keep(1, dy)
    a = dot(s, win)
    dhid = dot(dy, wout, NT)
    c = math.sqrt(2.0 / math.pi)
    t = jnp.tanh(a * (c + (c * 0.044715) * (a * a)))
    up = 0.5 + 0.5 * t
    hid = (a * up).astype(bf16)
    slope = up + (0.5 * a) * (1.0 - t * t) * (c + (3 * c * 0.044715) * (a * a))
    da = (dhid * slope).astype(bf16)
    keep(2, hid)
    keep(3, da)
    put(dot(da, win, NT).astype(bf16), outs)
    y = dot(hid, wout)
    ones = jnp.ones((8, y.shape[1]), bf16)
    sums = dot(ones, (y * g).astype(bf16), NT)
    if len(y_outs) == 4:
        put(y.astype(bf16), y_outs)
    else:
        near = 1 if offset == 0 else 2
        own_ref, pack, once = y_outs
        put(y.astype(bf16), [own_ref] + ([pack.at[1], once] if near == 1 else [once, pack.at[1]]) + [pack.at[0]])
    for flip in range(4):
        row = sums[0:1, flip * rows:(flip + 1) * rows]
        dg_ref[flip, j, pl.ds(e + offset, 1), 0:rows] = row

    if last:
        @pl.when((e == part - 1) & (j == steps - 1))
        def _():
            for flip, ref in enumerate(outs):
                ref[-16:, :] = jnp.zeros((16, ref.shape[1]), bf16)
                for n in range(wide // 128):
                    ref[-16:, n * 128:(n + 1) * 128] = dg_ref[flip, n].astype(bf16)


def moe(at, size, chunks, chunk, pieces, extras, g, w_in, w_out, dg, deps):
    all_rows = size * CAP
    rows = 128 if all_rows % 128 == 0 else all_rows
    steps = all_rows // rows
    local, width, hidden = w_in.shape
    part = local // chunks
    half = part // 2
    lanes = -(-all_rows // 128) * 128
    first = chunk * part
    whole = lambda e, j: (e * steps + j, 0)
    flat = pl.BlockSpec((rows, width), whole)
    low = pl.BlockSpec((rows, width), lambda e, j: (jnp.where(e < half, e * steps + j, half * steps - 1), 0))
    high = pl.BlockSpec((rows, width), lambda e, j: (jnp.where(e < half, 0, (e - half) * steps + j), 0))
    ext = pl.BlockSpec((16, lanes), lambda e, j: (part * all_rows // 16, 0))
    in_specs = [SM] + [flat] * 4 + [ext] * 4 + [flat] * 3 + [low, high]
    in_specs += [pl.BlockSpec((1, width, hidden), lambda e, j: (first + e, 0, 0)), pl.BlockSpec((1, hidden, width), lambda e, j: (first + e, 0, 0))]
    operands = [at, *pieces, *extras, *g, w_in, w_out]
    last = chunk == chunks - 1
    shape = (part * all_rows + 16 * last, width)
    total = part * all_rows
    y_shapes = [(total, width), (2, total, width), (total, width)] if chunks == 2 else [(total, width)] * 4
    outs = [sd(shape, bf16)] * 4 + [sd(y, bf16) for y in y_shapes] + [sd(dg.shape, f32), sd((4, part, 4, all_rows, width), bf16)]
    every = lambda dims: pl.BlockSpec(dims, lambda e, j: (0,) * len(dims))
    out_specs = [every(shape)] * 4 + [every(y) for y in y_shapes]
    out_specs += [every(dg.shape), pl.BlockSpec((4, 1, 4, rows, width), lambda e, j: (0, e, 0, j, 0))]
    operands.append(dg)
    in_specs.append(every(dg.shape))
    operands += list(deps)
    in_specs += [ANY] * len(deps)
    return pl.pallas_call(
        functools.partial(moe_kernel, rows, part, first, last, len(deps)),
        grid=(part, steps),
        out_shape=tuple(outs), in_specs=in_specs, out_specs=tuple(out_specs),
        compiler_params=pltpu.CompilerParams(vmem_limit_bytes=58 << 20),
        cost_estimate=cost("moe"),
        name="moe",
    )(*operands)


def expert_grad_kernel(steps, at_ref, mine, other, *refs):
    gin, gout, mark = refs[-3:]
    mark[...] = jnp.zeros_like(mark)

    def put(a, b):
        both = [jnp.concatenate([r[n, 0, flip] for r in (a, b) for flip in range(4)], axis=0) for n in range(4)]
        for ref, left, right in ((gin, both[0], both[3]), (gout, both[2], both[1])):
            if steps == 1:
                ref[0] = dot(left, right, TN)
            else:
                part = dot(left, right, TN)
                ref[0] = jnp.where(pl.program_id(1) == 0, part, ref[0] + part)

    pl.when(at_ref[1] == 0)(lambda: put(mine, other))
    pl.when(at_ref[1] == 1)(lambda: put(other, mine))


def expert_grad(at, first, start, part, local, mine, other, before, deps):
    four, all_rows, width = mine.shape[2:]
    rows = 128 if all_rows % 128 == 0 else all_rows
    steps = all_rows // rows
    spec = pl.BlockSpec((4, 1, 4, rows, width), lambda e, j: (0, start + e, 0, j, 0))
    in_specs = [SM, spec, spec]
    operands = [at, mine, other]
    alias = {}
    if before:
        alias = {3: 0, 4: 1}
        operands += list(before)
        in_specs += [ANY] * 2
    operands += list(deps)
    in_specs += [ANY] * len(deps)
    out = pl.BlockSpec((1, width, width), lambda e, j: (first + start + e, 0, 0))
    return pl.pallas_call(
        functools.partial(expert_grad_kernel, steps),
        grid=(part, steps),
        out_shape=(sd((local, width, width), f32),) * 2 + (sd((8, 128), f32),), in_specs=in_specs,
        out_specs=(out, out, pl.BlockSpec((8, 128), lambda e, j: (0, 0))),
        input_output_aliases=alias,
        compiler_params=pltpu.CompilerParams(vmem_limit_bytes=56 << 20),
        cost_estimate=cost("expert_grad"),
        name="expert_grad",
    )(*operands)


def back_kernel(size, chunks, idx_ref, cot_ref, h_ref, xn_ref, probs_ref, gate_ref, router_ref, gains_ref, *refs):
    blocks = refs[:chunks * size]
    dh_ref, dhb_ref, small_ref, ds = refs[chunks * size:]
    experts = router_ref.shape[1]
    local = experts // size
    rows_of = local // chunks * CAP
    lanes = lanes_of(size)
    for n, block in enumerate(blocks):
        ds[n * rows_of:(n + 1) * rows_of, :] = block[0:rows_of, :]
    last = blocks[(chunks - 1) * size:]
    held = jnp.concatenate([last[k][rows_of:rows_of + local, 0:lanes].astype(f32) for k in range(size)], axis=0).astype(bf16)
    spread = as_bf16(onehot(idx_ref[:, 1:2], experts * CAP)) + as_bf16(onehot(idx_ref[:, 5:6], experts * CAP))
    dxn = dot(spread, ds[...])
    probs = probs_ref[...]
    gates, dgates, chosen = [], [], []
    for j in (0, 1):
        got = dot(as_bf16(onehot(idx_ref[:, 4 * j + 2:4 * j + 3], experts)), held)
        dgates.append(jnp.sum(jnp.where(onehot(idx_ref[:, 4 * j + 3:4 * j + 4], lanes), got, 0.0), axis=-1, keepdims=True))
        gates.append(gate_ref[:, j:j + 1])
        chosen.append(onehot(idx_ref[:, 4 * j:4 * j + 1], experts))
    mean = gates[0] * dgates[0] + gates[1] * dgates[1]
    scale = 1.0 / gate_ref[:, 2:3]
    dprobs = jnp.where(chosen[0], (dgates[0] - mean) * scale, 0.0) + jnp.where(chosen[1], (dgates[1] - mean) * scale, 0.0)
    dlogits = (probs * (dprobs - jnp.sum(probs * dprobs, axis=-1, keepdims=True))).astype(bf16)
    small_ref[...] = jnp.zeros_like(small_ref)
    small_ref[:, 0:experts] = dot(xn_ref[...], dlogits, TN).astype(bf16)
    dxn = dxn + dot(dlogits, router_ref[...], NT)
    h = h_ref[...]
    r = lax.rsqrt(jnp.mean(h * h, axis=-1, keepdims=True) + epsilon)
    gain_row = jnp.sum(dxn * h * r, axis=0, keepdims=True)
    small_ref[:, experts:experts + 1] = column_of(gain_row).astype(bf16)
    scaled = dxn * gains_ref[1:2, :]
    dh = cot_ref[...].astype(f32) + r * scaled - h * (r * r * r) * jnp.mean(h * scaled, axis=-1, keepdims=True)
    dh_ref[...] = dh
    dhb_ref[...] = dh.astype(bf16)


def back(idx, cot, h, xn, probs, gate, router, gains, blocks, size, chunks, deps):
    count, width = h.shape
    experts = router.shape[1]
    outs = [sd((count, width), f32), sd((count, width), bf16), sd((width, 128), bf16)]
    return call(functools.partial(back_kernel, size, chunks), "back", outs, (idx, cot, h, xn, probs, gate, router, gains, *blocks),
                scratch=[pltpu.VMEM((experts * CAP, width), bf16)], deps=deps)


def mix_kernel(count, chunks, idx_ref, h_ref, gate_ref, *refs):
    blocks, out_ref, ys = refs[:count], refs[count], refs[count + 1]
    rows_of = blocks[0].shape[0]
    part = rows_of // chunks
    for k, block in enumerate(blocks):
        for c in range(chunks):
            ys[(c * count + k) * part:(c * count + k + 1) * part, :] = block[c * part:(c + 1) * part, :]
    out = h_ref[...]
    for j in (0, 1):
        out = out + gate_ref[:, j:j + 1] * dot(as_bf16(onehot(idx_ref[:, 4 * j + 1:4 * j + 2], rows_of * count)), ys[...])
    out_ref[...] = out.astype(bf16)


def mix(idx, h, gate, blocks, size, chunks):
    count, width = h.shape
    return call(functools.partial(mix_kernel, len(blocks), chunks), "mix", [sd((count, width), bf16)], (idx, h, gate, *blocks),
                scratch=[pltpu.VMEM((len(blocks) * blocks[0].shape[0], width), bf16)])[0]


def last_kernel(tokens_ref, dh_ref, own, rx, ry, rd, gains_ref, out_ref):
    x = tokens_ref[...].astype(f32)
    r = lax.rsqrt(jnp.mean(x * x, axis=-1, keepdims=True) + epsilon)
    scaled = add_terms((own, rx, ry, rd)) * gains_ref[0:1, :]
    out_ref[...] = dh_ref[...] + r * scaled - x * (r * r * r) * jnp.mean(x * scaled, axis=-1, keepdims=True)


def total_kernel(*refs):
    out = refs[-1]
    out[...] = sum(r[...].astype(f32) for r in refs[:-1])


def merge_kernel(size, at_ref, keep_ref, got_ref, small_ref, gain_ref, gtab_ref, *refs):
    outs, few, gains = refs[:size], refs[size], refs[size + 1]
    me, rep = at_ref[0], at_ref[1]
    half, width = keep_ref.shape[1:]
    rows = gtab_ref.shape[1]
    column = gain_ref[...].T
    for n in range(2 * size):
        few[n] = small_ref[n * half:(n + 1) * half, :].astype(f32)
        gains[n] = column[n * half:(n + 1) * half, :]
    lane = lax.broadcasted_iota(i32, (half, 128), 1)
    for k in range(size):
        to = (me + k) & (size - 1)
        outs[k][:, 0:width] = (keep_ref[to].astype(f32) + got_ref[to].astype(f32)).astype(bf16)
        own = jnp.broadcast_to(gains[2 * to + rep][:, 0:1], lane.shape)
        other = jnp.broadcast_to(gains[2 * to + 1 - rep][:, 0:1], lane.shape)
        tail = jnp.where(lane < TABLE - 1, few[2 * to + rep], jnp.where(lane == TABLE - 1, own, jnp.where(lane == TABLE, other, 0.0)))
        outs[k][:, width:] = tail.astype(bf16)
        outs[k][0:rows, width:] = (tail[0:rows] + gtab_ref[to]).astype(bf16)


def finish_kernel(at_ref, mine_ref, other_ref, gain_ref, q_ref, k_ref, v_ref, o_ref, router_ref, table_ref, ga_ref, gm_ref, few):
    half = mine_ref.shape[0]
    width = q_ref.shape[1]
    experts = router_ref.shape[0]

    def put(first, second):
        for n, ref in enumerate((q_ref, k_ref, v_ref, o_ref)):
            ref[0:half, :] = first[:, n * width:(n + 1) * width]
            ref[half:, :] = second[:, n * width:(n + 1) * width]
        a, b = first[:, 4 * width:], second[:, 4 * width:]
        lane = lax.broadcasted_iota(i32, a.shape, 1)
        few[0:half, :] = jnp.where(lane == TABLE - 1, a + jnp.broadcast_to(b[:, TABLE:TABLE + 1], a.shape), jnp.where(lane > TABLE, a + b, a))
        few[half:, :] = jnp.where(lane == TABLE - 1, b + jnp.broadcast_to(a[:, TABLE:TABLE + 1], b.shape), b)

    pl.when(at_ref[1] == 0)(lambda: put(mine_ref, other_ref))
    pl.when(at_ref[1] == 1)(lambda: put(other_ref, mine_ref))
    turned = few[...].T
    router_ref[...] = turned[0:experts, :]
    table_ref[...] = turned[TABLE + 1:TABLE + 1 + table_ref.shape[0], 0:table_ref.shape[1]]
    ga_ref[...] = turned[TABLE - 1:TABLE, :] / gain_ref[...].astype(f32)
    gm_ref[...] = turned[TABLE - 2:TABLE - 1, :]


def on_device(size, tokens, segments, routes, capacity, cotangent, rel_table, w_query, w_key, w_value, w_attn_out, gain_attn, gain_moe, w_router, w_in, w_out):
    z = lax.axis_index("expert").astype(i32)
    rep = lax.axis_index("rep").astype(i32)
    pos = lax.axis_index("tensor").astype(i32)
    at = jnp.stack([z, rep, pos])
    tok = tokens[0]
    cot = cotangent[0]
    count, width = tok.shape
    local = w_in.shape[0]
    experts = w_router.shape[1]
    chunks = 2 if local >= 4 else 1
    part = local // chunks
    rows_dev = w_query.shape[0]
    half = rows_dev // 2
    buckets = rel_table.shape[0] * size
    part_rows = part * CAP
    half_rows = part_rows * size // 2
    matrix = order_matrix(size, part, part_rows, 0, 0)

    packed = call(pack_kernel, "pack", [sd((half, 896), bf16)],
                  (at, w_query, w_key, w_value, w_router.T, w_attn_out, gain_attn, gain_moe, rel_table.T),
                  scratch=[pltpu.VMEM((rows_dev, 896), f32)], smem=1)[0]
    mine = [packed] + [to_expert(packed, k, size) for k in range(1, size)]
    idx = call(functools.partial(prepare_kernel, size, chunks), "prepare", [sd((count, 8), i32)], (z[None], routes[0].T, capacity[None]),
               smem=1, deps=(packed,))[0]
    pieces = gather_pieces(tok, count // 2)
    joined = call(join_kernel, "join", [sd((size * half, packed.shape[1]), bf16)], tuple(mine), deps=(*pieces[1:3], idx))[0]
    qkv_w, wo, router, gains, table = unpack(at, mine, to_core(joined), buckets)

    g_blocks = spread(idx, cot, 0, chunks * size, part_rows, (joined,), "spread_g")
    g_arrived = shifted(g_blocks[:size])

    xn, qkv = project(at, pieces, qkv_w, gains)
    g_ordered = [reorder(matrix, g_arrived, "order_g", (qkv,))]
    g_pieces = [gather_pieces(g_ordered[0], half_rows)]
    ready, window = (g_ordered[0],), g_pieces[0][1:3]
    if chunks == 2:
        g_late = shifted([after(b, g_ordered[0]) for b in g_blocks[size:]])
        window = (*window, *g_late[1:])
    o, lse, own, *parts = attn_fwd(at, table, qkv, segments, wo, ready)
    terms = scatter_direct(own, after(parts[0], *window), *parts[1:])
    h, xn2, probs, gate, *blocks = route(idx, tok, terms, router, gains, size, chunks, ())

    arrived = shifted(blocks)
    if chunks == 2:
        g_ordered.append(reorder(matrix, [after(g_late[0], xn2)] + g_late[1:], "order_g", (*blocks[1:], *g_pieces[0][3:])))
        g_pieces.append(gather_pieces(g_ordered[1], half_rows))
    ordered = [reorder(order_matrix(size, part, part_rows + 16, 16, 16), arrived, "order", g_ordered[1:])]
    got = [gather_direct(ordered[0])]
    if chunks == 2:
        blocks = spread(idx, xn2, 1, size, part_rows, (ordered[0], *g_pieces[1][1:]), "spread")
        ordered.append(reorder(matrix, shifted(blocks), "order"))
        got.append(gather_direct(ordered[1]))
    extras = got[0]
    ready = ordered[1:]

    step = max(part // 4, 1)
    pending = [(c, start) for c in range(chunks) for start in range(0, part, step)]
    grads = ()

    def expert_grads(many, *ready):
        nonlocal grads
        mark = ready[0]
        for c, start in pending[:many]:
            *grads, mark = expert_grad(at, c * part, start, step, local, acts[c], other_acts[c], grads, ready)
        del pending[:many]
        return mark

    acts, sums, ys = [], [], []
    dg_full = jnp.zeros((4, lanes_of(size) // 128, 16, 128), f32)
    for c in range(chunks):
        *outs, dg_full, act = moe(at, size, chunks, c, got[c], extras, g_pieces[c], w_in, w_out, dg_full, () if c else ready)
        sums.append(scatter_direct(*outs[:4]) if c < chunks - 1 else outs[:4])
        ys.append(outs[4:])
        acts.append(act)
    other_acts = [to_core(acts[0])]


    def give(c, extra, deps):
        given = call(functools.partial(give_back_kernel, size, extra), "give_back", [sd((part_rows + 16 * extra, width), bf16)] * size,
                     (matrix, *sums[c]), deps=deps)
        return given[0], [given[0]] + [to_expert(given[k], size - k, size) for k in range(1, size)]

    outs = list(sums[-1])
    if chunks == 2:
        outs = [*outs[:1], *[after(piece, *sums[0][1:]) for piece in outs[1:4]]]
    sums[-1] = scatter_direct(*outs)
    back_blocks = []
    mark = outs[0]
    if chunks == 2:
        mark, back_blocks = give(0, False, (mark,))
    mark = expert_grads(2, mark)
    mark = expert_grads(1, mark, *back_blocks[1:])
    if chunks == 2:
        acts[1] = after(acts[1], mark, *sums[-1][1:])
        other_acts.append(to_core(acts[1]))
    ready, blocks = give(chunks - 1, True, (mark,))
    if chunks == 2:
        y_packs = [after(ys[c][1], *sums[-1][1:]) for c in (0, 1)]
        y_got = [to_tensor(pack, flip) for flip, pack in zip((1, 2), y_packs)]
    else:
        y_terms = scatter_direct(*ys[0])
    mark = expert_grads(1, ready)
    ready = (mark, *y_packs) if chunks == 2 else (mark,)
    dh, dhb, small = back(idx, cot, h, xn2, probs, gate, router, gains, back_blocks + blocks, size, chunks, ready)
    dh_pieces = gather_direct(dhb)
    mark = expert_grads(2, dhb)
    small = after(small, mark)
    small = small + to_tensor(small, 1)
    if chunks == 2:
        y_parts, sent = scatter_end(*y_got, ys[1][2], ys[0][2], (mark,))
        mark = sent[0]

    gtab, dqkv = attn_bwd(at, size, table, dh_pieces, segments, wo, qkv, lse, (mark, small))
    small = small + to_tensor(small, 2)
    outs = [sd((local * CAP, width), bf16)] * size
    if chunks == 2:
        given = call(functools.partial(give_back_halves_kernel, size), "give_back_y", outs, (matrix, ys[0][0], ys[1][0], *y_parts), deps=(dqkv, small))
    else:
        given = call(functools.partial(give_back_kernel, size, False), "give_back_y", outs, (matrix, *y_terms), deps=(dqkv,))
    y_blocks = [given[0]] + [to_expert(given[k], size - k, size) for k in range(1, size)]
    keep, send, gain_row, own, *parts = attn_grad(at, size, dqkv, qkv_w, xn, dh_pieces, o, (given[0], small))
    small = small + to_core(small)
    terms = scatter_direct(own, *[after(p, *y_blocks[1:]) for p in parts])
    got = to_core(send)
    grad_tokens = call(last_kernel, "last", [sd((count, width), f32)], (tok, dh, *terms, gains))[0]
    output = mix(idx, h, gate, y_blocks, size, chunks)

    gain_row = gain_row + to_tensor(gain_row, 1)
    gain_row = gain_row + to_tensor(gain_row, 2)
    out_blocks = call(functools.partial(merge_kernel, size), "merge", [sd((half, packed.shape[1]), bf16)] * size,
                      (at, keep, got, small, gain_row, gtab), smem=1,
                      scratch=[pltpu.VMEM((2 * size, half, 128), f32), pltpu.VMEM((2 * size, half, 8), f32)])
    expert_grads(len(pending), out_blocks[0])
    total = call(total_kernel, "total", [sd(out_blocks[0].shape, f32)], tuple(shifted(out_blocks)), deps=(grads[0], *terms[1:]))[0]
    lw = w_query.shape[1]
    outs = [sd((rows_dev, lw), f32)] * 4 + [sd((experts, rows_dev), f32), sd(rel_table.T.shape, f32)] + [sd((1, rows_dev), f32)] * 2
    grad_q, grad_k, grad_v, grad_o, grad_router, grad_table, grad_ga, grad_gm = call(
        finish_kernel, "finish", outs, (at, total, to_core(total), gain_attn[None]), smem=1, scratch=[pltpu.VMEM((rows_dev, 128), f32)])
    return (output[None], grad_tokens[None], grad_table.T, grad_q, grad_k, grad_v, grad_o, grad_ga[0], grad_gm[0], grad_router.T, *grads)


def solution(mesh):
    by_token = P(("expert", "rep"), "tensor", None)
    both = P("expert", "tensor")
    return jax.shard_map(
        functools.partial(on_device, mesh.shape["expert"]),
        mesh=mesh,
        in_specs=(by_token, P(("expert", "rep"), None), by_token, P(), by_token, both, both, both, both, both, P("expert"), P("expert"),
                  P("expert", None), P("expert", None, "tensor"), P("expert", "tensor", None)),
        out_specs=(by_token, by_token, both, both, both, both, both, P("expert"), P("expert"), P("expert", None),
                   P("expert", None, "tensor"), P("expert", "tensor", None)),
        check_vma=False,
    )
```

time: 507 us -> 419 us (0.83)
  waiting for transfers between devices: 180 us -> 97.7 us
  Pallas kernels: 164 us -> 197 us
  between operations: 15 us -> 1.77 us
  starting transfers between devices: 101 us -> 88.8 us
  local copies, waits for them, and re-layouts: 29.5 us -> 22.6 us
  other arithmetic: 10.9 us -> 5.38 us
    ppermute x38 -> x41, waiting for transfers between devices: 115 us -> 52.2 us  [to_tensor(): return lax.ppermute(a, 'tensor', [(i, i ^ flip) for i in range(4)])]
    pallas_call x18 -> x43, Pallas kernels: 120 us -> 142 us  [the longest x25 103 us: call(): pl.pallas_call(body, out_shape=tuple(outs), in_specs=[SM] * smem + [VM] *...]
    ppermute x24 -> x27, waiting for transfers between devices: 65.2 us -> 45.2 us  [to_expert(): lax.ppermute(a, 'expert', [(i, (i + shift) % size) for i in range(size)])]
    ppermute x24 -> x27, starting transfers between devices: 47.2 us -> 35.7 us  [to_expert(): lax.ppermute(a, 'expert', [(i, (i + shift) % size) for i in range(size)])]
    pallas_call x2 -> x8, Pallas kernels: 44.6 us -> 54.6 us  [expert_grad(): pl.pallas_call(functools.partial(expert_grad_kernel, steps), grid=(part,...]
    convert_element_type x9 -> x0, other arithmetic: 6.56 us -> none  [the longest x4 3.35 us: scatter_pieces(): (x_late.astype(f32) + got_y[0].astype(f32)).astype(bf16)]
    ppermute x38 -> x41, starting transfers between devices: 37 us -> 32.5 us  [to_tensor(): return lax.ppermute(a, 'tensor', [(i, i ^ flip) for i in range(4)])]
    ppermute x9 -> x6, starting transfers between devices: 16.5 us -> 20.6 us  [to_core(): return lax.ppermute(a, 'rep', [(0, 1), (1, 0)])]
  transfers between devices with their start and end apart: 73 -> 74, of which waited for: 28 -> 17; matrix products, arithmetic and copies ran while one was open for 6% -> 3% of each run, Pallas kernels for 27% -> 41%
where the time goes in v1:
time: 419 us; the launch traced here: 413 us
  Pallas kernels  197 us (47%)
  waiting for transfers between devices  97.7 us (23%)
  starting transfers between devices  88.8 us (21%)
  local copies, waits for them, and re-layouts  22.6 us (5%)
  other arithmetic  5.38 us (1%)
    pallas_call x25, Pallas kernels, call(): pl.pallas_call(body, out_shape=tuple(outs), in_specs=[SM] * smem + [VM] *...  103 us
    pallas_call x8, Pallas kernels, expert_grad(): pl.pallas_call(functools.partial(expert_grad_kernel, steps), grid=(part,...  54.6 us
    ppermute x41, waiting for transfers between devices, to_tensor(): return lax.ppermute(a, 'tensor', [(i, i ^ flip) for i in range(4)])  52.2 us
    ppermute x27, waiting for transfers between devices, to_expert(): lax.ppermute(a, 'expert', [(i, (i + shift) % size) for i in range(size)])  45.2 us
    pallas_call x2, Pallas kernels, moe(): pl.pallas_call(functools.partial(moe_kernel, rows, part, first, last, len...  39.2 us
    ppermute x27, starting transfers between devices, to_expert(): lax.ppermute(a, 'expert', [(i, (i + shift) % size) for i in range(size)])  35.7 us
    ppermute x41, starting transfers between devices, to_tensor(): return lax.ppermute(a, 'tensor', [(i, i ^ flip) for i in range(4)])  32.5 us
    ppermute x6, starting transfers between devices, to_core(): return lax.ppermute(a, 'rep', [(0, 1), (1, 0)])  20.6 us
  transfers between devices with their start and end apart: 74, of which 17 were waited for; matrix products, arithmetic and copies ran while one was open for 3% of the time, Pallas kernels for 41%

profile of v1, /device:TPU:1, one launch (start us, length us, event | category | flops | bytes accessed | tf_op | source)
XLA Modules:
  0.0 412.7 jit_solution(10051731251722042507)
XLA Ops:
  13.5 8.9 %collective-permute-done.1.refs_2_.refs_3_ = bf16[96,896]{1,0:T(8,128)(2,1)S(1)} collective-permute-done((bf16[96,896]{1,0:T(8,128)(2,1)}, bf16[96,896]{1,0:T(8,128)(2,1)S(1)}, u32[]{:S(2)}, u32[]{:S(2)}) %collective-permute-start.1) | collective-permute-done | bytes 172064 | tf_op jit(solution)/shard_map/ppermute | solution.py:76
  31.8 4.9 %collective-permute-start.10 = (bf16[96,768]{1,0:T(8,128)(2,1)}, bf16[96,768]{1,0:T(8,128)(2,1)S(1)}, u32[]{:S(2)}, u32[]{:S(2)}) collective-permute-start(bf16[96,768]{1,0:T(8,128)(2,1)} %get-tuple-element.128), channel_id=1, source_target_pairs={{0,24},{8,0},{16,8},{24,16},{1,25},{9,1},{17,9},{25,17},{2,26},{10... | collective-permute-start | bytes 442376 | tf_op jit(solution)/shard_map/ppermute | solution.py:76
  58.5 12.3 %attn_fwd.1 = (bf16[1024,192]{1,0:T(8,128)(2,1)}, f32[1024,3]{1,0:T(8,128)}, bf16[256,768]{1,0:T(8,128)(2,1)}, bf16[256,768]{1,0:T(8,128)(2,1)}, bf16[256,768]{1,0:T(8,128)(2,1)}, /*index=5*/bf16[256,768]{1,0:T(8,128)(2,1)}) custom-call(s32[3]{0:T(128)} %pad_add_fusion.refs_0_.at_ref, f32[32,128]{1,0:T(8,128)} %get-tuple-element.120.refs_1_, ...), custom_call_target="tpu_custom_call" | custom-call | flops 14949999616 | bytes 1000 | tf_op jit(solution)/shard_map/attn_fwd/pallas_call | solution.py:48
  77.1 12.2 %collective-permute-done.17.refs_4_ = bf16[256,768]{1,0:T(8,128)(2,1)S(1)} collective-permute-done((bf16[256,768]{1,0:T(8,128)(2,1)}, bf16[256,768]{1,0:T(8,128)(2,1)S(1)}, u32[]{:S(2)}, u32[]{:S(2)}) %collective-permute-start.17) | collective-permute-done | bytes 393248 | tf_op jit(solution)/shard_map/ppermute | solution.py:72
  103.0 6.4 %collective-permute-done.27.refs_3_.g_px = bf16[384,768]{1,0:T(8,128)(2,1)S(1)} collective-permute-done((bf16[384,768]{1,0:T(8,128)(2,1)}, bf16[384,768]{1,0:T(8,128)(2,1)S(1)}, u32[]{:S(2)}, u32[]{:S(2)}) %collective-permute-start.27) | collective-permute-done | bytes 589856 | tf_op jit(solution)/shard_map/ppermute | solution.py:72
  141.2 7.4 %collective-permute-done.26.far.e_d = bf16[400,768]{1,0:T(8,128)(2,1)S(1)} collective-permute-done((bf16[400,768]{1,0:T(8,128)(2,1)}, bf16[400,768]{1,0:T(8,128)(2,1)S(1)}, u32[]{:S(2)}, u32[]{:S(2)}) %collective-permute-start.26) | collective-permute-done | bytes 614432 | tf_op jit(solution)/shard_map/ppermute | solution.py:72
  149.4 19.3 %moe.2 = (bf16[384,768]{1,0:T(8,128)(2,1)}, bf16[384,768]{1,0:T(8,128)(2,1)}, bf16[384,768]{1,0:T(8,128)(2,1)}, bf16[384,768]{1,0:T(8,128)(2,1)}, bf16[384,768]{...) custom-call(s32[3]{0:T(128)} %pad_add_fusion.refs_0_.at_ref, ...), custom_call_target="tpu_custom_call" | custom-call | flops 344999985152 | bytes 1000 | tf_op jit(solution)/shard_map/moe/pallas_call | solution.py:647
  171.8 12.4 %collective-permute-start.45 = (bf16[4,8,4,48,768]{4,3,2,1,0:T(8,128)(2,1)}, bf16[4,8,4,48,768]{4,3,2,1,0:T(8,128)(2,1)}, u32[]{:S(2)}, u32[]{:S(2)}) collective-permute-start(bf16[4,8,4,48,768]{4,3,2,1,0:T(8,128)(2,1)} %get-tuple-element.163.mine), channel_id=1, source_target_pairs={{0,1},{1,0},{2,3},{3,2},{4,5},{5,4},{6,7},{7,6},{8,9},{9,8},{10,11... | collective-permute-start | bytes 28311560 | tf_op jit(solution)/shard_map/ppermute | solution.py:80
  184.1 19.9 %moe.3 = (bf16[400,768]{1,0:T(8,128)(2,1)}, bf16[400,768]{1,0:T(8,128)(2,1)}, bf16[400,768]{1,0:T(8,128)(2,1)}, bf16[400,768]{1,0:T(8,128)(2,1)}, bf16[384,768]{...) custom-call(s32[3]{0:T(128)} %pad_add_fusion.refs_0_.at_ref, ...), custom_call_target="tpu_custom_call" | custom-call | flops 344999985152 | bytes 1000 | tf_op jit(solution)/shard_map/moe/pallas_call | solution.py:647
  212.5 6.7 %expert_grad.8 = (f32[16,768,768]{2,1,0:T(8,128)}, f32[16,768,768]{2,1,0:T(8,128)}, f32[8,128]{1,0:T(8,128)}) custom-call(s32[3]{0:T(128)} %pad_add_fusion.refs_0_.at_ref, bf16[4,8,4,48,768]{4,3,2,1,0:T(8,128)(2,1)} %get-tuple-element.163.mine, bf16[4,8,4,48,768]{4,3,2,1,0:T(8,128)(2,1)} %collective-permute-done.45.other, ...), custom_call_target="tpu_custom_call" | custom-call | flops 34500001792 | bytes 1000 | tf_op jit(solution)/shard_map/expert_grad/pallas_call | solution.py:689
  219.2 6.8 %expert_grad.9 = (f32[16,768,768]{2,1,0:T(8,128)}, f32[16,768,768]{2,1,0:T(8,128)}, f32[8,128]{1,0:T(8,128)}) custom-call(s32[3]{0:T(128)} %pad_add_fusion.refs_0_.at_ref, bf16[4,8,4,48,768]{4,3,2,1,0:T(8,128)(2,1)} %get-tuple-element.163.mine, ...), custom_call_target="tpu_custom_call", output_to_operand_aliasing={{0}: (3, {}), {1}: (4, {})} | custom-call | flops 34500001792 | bytes 1000 | tf_op jit(solution)/shard_map/expert_grad/pallas_call | solution.py:689
  227.8 6.7 %expert_grad.10 = (f32[16,768,768]{2,1,0:T(8,128)}, f32[16,768,768]{2,1,0:T(8,128)}, f32[8,128]{1,0:T(8,128)}) custom-call(s32[3]{0:T(128)} %pad_add_fusion.refs_0_.at_ref, bf16[4,8,4,48,768]{4,3,2,1,0:T(8,128)(2,1)} %get-tuple-element.163.mine, ...), custom_call_target="tpu_custom_call", output_to_operand_aliasing={{0}: (3, {}), {1}: (4, {})} | custom-call | flops 34500001792 | bytes 1000 | tf_op jit(solution)/shard_map/expert_grad/pallas_call | solution.py:689
  234.5 6.3 %collective-permute-done.41.refs_2_.refs_3_ = bf16[400,768]{1,0:T(8,128)(2,1)S(1)} collective-permute-done((bf16[400,768]{1,0:T(8,128)(2,1)}, bf16[400,768]{1,0:T(8,128)(2,1)S(1)}, u32[]{:S(2)}, u32[]{:S(2)}) %collective-permute-start.41) | collective-permute-done | bytes 614432 | tf_op jit(solution)/shard_map/ppermute | solution.py:72
  250.1 6.9 %expert_grad.11 = (f32[16,768,768]{2,1,0:T(8,128)}, f32[16,768,768]{2,1,0:T(8,128)}, f32[8,128]{1,0:T(8,128)}) custom-call(s32[3]{0:T(128)} %pad_add_fusion.refs_0_.at_ref, bf16[4,8,4,48,768]{4,3,2,1,0:T(8,128)(2,1)} %get-tuple-element.163.mine, ...), custom_call_target="tpu_custom_call", output_to_operand_aliasing={{0}: (3, {}), {1}: (4, {})} | custom-call | flops 34500001792 | bytes 1000 | tf_op jit(solution)/shard_map/expert_grad/pallas_call | solution.py:689
  257.0 8.4 %collective-permute-done.51.refs_14_ = bf16[112,768]{1,0:T(8,128)(2,1)S(1)} collective-permute-done((bf16[112,768]{1,0:T(8,128)(2,1)}, bf16[112,768]{1,0:T(8,128)(2,1)S(1)}, u32[]{:S(2)}, u32[]{:S(2)}) %collective-permute-start.51) | collective-permute-done | bytes 172064 | tf_op jit(solution)/shard_map/ppermute | solution.py:76
  266.1 4.9 %back.1 = (f32[256,768]{1,0:T(8,128)}, bf16[256,768]{1,0:T(8,128)(2,1)}, bf16[768,128]{1,0:T(8,128)(2,1)}) custom-call(s32[256,8]{1,0:T(8,128)} %prepare.1.refs_6_.refs_0_, bf16[256,768]{1,0:T(8,128)(2,1)} %bitcast.18, f32[256,768]{1,0:T(8,128)} %get-tuple-element.137.refs_2_.refs_1_, bf16[256,768]{1,0:T(8,128)(2,1)} %get-tuple-element.144.refs_1_.refs_3_, ...), custom_call_target="tpu_custom_call" | custom-call | flops 5750000128 | bytes 1000 | tf_op jit(solution)/shard_map/back/pallas_call | solution.py:48
  273.7 6.7 %expert_grad.12 = (f32[16,768,768]{2,1,0:T(8,128)}, f32[16,768,768]{2,1,0:T(8,128)}, f32[8,128]{1,0:T(8,128)}) custom-call(s32[3]{0:T(128)} %pad_add_fusion.refs_0_.at_ref, bf16[4,8,4,48,768]{4,3,2,1,0:T(8,128)(2,1)} %after.27.mine, bf16[4,8,4,48,768]{4,3,2,1,0:T(8,128)(2,1)} %collective-permute-done.49.other, ...), custom_call_target="tpu_custom_call", output_to_operand_aliasing={{0}: (3, {}), {1}: (4, {})} | custom-call | flops 34500001792 | bytes 1000 | tf_op jit(solution)/shard_map/expert_grad/pallas_call | solution.py:689
  280.4 6.9 %expert_grad.13 = (f32[16,768,768]{2,1,0:T(8,128)}, f32[16,768,768]{2,1,0:T(8,128)}, f32[8,128]{1,0:T(8,128)}) custom-call(s32[3]{0:T(128)} %pad_add_fusion.refs_0_.at_ref, bf16[4,8,4,48,768]{4,3,2,1,0:T(8,128)(2,1)} %after.27.mine, bf16[4,8,4,48,768]{4,3,2,1,0:T(8,128)(2,1)} %collective-permute-done.49.other, ...), custom_call_target="tpu_custom_call", output_to_operand_aliasing={{0}: (3, {}), {1}: (4, {})} | custom-call | flops 34500001792 | bytes 1000 | tf_op jit(solution)/shard_map/expert_grad/pallas_call | solution.py:689
  292.5 12.0 %collective-permute-done.58 = bf16[768,128]{1,0:T(8,128)(2,1)S(1)} collective-permute-done((bf16[768,128]{1,0:T(8,128)(2,1)}, bf16[768,128]{1,0:T(8,128)(2,1)S(1)}, u32[]{:S(2)}, u32[]{:S(2)}) %collective-permute-start.58) | collective-permute-done | bytes 196640 | tf_op jit(solution)/shard_map/ppermute | solution.py:72
  306.5 18.1 %attn_bwd.1 = (f32[4,8,128]{2,1,0:T(8,128)}, bf16[1024,576]{1,0:T(8,128)(2,1)}) custom-call(s32[3]{0:T(128)} %pad_add_fusion.refs_0_.at_ref, f32[32,128]{1,0:T(8,128)} %get-tuple-element.120.refs_1_, bf16[256,768]{1,0:T(8,128)(2,1)} %get-tuple-element.186.refs_2_.refs_4_, bf16[256,768]{1,0:T(8,128)(2,1)} %collective-permute-done.55.refs_3_.refs_5_, ...), custom_call_target="tpu_custom_call" | custom-call | flops 20700000256 | bytes 1000 | tf_op jit(solution)/shard_map/attn_bwd/pallas_call | solution.py:48
  331.5 8.2 %attn_grad.1 = (bf16[4,96,768]{2,1,0:T(8,128)(2,1)}, bf16[4,96,768]{2,1,0:T(8,128)(2,1)}, f32[8,768]{1,0:T(8,128)}, bf16[256,768]{1,0:T(8,128)(2,1)}, bf16[256,7...) custom-call(s32[3]{0:T(128)} %pad_add_fusion.refs_0_.at_ref, ...), custom_call_target="tpu_custom_call" | custom-call | flops 10350000128 | bytes 1000 | tf_op jit(solution)/shard_map/attn_grad/pallas_call | solution.py:48
  356.8 17.0 %collective-permute-done.61.refs_5_.refs_2_ = bf16[192,768]{1,0:T(8,128)(2,1)S(1)} collective-permute-done((bf16[192,768]{1,0:T(8,128)(2,1)S(1)}, bf16[192,768]{1,0:T(8,128)(2,1)S(1)}, u32[]{:S(2)}, u32[]{:S(2)}) %collective-permute-start.61) | collective-permute-done | bytes 294944 | tf_op jit(solution)/shard_map/ppermute | solution.py:76
  381.1 6.8 %expert_grad.14 = (f32[16,768,768]{2,1,0:T(8,128)}, f32[16,768,768]{2,1,0:T(8,128)}, f32[8,128]{1,0:T(8,128)}) custom-call(s32[3]{0:T(128)} %pad_add_fusion.refs_0_.at_ref, bf16[4,8,4,48,768]{4,3,2,1,0:T(8,128)(2,1)} %after.27.mine, bf16[4,8,4,48,768]{4,3,2,1,0:T(8,128)(2,1)} %collective-permute-done.49.other, ...), custom_call_target="tpu_custom_call", output_to_operand_aliasing={{0}: (3, {}), {1}: (4, {})} | custom-call | flops 34500001792 | bytes 1000 | tf_op jit(solution)/shard_map/expert_grad/pallas_call | solution.py:689
  390.8 7.0 %expert_grad.15 = (f32[16,768,768]{2,1,0:T(8,128)}, f32[16,768,768]{2,1,0:T(8,128)}, f32[8,128]{1,0:T(8,128)}) custom-call(s32[3]{0:T(128)} %pad_add_fusion.refs_0_.at_ref, bf16[4,8,4,48,768]{4,3,2,1,0:T(8,128)(2,1)} %after.27.mine, bf16[4,8,4,48,768]{4,3,2,1,0:T(8,128)(2,1)} %collective-permute-done.49.other, ...), custom_call_target="tpu_custom_call", output_to_operand_aliasing={{0}: (3, {}), {1}: (4, {})} | custom-call | flops 34500001792 | bytes 1000 | tf_op jit(solution)/shard_map/expert_grad/pallas_call | solution.py:689
  (323 shorter events, 177.8 us)
Async XLA Ops:
  0.6 21.8 %collective-permute-start.3 = (bf16[256,768]{1,0:T(8,128)(2,1)}, bf16[256,768]{1,0:T(8,128)(2,1)S(1)}, u32[]{:S(2)}, u32[]{:S(2)}) collective-permute-start(bf16[256,768]{1,0:T(8,128)(2,1)} %bitcast.19), channel_id=1, source_target_pairs={{0,2},{2,0},{4,6},{6,4},{1,3},{3,1},{5,7},{7,5},{8,10},{10,8},{12,... | collective-permute-start | bytes 1179656 | tf_op jit(solution)/shard_map/ppermute | solution.py:72
  126.5 22.0 %collective-permute-start.26 = (bf16[400,768]{1,0:T(8,128)(2,1)}, bf16[400,768]{1,0:T(8,128)(2,1)S(1)}, u32[]{:S(2)}, u32[]{:S(2)}) collective-permute-start(bf16[400,768]{1,0:T(8,128)(2,1)} %order.2.refs_2_.own.e_own), channel_id=1, source_target_pairs={{0,6},{2,4},{4,2},{6,0},{1,7},{3,5},{5,3},{7,1},{8,14},{10,12},{12... | collective-permute-start | bytes 1843208 | tf_op jit(solution)/shard_map/ppermute | solution.py:72
  138.5 32.0 %collective-permute-start.34 = (bf16[384,768]{1,0:T(8,128)(2,1)}, bf16[384,768]{1,0:T(8,128)(2,1)}, u32[]{:S(2)}, u32[]{:S(2)}) collective-permute-start(bf16[384,768]{1,0:T(8,128)(2,1)} %order.3.refs_0_.own), channel_id=1, source_target_pairs={{0,2},{2,0},{4,6},{6,4},{1,3},{3,1},{5,7},{7,5},{8,10},{10,8},{12,... | collective-permute-start | bytes 1769480 | tf_op jit(solution)/shard_map/ppermute | solution.py:72
  139.7 32.1 %collective-permute-start.35 = (bf16[384,768]{1,0:T(8,128)(2,1)}, bf16[384,768]{1,0:T(8,128)(2,1)}, u32[]{:S(2)}, u32[]{:S(2)}) collective-permute-start(bf16[384,768]{1,0:T(8,128)(2,1)} %order.3.refs_0_.own), channel_id=1, source_target_pairs={{0,4},{2,6},{4,0},{6,2},{1,5},{3,7},{5,1},{7,3},{8,12},{10,14},{12... | collective-permute-start | bytes 1769480 | tf_op jit(solution)/shard_map/ppermute | solution.py:72
  140.3 43.9 %collective-permute-start.36 = (bf16[384,768]{1,0:T(8,128)(2,1)}, bf16[384,768]{1,0:T(8,128)(2,1)}, u32[]{:S(2)}, u32[]{:S(2)}) collective-permute-start(bf16[384,768]{1,0:T(8,128)(2,1)} %order.3.refs_0_.own), channel_id=1, source_target_pairs={{0,6},{2,4},{4,2},{6,0},{1,7},{3,5},{5,3},{7,1},{8,14},{10,12},{12... | collective-permute-start | bytes 1769480 | tf_op jit(solution)/shard_map/ppermute | solution.py:72
  168.7 35.4 %collective-permute-start.37 = (bf16[384,768]{1,0:T(8,128)(2,1)}, bf16[384,768]{1,0:T(8,128)(2,1)}, u32[]{:S(2)}, u32[]{:S(2)}) collective-permute-start(bf16[384,768]{1,0:T(8,128)(2,1)} %get-tuple-element.154), channel_id=1, source_target_pairs={{0,2},{2,0},{4,6},{6,4},{1,3},{3,1},{5,7},{7,5},{8,10},{10,8},{12,... | collective-permute-start | bytes 1769480 | tf_op jit(solution)/shard_map/ppermute | solution.py:72
  170.5 33.6 %collective-permute-start.38 = (bf16[384,768]{1,0:T(8,128)(2,1)}, bf16[384,768]{1,0:T(8,128)(2,1)}, u32[]{:S(2)}, u32[]{:S(2)}) collective-permute-start(bf16[384,768]{1,0:T(8,128)(2,1)} %get-tuple-element.155), channel_id=1, source_target_pairs={{0,4},{2,6},{4,0},{6,2},{1,5},{3,7},{5,1},{7,3},{8,12},{10,14},{12... | collective-permute-start | bytes 1769480 | tf_op jit(solution)/shard_map/ppermute | solution.py:72
  170.5 33.6 %collective-permute-start.39 = (bf16[384,768]{1,0:T(8,128)(2,1)}, bf16[384,768]{1,0:T(8,128)(2,1)}, u32[]{:S(2)}, u32[]{:S(2)}) collective-permute-start(bf16[384,768]{1,0:T(8,128)(2,1)} %get-tuple-element.156), channel_id=1, source_target_pairs={{0,6},{2,4},{4,2},{6,0},{1,7},{3,5},{5,3},{7,1},{8,14},{10,12},{12... | collective-permute-start | bytes 1769480 | tf_op jit(solution)/shard_map/ppermute | solution.py:72
  171.8 40.6 %collective-permute-start.45 = (bf16[4,8,4,48,768]{4,3,2,1,0:T(8,128)(2,1)}, bf16[4,8,4,48,768]{4,3,2,1,0:T(8,128)(2,1)}, u32[]{:S(2)}, u32[]{:S(2)}) collective-permute-start(bf16[4,8,4,48,768]{4,3,2,1,0:T(8,128)(2,1)} %get-tuple-element.163.mine), channel_id=1, source_target_pairs={{0,1},{1,0},{2,3},{3,2},{4,5},{5,4},{6,7},{7,6},{8,9},{9,8},{10,11... | collective-permute-start | bytes 28311560 | tf_op jit(solution)/shard_map/ppermute | solution.py:80
  210.8 23.7 %collective-permute-start.42 = (bf16[400,768]{1,0:T(8,128)(2,1)}, bf16[400,768]{1,0:T(8,128)(2,1)S(1)}, u32[]{:S(2)}, u32[]{:S(2)}) collective-permute-start(bf16[400,768]{1,0:T(8,128)(2,1)} %after.24), channel_id=1, source_target_pairs={{0,6},{2,4},{4,2},{6,0},{1,7},{3,5},{5,3},{7,1},{8,14},{10,12},{12... | collective-permute-start | bytes 1843208 | tf_op jit(solution)/shard_map/ppermute | solution.py:72
  212.4 28.5 %collective-permute-start.41 = (bf16[400,768]{1,0:T(8,128)(2,1)}, bf16[400,768]{1,0:T(8,128)(2,1)S(1)}, u32[]{:S(2)}, u32[]{:S(2)}) collective-permute-start(bf16[400,768]{1,0:T(8,128)(2,1)} %after.23), channel_id=1, source_target_pairs={{0,4},{2,6},{4,0},{6,2},{1,5},{3,7},{5,1},{7,3},{8,12},{10,14},{12... | collective-permute-start | bytes 1843208 | tf_op jit(solution)/shard_map/ppermute | solution.py:72
  241.9 30.0 %collective-permute-start.49 = (bf16[4,8,4,48,768]{4,3,2,1,0:T(8,128)(2,1)}, bf16[4,8,4,48,768]{4,3,2,1,0:T(8,128)(2,1)}, u32[]{:S(2)}, u32[]{:S(2)}) collective-permute-start(bf16[4,8,4,48,768]{4,3,2,1,0:T(8,128)(2,1)} %after.27.mine), channel_id=1, source_target_pairs={{0,1},{1,0},{2,3},{3,2},{4,5},{5,4},{6,7},{7,6},{8,9},{9,8},{10,11... | collective-permute-start | bytes 28311560 | tf_op jit(solution)/shard_map/ppermute | solution.py:80
  243.2 44.2 %collective-permute-start.44 = (bf16[2,384,768]{2,1,0:T(8,128)(2,1)}, bf16[2,384,768]{2,1,0:T(8,128)(2,1)S(1)}, u32[]{:S(2)}, u32[]{:S(2)}) collective-permute-start(bf16[2,384,768]{2,1,0:T(8,128)(2,1)} %after.26.refs_18_), channel_id=1, source_target_pairs={{0,4},{2,6},{4,0},{6,2},{1,5},{3,7},{5,1},{7,3},{8,12},{10,14},{12... | collective-permute-start | bytes 3538952 | tf_op jit(solution)/shard_map/ppermute | solution.py:72
  257.0 30.6 %collective-permute-start.43 = (bf16[2,384,768]{2,1,0:T(8,128)(2,1)S(1)}, bf16[2,384,768]{2,1,0:T(8,128)(2,1)S(1)}, u32[]{:S(2)}, u32[]{:S(2)}) collective-permute-start(bf16[2,384,768]{2,1,0:T(8,128)(2,1)S(1)} %copy-done.8), channel_id=1, source_target_pairs={{0,2},{2,0},{4,6},{6,4},{1,3},{3,1},{5,7},{7,5},{8,10},{10,8},{12,... | collective-permute-start | bytes 3538952 | tf_op jit(solution)/shard_map/ppermute | solution.py:72
  271.0 34.5 %collective-permute-start.55 = (bf16[256,768]{1,0:T(8,128)(2,1)}, bf16[256,768]{1,0:T(8,128)(2,1)}, u32[]{:S(2)}, u32[]{:S(2)}) collective-permute-start(bf16[256,768]{1,0:T(8,128)(2,1)} %get-tuple-element.186.refs_2_.refs_4_), channel_id=1, source_target_pairs={{0,2},{2,0},{4,6},{6,4},{1,3},{3,1},{5,7},{7,5},{8,10},{10,8},{12,... | collective-permute-start | bytes 1179656 | tf_op jit(solution)/shard_map/ppermute | solution.py:72
  271.1 35.4 %collective-permute-start.56 = (bf16[256,768]{1,0:T(8,128)(2,1)}, bf16[256,768]{1,0:T(8,128)(2,1)}, u32[]{:S(2)}, u32[]{:S(2)}) collective-permute-start(bf16[256,768]{1,0:T(8,128)(2,1)} %get-tuple-element.186.refs_2_.refs_4_), channel_id=1, source_target_pairs={{0,4},{2,6},{4,0},{6,2},{1,5},{3,7},{5,1},{7,3},{8,12},{10,14},{12... | collective-permute-start | bytes 1179656 | tf_op jit(solution)/shard_map/ppermute | solution.py:72
  271.9 34.6 %collective-permute-start.57 = (bf16[256,768]{1,0:T(8,128)(2,1)}, bf16[256,768]{1,0:T(8,128)(2,1)}, u32[]{:S(2)}, u32[]{:S(2)}) collective-permute-start(bf16[256,768]{1,0:T(8,128)(2,1)} %get-tuple-element.186.refs_2_.refs_4_), channel_id=1, source_target_pairs={{0,6},{2,4},{4,2},{6,0},{1,7},{3,5},{5,3},{7,1},{8,14},{10,12},{12... | collective-permute-start | bytes 1179656 | tf_op jit(solution)/shard_map/ppermute | solution.py:72
  292.0 34.3 %collective-permute-start.53 = (bf16[384,768]{1,0:T(8,128)(2,1)}, bf16[384,768]{1,0:T(8,128)(2,1)S(1)}, u32[]{:S(2)}, u32[]{:S(2)}) collective-permute-start(bf16[384,768]{1,0:T(8,128)(2,1)} %get-tuple-element.190), channel_id=1, source_target_pairs={{0,4},{2,6},{4,0},{6,2},{1,5},{3,7},{5,1},{7,3},{8,12},{10,14},{12... | collective-permute-start | bytes 1769480 | tf_op jit(solution)/shard_map/ppermute | solution.py:72
  304.5 21.7 %collective-permute-start.54 = (bf16[384,768]{1,0:T(8,128)(2,1)}, bf16[384,768]{1,0:T(8,128)(2,1)S(1)}, u32[]{:S(2)}, u32[]{:S(2)}) collective-permute-start(bf16[384,768]{1,0:T(8,128)(2,1)} %get-tuple-element.191.refs_10_), channel_id=1, source_target_pairs={{0,2},{2,0},{4,6},{6,4},{1,3},{3,1},{5,7},{7,5},{8,10},{10,8},{12,... | collective-permute-start | bytes 1769480 | tf_op jit(solution)/shard_map/ppermute | solution.py:72
  339.8 37.6 %collective-permute-start.66 = (bf16[4,96,768]{2,1,0:T(8,128)(2,1)}, bf16[4,96,768]{2,1,0:T(8,128)(2,1)S(1)}, u32[]{:S(2)}, u32[]{:S(2)}) collective-permute-start(bf16[4,96,768]{2,1,0:T(8,128)(2,1)} %get-tuple-element.207), channel_id=1, source_target_pairs={{0,1},{1,0},{2,3},{3,2},{4,5},{5,4},{6,7},{7,6},{8,9},{9,8},{10,11... | collective-permute-start | bytes 1769480 | tf_op jit(solution)/shard_map/ppermute | solution.py:80
  345.6 28.3 %collective-permute-start.61 = (bf16[192,768]{1,0:T(8,128)(2,1)S(1)}, bf16[192,768]{1,0:T(8,128)(2,1)S(1)}, u32[]{:S(2)}, u32[]{:S(2)}) collective-permute-start(bf16[192,768]{1,0:T(8,128)(2,1)S(1)} %copy-done.43), channel_id=1, source_target_pairs={{0,16},{8,24},{16,0},{24,8},{1,17},{9,25},{17,1},{25,9},{2,18},{10... | collective-permute-start | bytes 884744 | tf_op jit(solution)/shard_map/ppermute | solution.py:76
  347.8 26.0 %collective-permute-start.62 = (bf16[192,768]{1,0:T(8,128)(2,1)S(1)}, bf16[192,768]{1,0:T(8,128)(2,1)S(1)}, u32[]{:S(2)}, u32[]{:S(2)}) collective-permute-start(bf16[192,768]{1,0:T(8,128)(2,1)S(1)} %copy-done.42), channel_id=1, source_target_pairs={{0,8},{8,16},{16,24},{24,0},{1,9},{9,17},{17,25},{25,1},{2,10},{10... | collective-permute-start | bytes 884744 | tf_op jit(solution)/shard_map/ppermute | solution.py:76
  376.5 21.4 %collective-permute-start.64 = (bf16[256,768]{1,0:T(8,128)(2,1)}, bf16[256,768]{1,0:T(8,128)(2,1)S(1)}, u32[]{:S(2)}, u32[]{:S(2)}) collective-permute-start(bf16[256,768]{1,0:T(8,128)(2,1)} %after.30), channel_id=1, source_target_pairs={{0,4},{2,6},{4,0},{6,2},{1,5},{3,7},{5,1},{7,3},{8,12},{10,14},{12... | collective-permute-start | bytes 1179656 | tf_op jit(solution)/shard_map/ppermute | solution.py:72
  376.8 21.1 %collective-permute-start.63 = (bf16[256,768]{1,0:T(8,128)(2,1)}, bf16[256,768]{1,0:T(8,128)(2,1)S(1)}, u32[]{:S(2)}, u32[]{:S(2)}) collective-permute-start(bf16[256,768]{1,0:T(8,128)(2,1)} %after.29), channel_id=1, source_target_pairs={{0,2},{2,0},{4,6},{6,4},{1,3},{3,1},{5,7},{7,5},{8,10},{10,8},{12,... | collective-permute-start | bytes 1179656 | tf_op jit(solution)/shard_map/ppermute | solution.py:72
  (117 other events, 911.3 us)

commit v2 on v1

--- a/solution.py
+++ b/solution.py
@@ -32,11 +32,11 @@
 
 
 ANY = pl.BlockSpec(memory_space=pl.ANY)
-TIMES = {"attn_fwd": 13, "attn_bwd": 18, "attn_grad": 9, "project": 5, "moe": 300, "expert_grad": 30, "back": 5, "route": 4}
+TIMES = {"attn_fwd": 13, "attn_bwd": 400, "attn_grad": 9, "project": 5, "moe": 300, "expert_grad": 1, "back": 5, "route": 4}
 
 
 def cost(name):
-    return pl.CostEstimate(flops=TIMES.get(name, 3) * 1_150_000_000, bytes_accessed=1000, transcendentals=0)
+    return pl.CostEstimate(flops=int(TIMES.get(name, 0.5) * 1_150_000_000), bytes_accessed=1000, transcendentals=0)
 
 
 def call(kernel, name, outs, operands, scratch=(), smem=0, flops=0, moved=4_000_000, deps=()):
@@ -154,18 +154,19 @@
         idx_ref[:, n:n + 1] = column
 
 
-def spread_kernel(first, idx_ref, rows_ref, *outs):
-    block = outs[0].shape[0]
-    width = block * len(outs)
+def spread_kernel(first, chunks, idx_ref, rows_ref, *outs):
+    count = len(outs)
+    block = outs[0].shape[0] // chunks
+    width = block * chunks * count
     spread = as_bf16(onehot(idx_ref[:, 1:2] - first, width)) + as_bf16(onehot(idx_ref[:, 5:6] - first, width))
     slots = dot(spread, rows_ref[...], TN).astype(bf16)
-    for n, ref in enumerate(outs):
-        ref[...] = slots[n * block:(n + 1) * block]
-
-
-def spread(idx, rows, chunk, blocks, block, deps, name):
-    return call(functools.partial(spread_kernel, chunk * blocks * block), name, [sd((block, rows.shape[1]), bf16)] * blocks, (idx, rows),
-                flops=400_000_000, moved=2_000_000, deps=deps)
+    for c in range(chunks):
+        for k, ref in enumerate(outs):
+            ref[c * block:(c + 1) * block, :] = slots[(c * count + k) * block:(c * count + k + 1) * block]
+
+
+def spread(idx, rows, chunk, count, block, deps, name, chunks):
+    return call(functools.partial(spread_kernel, chunk * count * block, chunks), name, [sd((block, rows.shape[1]), bf16)] * count, (idx, rows), deps=deps)
 
 
 def order_matrix(size, part, block, extra, out_extra):
@@ -186,6 +187,15 @@
     out_ref[...] = dot(m_ref[...], jnp.concatenate([b[...] for b in blocks], axis=0)).astype(bf16)
 
 
+def reorder_all_kernel(count, m_ref, *refs):
+    blocks, out_ref = refs[:count], refs[count]
+    block = m_ref.shape[1] // count
+    rows = m_ref.shape[0]
+    for c in range(out_ref.shape[0] // rows):
+        chosen = jnp.concatenate([b[c * block:(c + 1) * block, :] for b in blocks], axis=0)
+        out_ref[c * rows:(c + 1) * rows, :] = dot(m_ref[...], chosen).astype(bf16)
+
+
 def reorder(matrix, blocks, name, deps=()):
     rows = matrix.shape[0]
     width = blocks[0].shape[1]
@@ -214,7 +224,7 @@
             outs[k][n * block:(n + 1) * block, :] = back[k * block:(k + 1) * block]
 
 
-def pack_kernel(at_ref, q_ref, k_ref, v_ref, r_ref, o_ref, ga_ref, gm_ref, t_ref, out_ref, full):
+def pack_kernel(at_ref, q_ref, k_ref, v_ref, r_ref, o_ref, ga_ref, gm_ref, t_ref, out_ref, rest_ref, full):
     rows, width = q_ref.shape
     full[...] = jnp.zeros_like(full)
     place = 0
@@ -232,23 +242,18 @@
         @pl.when(at_ref[1] == r)
         def _():
             out_ref[...] = full[r * half:(r + 1) * half, :].astype(bf16)
-
-
-def join_kernel(*refs):
-    rows = refs[0].shape[0]
-    for n, ref in enumerate(refs[:-1]):
-        refs[-1][n * rows:(n + 1) * rows, :] = ref[...]
+            rest_ref[...] = full[(1 - r) * half:(2 - r) * half, :].astype(bf16)
 
 
 def unpack_kernel(size, at_ref, *refs):
-    mine, other = refs[:size], refs[size]
-    full, qkv_ref, wo_ref, router_ref, gains_ref, table_ref = refs[size + 1:]
+    mine, other = refs[:size], refs[size:2 * size]
+    full, qkv_ref, wo_ref, router_ref, gains_ref, table_ref = refs[2 * size:]
     me, rep = at_ref[0], at_ref[1]
     half = mine[0].shape[0]
     for k in range(size):
         z = (me - k + size) & (size - 1)
         full[2 * z + rep] = mine[k][...].astype(f32)
-        full[2 * z + 1 - rep] = other[k * half:(k + 1) * half, :].astype(f32)
+        full[2 * z + 1 - rep] = other[k][...].astype(f32)
     full = jnp.concatenate([full[n] for n in range(2 * size)], axis=0)
     qkv_ref[...] = full[:, 0:576].astype(bf16)
     router_ref[...] = full[:, 576:640].astype(bf16)
@@ -261,16 +266,16 @@
         table_ref[z * rows:(z + 1) * rows, :] = tail[z * 2 * half: z * 2 * half + rows, :]
 
 
-def unpack(at, mine, other, buckets):
+def unpack(at, mine, other, buckets, deps):
     size = len(mine)
     half, cols = mine[0].shape
     width = 2 * half * size
 
     def kernel(at_ref, *refs):
-        unpack_kernel(size, at_ref, *refs[:size + 1], refs[-1], *refs[size + 1:-1])
+        unpack_kernel(size, at_ref, *refs[:2 * size], refs[-1], *refs[2 * size:-1])
 
     outs = [sd((width, 576), bf16), sd((width, 192), bf16), sd((width, 64), bf16), sd((8, width), f32), sd((buckets, 128), f32)]
-    return call(kernel, "unpack", outs, (at, *mine, other), scratch=[pltpu.VMEM((2 * size, half, cols), f32)], smem=1)
+    return call(kernel, "unpack", outs, (at, *mine, *other), scratch=[pltpu.VMEM((2 * size, half, cols), f32)], smem=1, deps=deps)
 
 
 def piece_shapes(rows, width):
@@ -433,7 +438,7 @@
             gtab_ref[b // per, b % per:b % per + 1, TABLE + 1 + h:TABLE + 2 + h] = one + rest if b == buckets - 1 else one
 
 
-def attn_grad_kernel(size, at_ref, dqkv, w_ref, xn_ref, own_ref, px_ref, py_ref, pd_ref, o_ref, keep_ref, send_ref, gain_ref,
+def attn_grad_kernel(size, at_ref, dqkv, w_ref, xn_ref, own_ref, px_ref, py_ref, pd_ref, o_ref, small_ref, gtab_ref, keep_ref, send_ref,
                      out_own, out_x, out_y, out_d, dh, full):
     pos, rep = at_ref[2], at_ref[1]
     tok = out_own.shape[0]
@@ -451,22 +456,25 @@
     for flip, ref in enumerate((out_own, out_x, out_y, out_d)):
         ref[...] = dot(dqkv[at(flip), :], w, NT).astype(bf16)
     grad = dot(xn_ref[...], dqkv[...], TN)
-    gain_sum = jnp.sum(grad * w.astype(f32), axis=1, keepdims=True)
-    gain_ref[...] = jnp.broadcast_to(gain_sum, (gain_sum.shape[0], 128)).T[0:8, :]
     grad_out = dot(dh[...], o_ref[...], TN)
     part_rows = keep_ref.shape[1]
     for n in range(2 * size):
         full[n, :, 0:3 * width] = grad[n * part_rows:(n + 1) * part_rows].astype(bf16)
-        full[n, :, 3 * width:] = grad_out[n * part_rows:(n + 1) * part_rows].astype(bf16)
+        full[n, :, 3 * width:4 * width] = grad_out[n * part_rows:(n + 1) * part_rows].astype(bf16)
+        few = small_ref[n * part_rows:(n + 1) * part_rows, :]
+        full[n, :, 4 * width:] = few
+        if n % 2 == 0:
+            rows = gtab_ref.shape[1]
+            full[n, 0:rows, 4 * width:] = (few[0:rows].astype(f32) + gtab_ref[n // 2]).astype(bf16)
     for z in range(size):
         keep_ref[z] = full[2 * z + rep]
         send_ref[z] = full[2 * z + 1 - rep]
 
 
-def project(at, pieces, w, gains):
+def project(at, pieces, w, gains, deps):
     tok, width = pieces[0].shape
     return call(project_kernel, "project", [sd((4 * tok, width), bf16), sd((4 * tok, w.shape[1]), bf16)], (at, *pieces, w, gains),
-                smem=1, flops=2_000_000_000, moved=5_000_000)
+                smem=1, deps=deps)
 
 
 def attn_fwd(at, table, qkv, segr, wo, deps):
@@ -491,12 +499,12 @@
                 scratch=scratch, smem=2, flops=12_000_000_000, moved=8_000_000, deps=deps)
 
 
-def attn_grad(at, size, dqkv, w, xn, pieces, o, deps):
+def attn_grad(at, size, dqkv, w, xn, pieces, o, small, gtab, deps):
     tok, width = pieces[0].shape
-    cols = w.shape[1] + o.shape[1]
+    cols = w.shape[1] + o.shape[1] + small.shape[1]
     rows = width // (2 * size)
-    outs = [sd((size, rows, cols), bf16)] * 2 + [sd((8, width), f32)] + piece_shapes(tok, width)
-    return call(functools.partial(attn_grad_kernel, size), "attn_grad", outs, (at, dqkv, w, xn, *pieces, o),
+    outs = [sd((size, rows, cols), bf16)] * 2 + piece_shapes(tok, width)
+    return call(functools.partial(attn_grad_kernel, size), "attn_grad", outs, (at, dqkv, w, xn, *pieces, o, small, gtab),
                 scratch=[pltpu.VMEM((4 * tok, width), bf16), pltpu.VMEM((2 * size, rows, cols), bf16)], smem=1,
                 flops=4_000_000_000, moved=9_000_000, deps=deps)
 
@@ -547,7 +555,7 @@
                 flops=400_000_000, moved=5_000_000, deps=deps)
 
 
-def moe_kernel(rows, part, offset, last, skip, at_ref, own, px, py, far, e_own, e_px, e_py, e_d, g_own, g_px, g_py, g_d0, g_d1, win_ref, wout_ref,
+def moe_kernel(rows, part, offset, last, skip, at_ref, own, px, py, d0, d1, e_own, e_px, e_py, e_d, g_own, g_px, g_py, g_far, win_ref, wout_ref,
                dg_in, *refs):
     outs, y_outs, dg_ref, acts = refs[skip:skip + 4], refs[skip + 4:-2], refs[-2], refs[-1]
     e, j = pl.program_id(0), pl.program_id(1)
@@ -575,9 +583,9 @@
             ref[at, :] = value[flip * rows:(flip + 1) * rows]
 
     gate = jnp.concatenate([gate_of(r) for r in (e_own, e_px, e_py, e_d)], axis=0)
-    s = jnp.concatenate([own[...], px[...], py[...], far[...]], axis=0)
-    g_far = jnp.where(e < part // 2, g_d0[...].astype(f32), g_d1[...].astype(f32))
-    g = jnp.concatenate([g_own[...].astype(f32), g_px[...].astype(f32), g_py[...].astype(f32), g_far], axis=0)
+    far = jnp.where(e < part // 2, d0[...].astype(f32), d1[...].astype(f32)).astype(bf16)
+    s = jnp.concatenate([own[...], px[...], py[...], far], axis=0)
+    g = jnp.concatenate([g_own[...], g_px[...], g_py[...], g_far[...]], axis=0).astype(f32)
     keep(0, s)
     win, wout = win_ref[0], wout_ref[0]
     dy = (g * gate).astype(bf16)
@@ -621,17 +629,20 @@
     steps = all_rows // rows
     local, width, hidden = w_in.shape
     part = local // chunks
-    half = part // 2
     lanes = -(-all_rows // 128) * 128
     first = chunk * part
     whole = lambda e, j: (e * steps + j, 0)
     flat = pl.BlockSpec((rows, width), whole)
+    of_all = pl.BlockSpec((rows, width), lambda e, j: ((first + e) * steps + j, 0))
+    half = part // 2
     low = pl.BlockSpec((rows, width), lambda e, j: (jnp.where(e < half, e * steps + j, half * steps - 1), 0))
     high = pl.BlockSpec((rows, width), lambda e, j: (jnp.where(e < half, 0, (e - half) * steps + j), 0))
-    ext = pl.BlockSpec((16, lanes), lambda e, j: (part * all_rows // 16, 0))
-    in_specs = [SM] + [flat] * 4 + [ext] * 4 + [flat] * 3 + [low, high]
+    ext = lambda start: pl.BlockSpec((16, lanes), lambda e, j: (start // 16, 0))
+    two_steps = len(pieces) == 5
+    in_specs = [SM] + [flat] * 3 + ([low, high] if two_steps else [flat, flat])
+    in_specs += [ext(part * all_rows)] * 3 + [ext(half * all_rows)] + [of_all] * 3 + [flat]
     in_specs += [pl.BlockSpec((1, width, hidden), lambda e, j: (first + e, 0, 0)), pl.BlockSpec((1, hidden, width), lambda e, j: (first + e, 0, 0))]
-    operands = [at, *pieces, *extras, *g, w_in, w_out]
+    operands = [at, *pieces, *([] if two_steps else pieces[3:]), *extras, *g[:3], g[3 + chunk], w_in, w_out]
     last = chunk == chunks - 1
     shape = (part * all_rows + 16 * last, width)
     total = part * all_rows
@@ -756,10 +767,10 @@
     out_ref[...] = out.astype(bf16)
 
 
-def mix(idx, h, gate, blocks, size, chunks):
+def mix(idx, h, gate, blocks, size, chunks, deps):
     count, width = h.shape
     return call(functools.partial(mix_kernel, len(blocks), chunks), "mix", [sd((count, width), bf16)], (idx, h, gate, *blocks),
-                scratch=[pltpu.VMEM((len(blocks) * blocks[0].shape[0], width), bf16)])[0]
+                scratch=[pltpu.VMEM((len(blocks) * blocks[0].shape[0], width), bf16)], deps=deps)[0]
 
 
 def last_kernel(tokens_ref, dh_ref, own, rx, ry, rd, gains_ref, out_ref):
@@ -769,50 +780,46 @@
     out_ref[...] = dh_ref[...] + r * scaled - x * (r * r * r) * jnp.mean(x * scaled, axis=-1, keepdims=True)
 
 
-def total_kernel(*refs):
-    out = refs[-1]
-    out[...] = sum(r[...].astype(f32) for r in refs[:-1])
-
-
-def merge_kernel(size, at_ref, keep_ref, got_ref, small_ref, gain_ref, gtab_ref, *refs):
-    outs, few, gains = refs[:size], refs[size], refs[size + 1]
-    me, rep = at_ref[0], at_ref[1]
-    half, width = keep_ref.shape[1:]
-    rows = gtab_ref.shape[1]
-    column = gain_ref[...].T
-    for n in range(2 * size):
-        few[n] = small_ref[n * half:(n + 1) * half, :].astype(f32)
-        gains[n] = column[n * half:(n + 1) * half, :]
-    lane = lax.broadcasted_iota(i32, (half, 128), 1)
+def merge_kernel(size, at_ref, keep_ref, got_ref, *outs):
+    me = at_ref[0]
     for k in range(size):
         to = (me + k) & (size - 1)
-        outs[k][:, 0:width] = (keep_ref[to].astype(f32) + got_ref[to].astype(f32)).astype(bf16)
-        own = jnp.broadcast_to(gains[2 * to + rep][:, 0:1], lane.shape)
-        other = jnp.broadcast_to(gains[2 * to + 1 - rep][:, 0:1], lane.shape)
-        tail = jnp.where(lane < TABLE - 1, few[2 * to + rep], jnp.where(lane == TABLE - 1, own, jnp.where(lane == TABLE, other, 0.0)))
-        outs[k][:, width:] = tail.astype(bf16)
-        outs[k][0:rows, width:] = (tail[0:rows] + gtab_ref[to]).astype(bf16)
-
-
-def finish_kernel(at_ref, mine_ref, other_ref, gain_ref, q_ref, k_ref, v_ref, o_ref, router_ref, table_ref, ga_ref, gm_ref, few):
+        outs[k][...] = (keep_ref[to].astype(f32) + got_ref[to].astype(f32)).astype(bf16)
+
+
+def total_kernel(size, at_ref, q_ref, k_ref, v_ref, *refs):
+    blocks, out_ref, few_ref = refs[:size], refs[size], refs[size + 1]
+    total = sum(b[...].astype(f32) for b in blocks)
+    out_ref[...] = total
+    half = total.shape[0]
+    width = q_ref.shape[1]
+    few = total[:, 4 * width:]
+    lane = lax.broadcasted_iota(i32, few.shape, 1)
+    for r in (0, 1):
+        @pl.when(at_ref[1] == r)
+        def _():
+            product = sum(total[:, n * width:(n + 1) * width] * ref[r * half:(r + 1) * half, :].astype(f32) for n, ref in enumerate((q_ref, k_ref, v_ref)))
+            few_ref[...] = jnp.where(lane == TABLE - 1, jnp.sum(product, axis=1, keepdims=True), few)
+
+
+def finish_kernel(at_ref, mine_ref, other_ref, few_mine, few_other, gain_ref, q_ref, k_ref, v_ref, o_ref, router_ref, table_ref, ga_ref, gm_ref, few):
     half = mine_ref.shape[0]
     width = q_ref.shape[1]
     experts = router_ref.shape[0]
-
-    def put(first, second):
+    rows = table_ref.shape[1]
+
+    def put(first, second, few_first, few_second):
         for n, ref in enumerate((q_ref, k_ref, v_ref, o_ref)):
             ref[0:half, :] = first[:, n * width:(n + 1) * width]
             ref[half:, :] = second[:, n * width:(n + 1) * width]
-        a, b = first[:, 4 * width:], second[:, 4 * width:]
-        lane = lax.broadcasted_iota(i32, a.shape, 1)
-        few[0:half, :] = jnp.where(lane == TABLE - 1, a + jnp.broadcast_to(b[:, TABLE:TABLE + 1], a.shape), jnp.where(lane > TABLE, a + b, a))
-        few[half:, :] = jnp.where(lane == TABLE - 1, b + jnp.broadcast_to(a[:, TABLE:TABLE + 1], b.shape), b)
-
-    pl.when(at_ref[1] == 0)(lambda: put(mine_ref, other_ref))
-    pl.when(at_ref[1] == 1)(lambda: put(other_ref, mine_ref))
+        few[0:half, :] = few_first[...]
+        few[half:, :] = few_second[...]
+        table_ref[...] = first[:, 4 * width:].T[TABLE + 1:TABLE + 1 + table_ref.shape[0], 0:rows]
+
+    pl.when(at_ref[1] == 0)(lambda: put(mine_ref, other_ref, few_mine, few_other))
+    pl.when(at_ref[1] == 1)(lambda: put(other_ref, mine_ref, few_other, few_mine))
     turned = few[...].T
     router_ref[...] = turned[0:experts, :]
-    table_ref[...] = turned[TABLE + 1:TABLE + 1 + table_ref.shape[0], 0:table_ref.shape[1]]
     ga_ref[...] = turned[TABLE - 1:TABLE, :] / gain_ref[...].astype(f32)
     gm_ref[...] = turned[TABLE - 2:TABLE - 1, :]
 
@@ -836,41 +843,34 @@
     half_rows = part_rows * size // 2
     matrix = order_matrix(size, part, part_rows, 0, 0)
 
-    packed = call(pack_kernel, "pack", [sd((half, 896), bf16)],
-                  (at, w_query, w_key, w_value, w_router.T, w_attn_out, gain_attn, gain_moe, rel_table.T),
-                  scratch=[pltpu.VMEM((rows_dev, 896), f32)], smem=1)[0]
-    mine = [packed] + [to_expert(packed, k, size) for k in range(1, size)]
+    packed, rest = call(pack_kernel, "pack", [sd((half, 896), bf16)] * 2,
+                        (at, w_query, w_key, w_value, w_router.T, w_attn_out, gain_attn, gain_moe, rel_table.T),
+                        scratch=[pltpu.VMEM((rows_dev, 896), f32)], smem=1)
+    mine = [to_expert(packed, k, size) for k in range(1, size)]
+    other = [to_core(m) for m in mine]
+    pieces = gather_pieces(tok, count // 2)
     idx = call(functools.partial(prepare_kernel, size, chunks), "prepare", [sd((count, 8), i32)], (z[None], routes[0].T, capacity[None]),
                smem=1, deps=(packed,))[0]
-    pieces = gather_pieces(tok, count // 2)
-    joined = call(join_kernel, "join", [sd((size * half, packed.shape[1]), bf16)], tuple(mine), deps=(*pieces[1:3], idx))[0]
-    qkv_w, wo, router, gains, table = unpack(at, mine, to_core(joined), buckets)
-
-    g_blocks = spread(idx, cot, 0, chunks * size, part_rows, (joined,), "spread_g")
-    g_arrived = shifted(g_blocks[:size])
-
-    xn, qkv = project(at, pieces, qkv_w, gains)
-    g_ordered = [reorder(matrix, g_arrived, "order_g", (qkv,))]
-    g_pieces = [gather_pieces(g_ordered[0], half_rows)]
-    ready, window = (g_ordered[0],), g_pieces[0][1:3]
+
+    g_blocks = spread(idx, cot, 0, size, local * CAP, (*mine, *pieces[1:3]), "spread_g", chunks)
+    g_arrived = shifted(g_blocks)
+    qkv_w, wo, router, gains, table = unpack(at, [packed, *mine], [rest, *other], buckets, (idx,))
+
+    xn, qkv = project(at, pieces, qkv_w, gains, (g_blocks[0],))
+    o, lse, *parts = attn_fwd(at, table, qkv, segments, wo, ())
+    g_ordered = call(functools.partial(reorder_all_kernel, size), "order_g", [sd((local * CAP * size, width), bf16)], (matrix, *g_arrived), deps=(o,))[0]
+    terms = scatter_direct(parts[0], after(parts[1], g_ordered), *parts[2:])
+    h, xn2, probs, gate, *blocks = route(idx, tok, terms, router, gains, size, chunks, ())
+    g_pieces = gather_pieces(after(g_ordered, xn2), half_rows * chunks)
+
+    arrived = shifted(blocks)
+    ordered = [reorder(order_matrix(size, part, part_rows + 16, 16, 16), arrived, "order")]
+    got = [gather_pieces(ordered[0], half_rows)]
     if chunks == 2:
-        g_late = shifted([after(b, g_ordered[0]) for b in g_blocks[size:]])
-        window = (*window, *g_late[1:])
-    o, lse, own, *parts = attn_fwd(at, table, qkv, segments, wo, ready)
-    terms = scatter_direct(own, after(parts[0], *window), *parts[1:])
-    h, xn2, probs, gate, *blocks = route(idx, tok, terms, router, gains, size, chunks, ())
-
-    arrived = shifted(blocks)
-    if chunks == 2:
-        g_ordered.append(reorder(matrix, [after(g_late[0], xn2)] + g_late[1:], "order_g", (*blocks[1:], *g_pieces[0][3:])))
-        g_pieces.append(gather_pieces(g_ordered[1], half_rows))
-    ordered = [reorder(order_matrix(size, part, part_rows + 16, 16, 16), arrived, "order", g_ordered[1:])]
-    got = [gather_direct(ordered[0])]
-    if chunks == 2:
-        blocks = spread(idx, xn2, 1, size, part_rows, (ordered[0], *g_pieces[1][1:]), "spread")
+        blocks = spread(idx, xn2, 1, size, part_rows, (ordered[0], *g_pieces[1:3]), "spread", 1)
         ordered.append(reorder(matrix, shifted(blocks), "order"))
         got.append(gather_direct(ordered[1]))
-    extras = got[0]
+    extras = (*got[0][:3], got[0][4])
     ready = ordered[1:]
 
     step = max(part // 4, 1)
@@ -888,7 +888,7 @@
     acts, sums, ys = [], [], []
     dg_full = jnp.zeros((4, lanes_of(size) // 128, 16, 128), f32)
     for c in range(chunks):
-        *outs, dg_full, act = moe(at, size, chunks, c, got[c], extras, g_pieces[c], w_in, w_out, dg_full, () if c else ready)
+        *outs, dg_full, act = moe(at, size, chunks, c, got[c], extras, g_pieces, w_in, w_out, dg_full, () if c else ready)
         sums.append(scatter_direct(*outs[:4]) if c < chunks - 1 else outs[:4])
         ys.append(outs[4:])
         acts.append(act)
@@ -908,54 +908,53 @@
     mark = outs[0]
     if chunks == 2:
         mark, back_blocks = give(0, False, (mark,))
-    mark = expert_grads(2, mark)
+    mark = expert_grads(1, mark)
     mark = expert_grads(1, mark, *back_blocks[1:])
-    if chunks == 2:
-        acts[1] = after(acts[1], mark, *sums[-1][1:])
-        other_acts.append(to_core(acts[1]))
+    mark = expert_grads(1, mark)
     ready, blocks = give(chunks - 1, True, (mark,))
     if chunks == 2:
-        y_packs = [after(ys[c][1], *sums[-1][1:]) for c in (0, 1)]
+        y_packs = [after(ys[c][1], mark, *sums[-1][1:]) for c in (0, 1)]
         y_got = [to_tensor(pack, flip) for flip, pack in zip((1, 2), y_packs)]
     else:
         y_terms = scatter_direct(*ys[0])
-    mark = expert_grads(1, ready)
-    ready = (mark, *y_packs) if chunks == 2 else (mark,)
+    ready = (ready, *y_packs) if chunks == 2 else (ready,)
     dh, dhb, small = back(idx, cot, h, xn2, probs, gate, router, gains, back_blocks + blocks, size, chunks, ready)
     dh_pieces = gather_direct(dhb)
-    mark = expert_grads(2, dhb)
-    small = after(small, mark)
-    small = small + to_tensor(small, 1)
+    mark = expert_grads(1, dhb)
+    if chunks == 2:
+        acts[1] = after(acts[1], mark)
+        other_acts.append(to_core(acts[1]))
     if chunks == 2:
         y_parts, sent = scatter_end(*y_got, ys[1][2], ys[0][2], (mark,))
         mark = sent[0]
 
-    gtab, dqkv = attn_bwd(at, size, table, dh_pieces, segments, wo, qkv, lse, (mark, small))
-    small = small + to_tensor(small, 2)
+    y_late = (y_parts[1], y_parts[3]) if chunks == 2 else ()
+    gtab, dqkv = attn_bwd(at, size, table, dh_pieces, segments, wo, qkv, lse, (mark,))
+    keep, send, own, *parts = attn_grad(at, size, dqkv, qkv_w, xn, dh_pieces, o, small, gtab, y_late)
+    terms = scatter_direct(own, *parts)
+    got = to_core(send)
+    out_blocks = call(functools.partial(merge_kernel, size), "merge", [sd((half, packed.shape[1]), bf16)] * size,
+                      (at, keep, got), smem=1)
     outs = [sd((local * CAP, width), bf16)] * size
     if chunks == 2:
-        given = call(functools.partial(give_back_halves_kernel, size), "give_back_y", outs, (matrix, ys[0][0], ys[1][0], *y_parts), deps=(dqkv, small))
+        given = call(functools.partial(give_back_halves_kernel, size), "give_back_y", outs, (matrix, ys[0][0], ys[1][0], *y_parts), deps=(out_blocks[0],))
     else:
-        given = call(functools.partial(give_back_kernel, size, False), "give_back_y", outs, (matrix, *y_terms), deps=(dqkv,))
+        given = call(functools.partial(give_back_kernel, size, False), "give_back_y", outs, (matrix, *y_terms), deps=(out_blocks[0],))
     y_blocks = [given[0]] + [to_expert(given[k], size - k, size) for k in range(1, size)]
-    keep, send, gain_row, own, *parts = attn_grad(at, size, dqkv, qkv_w, xn, dh_pieces, o, (given[0], small))
-    small = small + to_core(small)
-    terms = scatter_direct(own, *[after(p, *y_blocks[1:]) for p in parts])
-    got = to_core(send)
     grad_tokens = call(last_kernel, "last", [sd((count, width), f32)], (tok, dh, *terms, gains))[0]
-    output = mix(idx, h, gate, y_blocks, size, chunks)
-
-    gain_row = gain_row + to_tensor(gain_row, 1)
-    gain_row = gain_row + to_tensor(gain_row, 2)
-    out_blocks = call(functools.partial(merge_kernel, size), "merge", [sd((half, packed.shape[1]), bf16)] * size,
-                      (at, keep, got, small, gain_row, gtab), smem=1,
-                      scratch=[pltpu.VMEM((2 * size, half, 128), f32), pltpu.VMEM((2 * size, half, 8), f32)])
-    expert_grads(len(pending), out_blocks[0])
-    total = call(total_kernel, "total", [sd(out_blocks[0].shape, f32)], tuple(shifted(out_blocks)), deps=(grads[0], *terms[1:]))[0]
+    mark = expert_grads(1, out_blocks[0], given[0])
+    mark = expert_grads(max(len(pending) - 2, 0), mark, *terms[1:])
+    total, gain = call(functools.partial(total_kernel, size), "total", [sd(out_blocks[0].shape, f32), sd((half, 128), f32)],
+                       (at, w_query, w_key, w_value, *shifted(out_blocks)), smem=1, deps=(mark, *terms[1:]))
+    mark = expert_grads(1, total)
+    gain = gain + to_tensor(gain, 1)
+    mark = expert_grads(1, mark, gain)
+    gain = gain + to_tensor(gain, 2)
+    output = mix(idx, h, gate, y_blocks, size, chunks, (total,))
     lw = w_query.shape[1]
     outs = [sd((rows_dev, lw), f32)] * 4 + [sd((experts, rows_dev), f32), sd(rel_table.T.shape, f32)] + [sd((1, rows_dev), f32)] * 2
     grad_q, grad_k, grad_v, grad_o, grad_router, grad_table, grad_ga, grad_gm = call(
-        finish_kernel, "finish", outs, (at, total, to_core(total), gain_attn[None]), smem=1, scratch=[pltpu.VMEM((rows_dev, 128), f32)])
+        finish_kernel, "finish", outs, (at, total, to_core(total), gain, to_core(gain), gain_attn[None]), smem=1, scratch=[pltpu.VMEM((rows_dev, 128), f32)], deps=(output, mark))
     return (output[None], grad_tokens[None], grad_table.T, grad_q, grad_k, grad_v, grad_o, grad_ga[0], grad_gm[0], grad_router.T, *grads)
 
 

time: 419 us -> 379 us (0.905)
  waiting for transfers between devices: 97.7 us -> 65.5 us
  starting transfers between devices: 88.8 us -> 97.2 us
  local copies, waits for them, and re-layouts: 22.6 us -> 17.3 us
  Pallas kernels: 197 us -> 192 us
  other arithmetic: 5.38 us -> 0.69 us
    ppermute x41 -> x36, waiting for transfers between devices: 52.2 us -> 28.3 us  [to_tensor(): return lax.ppermute(a, 'tensor', [(i, i ^ flip) for i in range(4)])]
    ppermute x6 -> x8, starting transfers between devices: 20.6 us -> 35.2 us  [to_core(): return lax.ppermute(a, 'rep', [(0, 1), (1, 0)])]
    ppermute x27 -> x24, waiting for transfers between devices: 45.2 us -> 37.2 us  [to_expert(): lax.ppermute(a, 'expert', [(i, (i + shift) % size) for i in range(size)])]
    add x5 -> x2, other arithmetic: 4.73 us -> 0.02 us  [the longest x1 0.01 us: on_device(): gain = gain + to_tensor(gain, 1)]
    pallas_call x25 -> x23, Pallas kernels: 103 us -> 98.1 us  [call(): pl.pallas_call(body, out_shape=tuple(outs), in_specs=[SM] * smem + [VM] *...]
    unnamed x134 -> x124, local copies, waits for them, and re-layouts: 17.5 us -> 14 us
    ppermute x27 -> x24, starting transfers between devices: 35.7 us -> 32.6 us  [to_expert(): lax.ppermute(a, 'expert', [(i, (i + shift) % size) for i in range(size)])]
    ppermute x41 -> x36, starting transfers between devices: 32.5 us -> 29.4 us  [to_tensor(): return lax.ppermute(a, 'tensor', [(i, i ^ flip) for i in range(4)])]
  transfers between devices with their start and end apart: 74 -> 68, of which waited for: 17 -> 15; matrix products, arithmetic and copies ran while one was open for 3% -> 1% of each run, Pallas kernels for 41% -> 50%
where the time goes in v2:
time: 379 us; the launch traced here: 374 us
  Pallas kernels  192 us (51%)
  starting transfers between devices  97.2 us (26%)
  waiting for transfers between devices  65.5 us (17%)
  local copies, waits for them, and re-layouts  17.3 us (5%)
    pallas_call x23, Pallas kernels, call(): pl.pallas_call(body, out_shape=tuple(outs), in_specs=[SM] * smem + [VM] *...  98.1 us
    pallas_call x8, Pallas kernels, expert_grad(): pl.pallas_call(functools.partial(expert_grad_kernel, steps), grid=(part,...  54.4 us
    pallas_call x2, Pallas kernels, moe(): pl.pallas_call(functools.partial(moe_kernel, rows, part, first, last, len...  39.4 us
    ppermute x24, waiting for transfers between devices, to_expert(): lax.ppermute(a, 'expert', [(i, (i + shift) % size) for i in range(size)])  37.2 us
    ppermute x8, starting transfers between devices, to_core(): return lax.ppermute(a, 'rep', [(0, 1), (1, 0)])  35.2 us
    ppermute x24, starting transfers between devices, to_expert(): lax.ppermute(a, 'expert', [(i, (i + shift) % size) for i in range(size)])  32.6 us
    ppermute x36, starting transfers between devices, to_tensor(): return lax.ppermute(a, 'tensor', [(i, i ^ flip) for i in range(4)])  29.4 us
    ppermute x36, waiting for transfers between devices, to_tensor(): return lax.ppermute(a, 'tensor', [(i, i ^ flip) for i in range(4)])  28.3 us
  transfers between devices with their start and end apart: 68, of which 15 were waited for; matrix products, arithmetic and copies ran while one was open for 1% of the time, Pallas kernels for 50%

profile of v2, /device:TPU:1, one launch (start us, length us, event | category | flops | bytes accessed | tf_op | source)
XLA Modules:
  0.0 374.0 jit_solution(15450582693354352714)
XLA Ops:
  16.8 8.1 %collective-permute-done.1.refs_3_ = bf16[96,896]{1,0:T(8,128)(2,1)S(1)} collective-permute-done((bf16[96,896]{1,0:T(8,128)(2,1)}, bf16[96,896]{1,0:T(8,128)(2,1)S(1)}, u32[]{:S(2)}, u32[]{:S(2)}) %collective-permute-start.1) | collective-permute-done | bytes 172064 | tf_op jit(solution)/shard_map/ppermute | solution.py:76
  40.9 4.5 %project.1 = (bf16[1024,768]{1,0:T(8,128)(2,1)}, bf16[1024,576]{1,0:T(8,128)(2,1)}) custom-call(s32[3]{0:T(128)} %pad_add_fusion.refs_0_.at_ref, bf16[256,768]{1,0:T(8,128)(2,1)} %bitcast.20, bf16[256,768]{1,0:T(8,128)(2,1)} %copy-done.26, bf16[256,768]{1,0:T(8,128)(2,1)} %copy-done.25, bf16[128,768]{1,0:T(8,128)(2,1)} %copy-done.44, ...), custom_call_target="tpu_custom_call" | custom-call | flops 5750000128 | bytes 1000 | tf_op jit(solution)/shard_map/project/pallas_call | solution.py:48
  45.3 12.3 %attn_fwd.1 = (bf16[1024,192]{1,0:T(8,128)(2,1)}, f32[1024,3]{1,0:T(8,128)}, bf16[256,768]{1,0:T(8,128)(2,1)}, bf16[256,768]{1,0:T(8,128)(2,1)}, bf16[256,768]{1,0:T(8,128)(2,1)}, /*index=5*/bf16[256,768]{1,0:T(8,128)(2,1)}) custom-call(s32[3]{0:T(128)} %pad_add_fusion.refs_0_.at_ref, f32[32,128]{1,0:T(8,128)} %get-tuple-element.125.refs_1_, ...), custom_call_target="tpu_custom_call" | custom-call | flops 14949999616 | bytes 1000 | tf_op jit(solution)/shard_map/attn_fwd/pallas_call | solution.py:48
  64.4 11.1 %collective-permute-done.14.refs_4_ = bf16[256,768]{1,0:T(8,128)(2,1)S(1)} collective-permute-done((bf16[256,768]{1,0:T(8,128)(2,1)}, bf16[256,768]{1,0:T(8,128)(2,1)S(1)}, u32[]{:S(2)}, u32[]{:S(2)}) %collective-permute-start.14) | collective-permute-done | bytes 393248 | tf_op jit(solution)/shard_map/ppermute | solution.py:72
  90.2 9.1 %collective-permute-done.17.refs_3_ = bf16[112,768]{1,0:T(8,128)(2,1)S(1)} collective-permute-done((bf16[112,768]{1,0:T(8,128)(2,1)}, bf16[112,768]{1,0:T(8,128)(2,1)S(1)}, u32[]{:S(2)}, u32[]{:S(2)}) %collective-permute-start.17) | collective-permute-done | bytes 172064 | tf_op jit(solution)/shard_map/ppermute | solution.py:76
  114.2 6.4 %collective-permute-done.20.py.e_py = bf16[400,768]{1,0:T(8,128)(2,1)S(1)} collective-permute-done((bf16[400,768]{1,0:T(8,128)(2,1)}, bf16[400,768]{1,0:T(8,128)(2,1)S(1)}, u32[]{:S(2)}, u32[]{:S(2)}) %collective-permute-start.20) | collective-permute-done | bytes 614432 | tf_op jit(solution)/shard_map/ppermute | solution.py:72
  134.1 5.5 %collective-permute-done.21.d0 = bf16[192,768]{1,0:T(8,128)(2,1)S(1)} collective-permute-done((bf16[192,768]{1,0:T(8,128)(2,1)S(1)}, bf16[192,768]{1,0:T(8,128)(2,1)S(1)}, u32[]{:S(2)}, u32[]{:S(2)}) %collective-permute-start.21) | collective-permute-done | bytes 294944 | tf_op jit(solution)/shard_map/ppermute | solution.py:72
  141.8 19.4 %moe.2 = (bf16[384,768]{1,0:T(8,128)(2,1)}, bf16[384,768]{1,0:T(8,128)(2,1)}, bf16[384,768]{1,0:T(8,128)(2,1)}, bf16[384,768]{1,0:T(8,128)(2,1)}, bf16[384,768]{...) custom-call(s32[3]{0:T(128)} %pad_add_fusion.refs_0_.at_ref, ...), custom_call_target="tpu_custom_call" | custom-call | flops 344999985152 | bytes 1000 | tf_op jit(solution)/shard_map/moe/pallas_call | solution.py:658
  164.0 12.8 %collective-permute-start.33 = (bf16[4,8,4,48,768]{4,3,2,1,0:T(8,128)(2,1)}, bf16[4,8,4,48,768]{4,3,2,1,0:T(8,128)(2,1)}, u32[]{:S(2)}, u32[]{:S(2)}) collective-permute-start(bf16[4,8,4,48,768]{4,3,2,1,0:T(8,128)(2,1)} %get-tuple-element.155.mine), channel_id=1, source_target_pairs={{0,1},{1,0},{2,3},{3,2},{4,5},{5,4},{6,7},{7,6},{8,9},{9,8},{10,11... | collective-permute-start | bytes 28311560 | tf_op jit(solution)/shard_map/ppermute | solution.py:80
  176.7 20.0 %moe.3 = (bf16[400,768]{1,0:T(8,128)(2,1)}, bf16[400,768]{1,0:T(8,128)(2,1)}, bf16[400,768]{1,0:T(8,128)(2,1)}, bf16[400,768]{1,0:T(8,128)(2,1)}, bf16[384,768]{...) custom-call(s32[3]{0:T(128)} %pad_add_fusion.refs_0_.at_ref, ...), custom_call_target="tpu_custom_call" | custom-call | flops 344999985152 | bytes 1000 | tf_op jit(solution)/shard_map/moe/pallas_call | solution.py:658
  210.1 6.7 %expert_grad.8 = (f32[16,768,768]{2,1,0:T(8,128)}, f32[16,768,768]{2,1,0:T(8,128)}, f32[8,128]{1,0:T(8,128)}) custom-call(s32[3]{0:T(128)} %pad_add_fusion.refs_0_.at_ref, bf16[4,8,4,48,768]{4,3,2,1,0:T(8,128)(2,1)} %get-tuple-element.155.mine, bf16[4,8,4,48,768]{4,3,2,1,0:T(8,128)(2,1)} %collective-permute-done.33.other, ...), custom_call_target="tpu_custom_call" | custom-call | flops 1150000000 | bytes 1000 | tf_op jit(solution)/shard_map/expert_grad/pallas_call | solution.py:700
  217.8 6.7 %expert_grad.9 = (f32[16,768,768]{2,1,0:T(8,128)}, f32[16,768,768]{2,1,0:T(8,128)}, f32[8,128]{1,0:T(8,128)}) custom-call(s32[3]{0:T(128)} %pad_add_fusion.refs_0_.at_ref, bf16[4,8,4,48,768]{4,3,2,1,0:T(8,128)(2,1)} %get-tuple-element.155.mine, ...), custom_call_target="tpu_custom_call", output_to_operand_aliasing={{0}: (3, {}), {1}: (4, {})} | custom-call | flops 1150000000 | bytes 1000 | tf_op jit(solution)/shard_map/expert_grad/pallas_call | solution.py:700
  224.5 6.8 %expert_grad.10 = (f32[16,768,768]{2,1,0:T(8,128)}, f32[16,768,768]{2,1,0:T(8,128)}, f32[8,128]{1,0:T(8,128)}) custom-call(s32[3]{0:T(128)} %pad_add_fusion.refs_0_.at_ref, bf16[4,8,4,48,768]{4,3,2,1,0:T(8,128)(2,1)} %get-tuple-element.155.mine, ...), custom_call_target="tpu_custom_call", output_to_operand_aliasing={{0}: (3, {}), {1}: (4, {})} | custom-call | flops 1150000000 | bytes 1000 | tf_op jit(solution)/shard_map/expert_grad/pallas_call | solution.py:700
  240.8 4.7 %collective-permute-done.46.refs_14_ = bf16[112,768]{1,0:T(8,128)(2,1)S(1)} collective-permute-done((bf16[112,768]{1,0:T(8,128)(2,1)}, bf16[112,768]{1,0:T(8,128)(2,1)S(1)}, u32[]{:S(2)}, u32[]{:S(2)}) %collective-permute-start.46) | collective-permute-done | bytes 172064 | tf_op jit(solution)/shard_map/ppermute | solution.py:76
  246.2 4.9 %back.1 = (f32[256,768]{1,0:T(8,128)}, bf16[256,768]{1,0:T(8,128)(2,1)}, bf16[768,128]{1,0:T(8,128)(2,1)}) custom-call(s32[256,8]{1,0:T(8,128)} %prepare.1.refs_9_.refs_0_, bf16[256,768]{1,0:T(8,128)(2,1)} %bitcast.25, f32[256,768]{1,0:T(8,128)} %get-tuple-element.140.refs_2_.refs_1_, bf16[256,768]{1,0:T(8,128)(2,1)} %get-tuple-element.146.refs_1_.refs_3_, ...), custom_call_target="tpu_custom_call" | custom-call | flops 5750000128 | bytes 1000 | tf_op jit(solution)/shard_map/back/pallas_call | solution.py:48
  253.8 6.9 %expert_grad.11 = (f32[16,768,768]{2,1,0:T(8,128)}, f32[16,768,768]{2,1,0:T(8,128)}, f32[8,128]{1,0:T(8,128)}) custom-call(s32[3]{0:T(128)} %pad_add_fusion.refs_0_.at_ref, bf16[4,8,4,48,768]{4,3,2,1,0:T(8,128)(2,1)} %get-tuple-element.155.mine, ...), custom_call_target="tpu_custom_call", output_to_operand_aliasing={{0}: (3, {}), {1}: (4, {})} | custom-call | flops 1150000000 | bytes 1000 | tf_op jit(solution)/shard_map/expert_grad/pallas_call | solution.py:700
  260.7 12.9 %collective-permute-start.60 = (bf16[4,8,4,48,768]{4,3,2,1,0:T(8,128)(2,1)}, bf16[4,8,4,48,768]{4,3,2,1,0:T(8,128)(2,1)}, u32[]{:S(2)}, u32[]{:S(2)}) collective-permute-start(bf16[4,8,4,48,768]{4,3,2,1,0:T(8,128)(2,1)} %after.15.mine), channel_id=1, source_target_pairs={{0,1},{1,0},{2,3},{3,2},{4,5},{5,4},{6,7},{7,6},{8,9},{9,8},{10,11... | collective-permute-start | bytes 28311560 | tf_op jit(solution)/shard_map/ppermute | solution.py:80
  281.5 18.0 %attn_bwd.1 = (f32[4,8,128]{2,1,0:T(8,128)}, bf16[1024,576]{1,0:T(8,128)(2,1)}) custom-call(s32[3]{0:T(128)} %pad_add_fusion.refs_0_.at_ref, f32[32,128]{1,0:T(8,128)} %get-tuple-element.125.refs_1_, bf16[256,768]{1,0:T(8,128)(2,1)} %get-tuple-element.185.refs_2_.refs_4_, bf16[256,768]{1,0:T(8,128)(2,1)} %copy-done.33, bf16[256,768]{1,0:T(8,128)(2,1)} %copy-done.32, ...), custom_call_target="tpu_custom_call" | custom-call | flops 460000002048 | bytes 1000 | tf_op jit(solution)/shard_map/attn_bwd/pallas_call | solution.py:48
  299.6 7.4 %attn_grad.1 = (bf16[4,96,896]{2,1,0:T(8,128)(2,1)}, bf16[4,96,896]{2,1,0:T(8,128)(2,1)}, bf16[256,768]{1,0:T(8,128)(2,1)}, bf16[256,768]{1,0:T(8,128)(2,1)}, bf...) custom-call(s32[3]{0:T(128)} %pad_add_fusion.refs_0_.at_ref, bf16[1024,576]{1,0:T(8,128)(2,1)} %get-tuple-element.190.refs_1_, ...), custom_call_target="tpu_custom_call" | custom-call | flops 10350000128 | bytes 1000 | tf_op jit(solution)/shard_map/attn_grad/pallas_call | solution.py:48
  313.7 4.2 %give_back_y.1 = (bf16[192,768]{1,0:T(8,128)(2,1)}, bf16[192,768]{1,0:T(8,128)(2,1)}, bf16[192,768]{1,0:T(8,128)(2,1)}, bf16[192,768]{1,0:T(8,128)(2,1)}) custom-call(bf16[384,384]{1,0:T(8,128)(2,1)} %constant.17.clone.refs_0_, bf16[384,768]{1,0:T(8,128)(2,1)} %get-tuple-element.151.refs_1_, bf16[384,768]{1,0:T(8,128)(2,1)} %get-tuple-element.153.refs_2_, ...), custom_call_target="tpu_custom_call" | custom-call | flops 575000000 | bytes 1000 | tf_op jit(solution)/shard_map/give_back_y/pallas_call | solution.py:48
  321.8 6.8 %expert_grad.12 = (f32[16,768,768]{2,1,0:T(8,128)}, f32[16,768,768]{2,1,0:T(8,128)}, f32[8,128]{1,0:T(8,128)}) custom-call(s32[3]{0:T(128)} %pad_add_fusion.refs_0_.at_ref, bf16[4,8,4,48,768]{4,3,2,1,0:T(8,128)(2,1)} %after.15.mine, bf16[4,8,4,48,768]{4,3,2,1,0:T(8,128)(2,1)} %collective-permute-done.60.other, ...), custom_call_target="tpu_custom_call", output_to_operand_aliasing={{0}: (3, {}), {1}: (4, {})} | custom-call | flops 1150000000 | bytes 1000 | tf_op jit(solution)/shard_map/expert_grad/pallas_call | solution.py:700
  331.2 6.8 %expert_grad.13 = (f32[16,768,768]{2,1,0:T(8,128)}, f32[16,768,768]{2,1,0:T(8,128)}, f32[8,128]{1,0:T(8,128)}) custom-call(s32[3]{0:T(128)} %pad_add_fusion.refs_0_.at_ref, bf16[4,8,4,48,768]{4,3,2,1,0:T(8,128)(2,1)} %after.15.mine, bf16[4,8,4,48,768]{4,3,2,1,0:T(8,128)(2,1)} %collective-permute-done.60.other, ...), custom_call_target="tpu_custom_call", output_to_operand_aliasing={{0}: (3, {}), {1}: (4, {})} | custom-call | flops 1150000000 | bytes 1000 | tf_op jit(solution)/shard_map/expert_grad/pallas_call | solution.py:700
  347.3 7.0 %expert_grad.14 = (f32[16,768,768]{2,1,0:T(8,128)}, f32[16,768,768]{2,1,0:T(8,128)}, f32[8,128]{1,0:T(8,128)}) custom-call(s32[3]{0:T(128)} %pad_add_fusion.refs_0_.at_ref, bf16[4,8,4,48,768]{4,3,2,1,0:T(8,128)(2,1)} %after.15.mine, bf16[4,8,4,48,768]{4,3,2,1,0:T(8,128)(2,1)} %collective-permute-done.60.other, ...), custom_call_target="tpu_custom_call", output_to_operand_aliasing={{0}: (3, {}), {1}: (4, {})} | custom-call | flops 1150000000 | bytes 1000 | tf_op jit(solution)/shard_map/expert_grad/pallas_call | solution.py:700
  364.0 6.8 %expert_grad.15 = (f32[16,768,768]{2,1,0:T(8,128)}, f32[16,768,768]{2,1,0:T(8,128)}, f32[8,128]{1,0:T(8,128)}) custom-call(s32[3]{0:T(128)} %pad_add_fusion.refs_0_.at_ref, bf16[4,8,4,48,768]{4,3,2,1,0:T(8,128)(2,1)} %after.15.mine, bf16[4,8,4,48,768]{4,3,2,1,0:T(8,128)(2,1)} %collective-permute-done.60.other, ...), custom_call_target="tpu_custom_call", output_to_operand_aliasing={{0}: (3, {}), {1}: (4, {})} | custom-call | flops 1150000000 | bytes 1000 | tf_op jit(solution)/shard_map/expert_grad/pallas_call | solution.py:700
  (288 shorter events, 156.8 us)
Async XLA Ops:
  0.6 25.3 %collective-permute-start.7 = (bf16[256,768]{1,0:T(8,128)(2,1)}, bf16[256,768]{1,0:T(8,128)(2,1)S(1)}, u32[]{:S(2)}, u32[]{:S(2)}) collective-permute-start(bf16[256,768]{1,0:T(8,128)(2,1)} %bitcast.18), channel_id=1, source_target_pairs={{0,4},{2,6},{4,0},{6,2},{1,5},{3,7},{5,1},{7,3},{8,12},{10,14},{12... | collective-permute-start | bytes 1179656 | tf_op jit(solution)/shard_map/ppermute | solution.py:72
  81.4 25.1 %collective-permute-start.23 = (bf16[768,768]{1,0:T(8,128)(2,1)}, bf16[768,768]{1,0:T(8,128)(2,1)S(1)}, u32[]{:S(2)}, u32[]{:S(2)}) collective-permute-start(bf16[768,768]{1,0:T(8,128)(2,1)} %after.9.g_own), channel_id=1, source_target_pairs={{0,2},{2,0},{4,6},{6,4},{1,3},{3,1},{5,7},{7,5},{8,10},{10,8},{12,... | collective-permute-start | bytes 3538952 | tf_op jit(solution)/shard_map/ppermute | solution.py:72
  82.6 25.2 %collective-permute-start.24 = (bf16[768,768]{1,0:T(8,128)(2,1)}, bf16[768,768]{1,0:T(8,128)(2,1)S(1)}, u32[]{:S(2)}, u32[]{:S(2)}) collective-permute-start(bf16[768,768]{1,0:T(8,128)(2,1)} %after.9.g_own), channel_id=1, source_target_pairs={{0,4},{2,6},{4,0},{6,2},{1,5},{3,7},{5,1},{7,3},{8,12},{10,14},{12... | collective-permute-start | bytes 3538952 | tf_op jit(solution)/shard_map/ppermute | solution.py:72
  106.5 34.5 %collective-permute-start.25 = (bf16[384,768]{1,0:T(8,128)(2,1)S(1)}, bf16[384,768]{1,0:T(8,128)(2,1)S(1)}, u32[]{:S(2)}, u32[]{:S(2)}) collective-permute-start(bf16[384,768]{1,0:T(8,128)(2,1)S(1)} %slice.28), channel_id=1, source_target_pairs={{0,4},{2,6},{4,0},{6,2},{1,5},{3,7},{5,1},{7,3},{8,12},{10,14},{12... | collective-permute-start | bytes 1769480 | tf_op jit(solution)/shard_map/ppermute | solution.py:72
  129.3 33.3 %collective-permute-start.32 = (bf16[384,768]{1,0:T(8,128)(2,1)}, bf16[384,768]{1,0:T(8,128)(2,1)}, u32[]{:S(2)}, u32[]{:S(2)}) collective-permute-start(bf16[384,768]{1,0:T(8,128)(2,1)} %slice.29), channel_id=1, source_target_pairs={{0,2},{2,0},{4,6},{6,4},{1,3},{3,1},{5,7},{7,5},{8,10},{10,8},{12,... | collective-permute-start | bytes 1769480 | tf_op jit(solution)/shard_map/ppermute | solution.py:72
  133.6 29.1 %collective-permute-start.31 = (bf16[384,768]{1,0:T(8,128)(2,1)}, bf16[384,768]{1,0:T(8,128)(2,1)}, u32[]{:S(2)}, u32[]{:S(2)}) collective-permute-start(bf16[384,768]{1,0:T(8,128)(2,1)} %order.3.refs_0_.own), channel_id=1, source_target_pairs={{0,6},{2,4},{4,2},{6,0},{1,7},{3,5},{5,3},{7,1},{8,14},{10,12},{12... | collective-permute-start | bytes 1769480 | tf_op jit(solution)/shard_map/ppermute | solution.py:72
  140.7 36.0 %collective-permute-start.29 = (bf16[384,768]{1,0:T(8,128)(2,1)}, bf16[384,768]{1,0:T(8,128)(2,1)}, u32[]{:S(2)}, u32[]{:S(2)}) collective-permute-start(bf16[384,768]{1,0:T(8,128)(2,1)} %order.3.refs_0_.own), channel_id=1, source_target_pairs={{0,2},{2,0},{4,6},{6,4},{1,3},{3,1},{5,7},{7,5},{8,10},{10,8},{12,... | collective-permute-start | bytes 1769480 | tf_op jit(solution)/shard_map/ppermute | solution.py:72
  161.2 35.5 %collective-permute-start.34 = (bf16[384,768]{1,0:T(8,128)(2,1)}, bf16[384,768]{1,0:T(8,128)(2,1)}, u32[]{:S(2)}, u32[]{:S(2)}) collective-permute-start(bf16[384,768]{1,0:T(8,128)(2,1)} %get-tuple-element.157), channel_id=1, source_target_pairs={{0,2},{2,0},{4,6},{6,4},{1,3},{3,1},{5,7},{7,5},{8,10},{10,8},{12,... | collective-permute-start | bytes 1769480 | tf_op jit(solution)/shard_map/ppermute | solution.py:72
  162.5 34.2 %collective-permute-start.35 = (bf16[384,768]{1,0:T(8,128)(2,1)}, bf16[384,768]{1,0:T(8,128)(2,1)}, u32[]{:S(2)}, u32[]{:S(2)}) collective-permute-start(bf16[384,768]{1,0:T(8,128)(2,1)} %get-tuple-element.158), channel_id=1, source_target_pairs={{0,4},{2,6},{4,0},{6,2},{1,5},{3,7},{5,1},{7,3},{8,12},{10,14},{12... | collective-permute-start | bytes 1769480 | tf_op jit(solution)/shard_map/ppermute | solution.py:72
  162.8 34.0 %collective-permute-start.36 = (bf16[384,768]{1,0:T(8,128)(2,1)}, bf16[384,768]{1,0:T(8,128)(2,1)}, u32[]{:S(2)}, u32[]{:S(2)}) collective-permute-start(bf16[384,768]{1,0:T(8,128)(2,1)} %get-tuple-element.159), channel_id=1, source_target_pairs={{0,6},{2,4},{4,2},{6,0},{1,7},{3,5},{5,3},{7,1},{8,14},{10,12},{12... | collective-permute-start | bytes 1769480 | tf_op jit(solution)/shard_map/ppermute | solution.py:72
  164.0 43.1 %collective-permute-start.33 = (bf16[4,8,4,48,768]{4,3,2,1,0:T(8,128)(2,1)}, bf16[4,8,4,48,768]{4,3,2,1,0:T(8,128)(2,1)}, u32[]{:S(2)}, u32[]{:S(2)}) collective-permute-start(bf16[4,8,4,48,768]{4,3,2,1,0:T(8,128)(2,1)} %get-tuple-element.155.mine), channel_id=1, source_target_pairs={{0,1},{1,0},{2,3},{3,2},{4,5},{5,4},{6,7},{7,6},{8,9},{9,8},{10,11... | collective-permute-start | bytes 28311560 | tf_op jit(solution)/shard_map/ppermute | solution.py:80
  196.8 34.5 %collective-permute-start.40 = (bf16[400,768]{1,0:T(8,128)(2,1)}, bf16[400,768]{1,0:T(8,128)(2,1)S(1)}, u32[]{:S(2)}, u32[]{:S(2)}) collective-permute-start(bf16[400,768]{1,0:T(8,128)(2,1)} %after.10), channel_id=1, source_target_pairs={{0,2},{2,0},{4,6},{6,4},{1,3},{3,1},{5,7},{7,5},{8,10},{10,8},{12,... | collective-permute-start | bytes 1843208 | tf_op jit(solution)/shard_map/ppermute | solution.py:72
  196.9 34.4 %collective-permute-start.41 = (bf16[400,768]{1,0:T(8,128)(2,1)}, bf16[400,768]{1,0:T(8,128)(2,1)S(1)}, u32[]{:S(2)}, u32[]{:S(2)}) collective-permute-start(bf16[400,768]{1,0:T(8,128)(2,1)} %after.11), channel_id=1, source_target_pairs={{0,4},{2,6},{4,0},{6,2},{1,5},{3,7},{5,1},{7,3},{8,12},{10,14},{12... | collective-permute-start | bytes 1843208 | tf_op jit(solution)/shard_map/ppermute | solution.py:72
  197.0 34.3 %collective-permute-start.42 = (bf16[400,768]{1,0:T(8,128)(2,1)}, bf16[400,768]{1,0:T(8,128)(2,1)S(1)}, u32[]{:S(2)}, u32[]{:S(2)}) collective-permute-start(bf16[400,768]{1,0:T(8,128)(2,1)} %after.12), channel_id=1, source_target_pairs={{0,6},{2,4},{4,2},{6,0},{1,7},{3,5},{5,3},{7,1},{8,14},{10,12},{12... | collective-permute-start | bytes 1843208 | tf_op jit(solution)/shard_map/ppermute | solution.py:72
  232.5 28.2 %collective-permute-start.43 = (bf16[2,384,768]{2,1,0:T(8,128)(2,1)}, bf16[2,384,768]{2,1,0:T(8,128)(2,1)S(1)}, u32[]{:S(2)}, u32[]{:S(2)}) collective-permute-start(bf16[2,384,768]{2,1,0:T(8,128)(2,1)} %after.13.refs_17_), channel_id=1, source_target_pairs={{0,2},{2,0},{4,6},{6,4},{1,3},{3,1},{5,7},{7,5},{8,10},{10,8},{12,... | collective-permute-start | bytes 3538952 | tf_op jit(solution)/shard_map/ppermute | solution.py:72
  232.6 41.1 %collective-permute-start.44 = (bf16[2,384,768]{2,1,0:T(8,128)(2,1)}, bf16[2,384,768]{2,1,0:T(8,128)(2,1)S(1)}, u32[]{:S(2)}, u32[]{:S(2)}) collective-permute-start(bf16[2,384,768]{2,1,0:T(8,128)(2,1)} %after.14.refs_18_), channel_id=1, source_target_pairs={{0,4},{2,6},{4,0},{6,2},{1,5},{3,7},{5,1},{7,3},{8,12},{10,14},{12... | collective-permute-start | bytes 3538952 | tf_op jit(solution)/shard_map/ppermute | solution.py:72
  251.1 28.2 %collective-permute-start.52 = (bf16[256,768]{1,0:T(8,128)(2,1)}, bf16[256,768]{1,0:T(8,128)(2,1)S(1)}, u32[]{:S(2)}, u32[]{:S(2)}) collective-permute-start(bf16[256,768]{1,0:T(8,128)(2,1)} %get-tuple-element.185.refs_2_.refs_4_), channel_id=1, source_target_pairs={{0,6},{2,4},{4,2},{6,0},{1,7},{3,5},{5,3},{7,1},{8,14},{10,12},{12... | collective-permute-start | bytes 1179656 | tf_op jit(solution)/shard_map/ppermute | solution.py:72
  253.5 27.2 %collective-permute-start.51 = (bf16[256,768]{1,0:T(8,128)(2,1)}, bf16[256,768]{1,0:T(8,128)(2,1)S(1)}, u32[]{:S(2)}, u32[]{:S(2)}) collective-permute-start(bf16[256,768]{1,0:T(8,128)(2,1)} %get-tuple-element.185.refs_2_.refs_4_), channel_id=1, source_target_pairs={{0,4},{2,6},{4,0},{6,2},{1,5},{3,7},{5,1},{7,3},{8,12},{10,14},{12... | collective-permute-start | bytes 1179656 | tf_op jit(solution)/shard_map/ppermute | solution.py:72
  253.5 27.2 %collective-permute-start.50 = (bf16[256,768]{1,0:T(8,128)(2,1)}, bf16[256,768]{1,0:T(8,128)(2,1)S(1)}, u32[]{:S(2)}, u32[]{:S(2)}) collective-permute-start(bf16[256,768]{1,0:T(8,128)(2,1)} %get-tuple-element.185.refs_2_.refs_4_), channel_id=1, source_target_pairs={{0,2},{2,0},{4,6},{6,4},{1,3},{3,1},{5,7},{7,5},{8,10},{10,8},{12,... | collective-permute-start | bytes 1179656 | tf_op jit(solution)/shard_map/ppermute | solution.py:72
  260.7 59.6 %collective-permute-start.60 = (bf16[4,8,4,48,768]{4,3,2,1,0:T(8,128)(2,1)}, bf16[4,8,4,48,768]{4,3,2,1,0:T(8,128)(2,1)}, u32[]{:S(2)}, u32[]{:S(2)}) collective-permute-start(bf16[4,8,4,48,768]{4,3,2,1,0:T(8,128)(2,1)} %after.15.mine), channel_id=1, source_target_pairs={{0,1},{1,0},{2,3},{3,2},{4,5},{5,4},{6,7},{7,6},{8,9},{9,8},{10,11... | collective-permute-start | bytes 28311560 | tf_op jit(solution)/shard_map/ppermute | solution.py:80
  328.7 25.7 %collective-permute-start.54 = (bf16[192,768]{1,0:T(8,128)(2,1)S(1)}, bf16[192,768]{1,0:T(8,128)(2,1)S(1)}, u32[]{:S(2)}, u32[]{:S(2)}) collective-permute-start(bf16[192,768]{1,0:T(8,128)(2,1)S(1)} %copy-done.41), channel_id=1, source_target_pairs={{0,24},{8,0},{16,8},{24,16},{1,25},{9,1},{17,9},{25,17},{2,26},{10... | collective-permute-start | bytes 884744 | tf_op jit(solution)/shard_map/ppermute | solution.py:76
  329.3 28.9 %collective-permute-start.55 = (bf16[192,768]{1,0:T(8,128)(2,1)S(1)}, bf16[192,768]{1,0:T(8,128)(2,1)S(1)}, u32[]{:S(2)}, u32[]{:S(2)}) collective-permute-start(bf16[192,768]{1,0:T(8,128)(2,1)S(1)} %copy-done.40), channel_id=1, source_target_pairs={{0,16},{8,24},{16,0},{24,8},{1,17},{9,25},{17,1},{25,9},{2,18},{10... | collective-permute-start | bytes 884744 | tf_op jit(solution)/shard_map/ppermute | solution.py:76
  330.0 28.2 %collective-permute-start.56 = (bf16[192,768]{1,0:T(8,128)(2,1)S(1)}, bf16[192,768]{1,0:T(8,128)(2,1)S(1)}, u32[]{:S(2)}, u32[]{:S(2)}) collective-permute-start(bf16[192,768]{1,0:T(8,128)(2,1)S(1)} %copy-done.39), channel_id=1, source_target_pairs={{0,8},{8,16},{16,24},{24,0},{1,9},{9,17},{17,25},{25,1},{2,10},{10... | collective-permute-start | bytes 884744 | tf_op jit(solution)/shard_map/ppermute | solution.py:76
  341.0 29.8 %collective-permute-start.64 = (f32[96,896]{1,0:T(8,128)}, f32[96,896]{1,0:T(8,128)S(1)}, u32[]{:S(2)}, u32[]{:S(2)}) collective-permute-start(f32[96,896]{1,0:T(8,128)} %get-tuple-element.214.refs_7_.refs_2_.refs_1_), channel_id=1, source_target_pairs={{0,1},{1,0},{2,3},{3,2},{4,5},{5,4},{6,7},{7,6},{8,9},{9,8},{10,11... | collective-permute-start | bytes 1032200 | tf_op jit(solution)/shard_map/ppermute | solution.py:80
  (106 other events, 848.6 us)

commit v3 on v2

--- a/solution.py
+++ b/solution.py
@@ -846,20 +846,22 @@
     packed, rest = call(pack_kernel, "pack", [sd((half, 896), bf16)] * 2,
                         (at, w_query, w_key, w_value, w_router.T, w_attn_out, gain_attn, gain_moe, rel_table.T),
                         scratch=[pltpu.VMEM((rows_dev, 896), f32)], smem=1)
-    mine = [to_expert(packed, k, size) for k in range(1, size)]
-    other = [to_core(m) for m in mine]
     pieces = gather_pieces(tok, count // 2)
     idx = call(functools.partial(prepare_kernel, size, chunks), "prepare", [sd((count, 8), i32)], (z[None], routes[0].T, capacity[None]),
                smem=1, deps=(packed,))[0]
 
-    g_blocks = spread(idx, cot, 0, size, local * CAP, (*mine, *pieces[1:3]), "spread_g", chunks)
+    g_blocks = spread(idx, cot, 0, size, local * CAP, (), "spread_g", chunks)
+    mine = [after(to_expert(packed, k, size), g_blocks[0]) for k in range(1, size)]
+    other = [to_core(m) for m in mine]
+    g_blocks = [g_blocks[0]] + [after(b, *mine) for b in g_blocks[1:]]
     g_arrived = shifted(g_blocks)
-    qkv_w, wo, router, gains, table = unpack(at, [packed, *mine], [rest, *other], buckets, (idx,))
-
-    xn, qkv = project(at, pieces, qkv_w, gains, (g_blocks[0],))
+    qkv_w, wo, router, gains, table = unpack(at, [packed, *mine], [rest, *other], buckets, pieces[1:3])
+
+    xn, qkv = project(at, pieces, qkv_w, gains, tuple(g_blocks[1:]))
     o, lse, *parts = attn_fwd(at, table, qkv, segments, wo, ())
     g_ordered = call(functools.partial(reorder_all_kernel, size), "order_g", [sd((local * CAP * size, width), bf16)], (matrix, *g_arrived), deps=(o,))[0]
-    terms = scatter_direct(parts[0], after(parts[1], g_ordered), *parts[2:])
+    terms = scatter_direct(parts[0], after(parts[1], g_ordered), parts[2], parts[3])
+    terms = (*terms[:2], after(terms[2], gains), after(terms[3], gains))
     h, xn2, probs, gate, *blocks = route(idx, tok, terms, router, gains, size, chunks, ())
     g_pieces = gather_pieces(after(g_ordered, xn2), half_rows * chunks)
 
@@ -910,14 +912,13 @@
         mark, back_blocks = give(0, False, (mark,))
     mark = expert_grads(1, mark)
     mark = expert_grads(1, mark, *back_blocks[1:])
-    mark = expert_grads(1, mark)
     ready, blocks = give(chunks - 1, True, (mark,))
     if chunks == 2:
         y_packs = [after(ys[c][1], mark, *sums[-1][1:]) for c in (0, 1)]
         y_got = [to_tensor(pack, flip) for flip, pack in zip((1, 2), y_packs)]
     else:
         y_terms = scatter_direct(*ys[0])
-    ready = (ready, *y_packs) if chunks == 2 else (ready,)
+    ready = (expert_grads(1, ready), *y_packs) if chunks == 2 else (ready,)
     dh, dhb, small = back(idx, cot, h, xn2, probs, gate, router, gains, back_blocks + blocks, size, chunks, ready)
     dh_pieces = gather_direct(dhb)
     mark = expert_grads(1, dhb)
@@ -934,7 +935,7 @@
     terms = scatter_direct(own, *parts)
     got = to_core(send)
     out_blocks = call(functools.partial(merge_kernel, size), "merge", [sd((half, packed.shape[1]), bf16)] * size,
-                      (at, keep, got), smem=1)
+                      (at, keep, got), smem=1, deps=other_acts[1:])
     outs = [sd((local * CAP, width), bf16)] * size
     if chunks == 2:
         given = call(functools.partial(give_back_halves_kernel, size), "give_back_y", outs, (matrix, ys[0][0], ys[1][0], *y_parts), deps=(out_blocks[0],))
@@ -948,9 +949,9 @@
                        (at, w_query, w_key, w_value, *shifted(out_blocks)), smem=1, deps=(mark, *terms[1:]))
     mark = expert_grads(1, total)
     gain = gain + to_tensor(gain, 1)
-    mark = expert_grads(1, mark, gain)
+    mark = expert_grads(len(pending), mark, gain)
     gain = gain + to_tensor(gain, 2)
-    output = mix(idx, h, gate, y_blocks, size, chunks, (total,))
+    output = mix(idx, h, gate, y_blocks, size, chunks, (mark,))
     lw = w_query.shape[1]
     outs = [sd((rows_dev, lw), f32)] * 4 + [sd((experts, rows_dev), f32), sd(rel_table.T.shape, f32)] + [sd((1, rows_dev), f32)] * 2
     grad_q, grad_k, grad_v, grad_o, grad_router, grad_table, grad_ga, grad_gm = call(

time: 379 us -> 364 us (0.960)
  waiting for transfers between devices: 65.5 us -> 43.5 us
  starting transfers between devices: 97.2 us -> 101 us
    ppermute x24, waiting for transfers between devices: 37.2 us -> 19 us  [to_expert(): lax.ppermute(a, 'expert', [(i, (i + shift) % size) for i in range(size)])]
    ppermute x8, starting transfers between devices: 35.2 us -> 25.9 us  [to_core(): return lax.ppermute(a, 'rep', [(0, 1), (1, 0)])]
    ppermute x36, starting transfers between devices: 29.4 us -> 37.6 us  [to_tensor(): return lax.ppermute(a, 'tensor', [(i, i ^ flip) for i in range(4)])]
    ppermute x24, starting transfers between devices: 32.6 us -> 37.7 us  [to_expert(): lax.ppermute(a, 'expert', [(i, (i + shift) % size) for i in range(size)])]
  transfers between devices with their start and end apart: 68 -> 68, of which waited for: 15 -> 10; matrix products, arithmetic and copies ran while one was open for 1% -> 1% of each run, Pallas kernels for 50% -> 52%
where the time goes in v3:
time: 364 us; the launch traced here: 360 us
  Pallas kernels  192 us (53%)
  starting transfers between devices  101 us (28%)
  waiting for transfers between devices  43.5 us (12%)
  local copies, waits for them, and re-layouts  20.2 us (6%)
    pallas_call x23, Pallas kernels, call(): pl.pallas_call(body, out_shape=tuple(outs), in_specs=[SM] * smem + [VM] *...  98 us
    pallas_call x8, Pallas kernels, expert_grad(): pl.pallas_call(functools.partial(expert_grad_kernel, steps), grid=(part,...  54.4 us
    pallas_call x2, Pallas kernels, moe(): pl.pallas_call(functools.partial(moe_kernel, rows, part, first, last, len...  39.4 us
    ppermute x24, starting transfers between devices, to_expert(): lax.ppermute(a, 'expert', [(i, (i + shift) % size) for i in range(size)])  37.7 us
    ppermute x36, starting transfers between devices, to_tensor(): return lax.ppermute(a, 'tensor', [(i, i ^ flip) for i in range(4)])  37.6 us
    ppermute x8, starting transfers between devices, to_core(): return lax.ppermute(a, 'rep', [(0, 1), (1, 0)])  25.9 us
    ppermute x36, waiting for transfers between devices, to_tensor(): return lax.ppermute(a, 'tensor', [(i, i ^ flip) for i in range(4)])  24.5 us
    ppermute x24, waiting for transfers between devices, to_expert(): lax.ppermute(a, 'expert', [(i, (i + shift) % size) for i in range(size)])  19 us
  transfers between devices with their start and end apart: 68, of which 10 were waited for; matrix products, arithmetic and copies ran while one was open for 1% of the time, Pallas kernels for 52%

profile of v3, /device:TPU:1, one launch (start us, length us, event | category | flops | bytes accessed | tf_op | source)
XLA Modules:
  0.0 359.6 jit_solution(10482097348038448825)
XLA Ops:
  25.0 5.0 %collective-permute-start.12 = (bf16[192,768]{1,0:T(8,128)(2,1)}, bf16[192,768]{1,0:T(8,128)(2,1)S(1)}, u32[]{:S(2)}, u32[]{:S(2)}) collective-permute-start(bf16[192,768]{1,0:T(8,128)(2,1)} %after.21.refs_10_), channel_id=1, source_target_pairs={{0,24},{8,0},{16,8},{24,16},{1,25},{9,1},{17,9},{25,17},{2,26},{10... | collective-permute-start | bytes 884744 | tf_op jit(solution)/shard_map/ppermute | solution.py:76
  34.4 4.5 %project.1 = (bf16[1024,768]{1,0:T(8,128)(2,1)}, bf16[1024,576]{1,0:T(8,128)(2,1)}) custom-call(s32[3]{0:T(128)} %pad_add_fusion.refs_0_.at_ref, bf16[256,768]{1,0:T(8,128)(2,1)} %bitcast.20, bf16[256,768]{1,0:T(8,128)(2,1)} %copy-done.14, bf16[256,768]{1,0:T(8,128)(2,1)} %copy-done.13, bf16[128,768]{1,0:T(8,128)(2,1)} %copy-done.50, ...), custom_call_target="tpu_custom_call" | custom-call | flops 5750000128 | bytes 1000 | tf_op jit(solution)/shard_map/project/pallas_call | solution.py:48
  38.8 12.3 %attn_fwd.1 = (bf16[1024,192]{1,0:T(8,128)(2,1)}, f32[1024,3]{1,0:T(8,128)}, bf16[256,768]{1,0:T(8,128)(2,1)}, bf16[256,768]{1,0:T(8,128)(2,1)}, bf16[256,768]{1,0:T(8,128)(2,1)}, /*index=5*/bf16[256,768]{1,0:T(8,128)(2,1)}) custom-call(s32[3]{0:T(128)} %pad_add_fusion.refs_0_.at_ref, f32[32,128]{1,0:T(8,128)} %get-tuple-element.126.refs_1_, ...), custom_call_target="tpu_custom_call" | custom-call | flops 14949999616 | bytes 1000 | tf_op jit(solution)/shard_map/attn_fwd/pallas_call | solution.py:48
  60.3 8.7 %collective-permute-done.14.refs_0_ = bf16[256,768]{1,0:T(8,128)(2,1)S(1)} collective-permute-done((bf16[256,768]{1,0:T(8,128)(2,1)}, bf16[256,768]{1,0:T(8,128)(2,1)S(1)}, u32[]{:S(2)}, u32[]{:S(2)}) %collective-permute-start.14) | collective-permute-done | bytes 393248 | tf_op jit(solution)/shard_map/ppermute | solution.py:72
  71.2 4.1 %route.1 = (f32[256,768]{1,0:T(8,128)}, bf16[256,768]{1,0:T(8,128)(2,1)}, f32[256,64]{1,0:T(8,128)}, f32[256,8]{1,0:T(8,128)}, bf16[112,768]{1,0:T(8,128)(2,1)},...) custom-call(s32[256,8]{1,0:T(8,128)} %prepare.1.refs_0_, bf16[256,768]{1,0:T(8,128)(2,1)} %bitcast.21, ...), custom_call_target="tpu_custom_call" | custom-call | flops 4600000000 | bytes 1000 | tf_op jit(solution)/shard_map/route/pallas_call | solution.py:48
  84.8 9.3 %collective-permute-done.17.refs_3_ = bf16[112,768]{1,0:T(8,128)(2,1)S(1)} collective-permute-done((bf16[112,768]{1,0:T(8,128)(2,1)}, bf16[112,768]{1,0:T(8,128)(2,1)S(1)}, u32[]{:S(2)}, u32[]{:S(2)}) %collective-permute-start.17) | collective-permute-done | bytes 172064 | tf_op jit(solution)/shard_map/ppermute | solution.py:76
  108.8 6.9 %collective-permute-done.20.py.e_py = bf16[400,768]{1,0:T(8,128)(2,1)S(1)} collective-permute-done((bf16[400,768]{1,0:T(8,128)(2,1)}, bf16[400,768]{1,0:T(8,128)(2,1)S(1)}, u32[]{:S(2)}, u32[]{:S(2)}) %collective-permute-start.20) | collective-permute-done | bytes 614432 | tf_op jit(solution)/shard_map/ppermute | solution.py:72
  128.9 5.9 %collective-permute-done.21.d0 = bf16[192,768]{1,0:T(8,128)(2,1)S(1)} collective-permute-done((bf16[192,768]{1,0:T(8,128)(2,1)S(1)}, bf16[192,768]{1,0:T(8,128)(2,1)S(1)}, u32[]{:S(2)}, u32[]{:S(2)}) %collective-permute-start.21) | collective-permute-done | bytes 294944 | tf_op jit(solution)/shard_map/ppermute | solution.py:72
  138.5 19.4 %moe.2 = (bf16[384,768]{1,0:T(8,128)(2,1)}, bf16[384,768]{1,0:T(8,128)(2,1)}, bf16[384,768]{1,0:T(8,128)(2,1)}, bf16[384,768]{1,0:T(8,128)(2,1)}, bf16[384,768]{...) custom-call(s32[3]{0:T(128)} %pad_add_fusion.refs_0_.at_ref, ...), custom_call_target="tpu_custom_call" | custom-call | flops 344999985152 | bytes 1000 | tf_op jit(solution)/shard_map/moe/pallas_call | solution.py:658
  160.6 8.5 %collective-permute-start.33 = (bf16[4,8,4,48,768]{4,3,2,1,0:T(8,128)(2,1)}, bf16[4,8,4,48,768]{4,3,2,1,0:T(8,128)(2,1)}, u32[]{:S(2)}, u32[]{:S(2)}) collective-permute-start(bf16[4,8,4,48,768]{4,3,2,1,0:T(8,128)(2,1)} %get-tuple-element.155.mine), channel_id=1, source_target_pairs={{0,1},{1,0},{2,3},{3,2},{4,5},{5,4},{6,7},{7,6},{8,9},{9,8},{10,11... | collective-permute-start | bytes 28311560 | tf_op jit(solution)/shard_map/ppermute | solution.py:80
  169.2 20.0 %moe.3 = (bf16[400,768]{1,0:T(8,128)(2,1)}, bf16[400,768]{1,0:T(8,128)(2,1)}, bf16[400,768]{1,0:T(8,128)(2,1)}, bf16[400,768]{1,0:T(8,128)(2,1)}, bf16[384,768]{...) custom-call(s32[3]{0:T(128)} %pad_add_fusion.refs_0_.at_ref, ...), custom_call_target="tpu_custom_call" | custom-call | flops 344999985152 | bytes 1000 | tf_op jit(solution)/shard_map/moe/pallas_call | solution.py:658
  205.0 6.7 %expert_grad.8 = (f32[16,768,768]{2,1,0:T(8,128)}, f32[16,768,768]{2,1,0:T(8,128)}, f32[8,128]{1,0:T(8,128)}) custom-call(s32[3]{0:T(128)} %pad_add_fusion.refs_0_.at_ref, bf16[4,8,4,48,768]{4,3,2,1,0:T(8,128)(2,1)} %get-tuple-element.155.mine, bf16[4,8,4,48,768]{4,3,2,1,0:T(8,128)(2,1)} %collective-permute-done.33.other, ...), custom_call_target="tpu_custom_call" | custom-call | flops 1150000000 | bytes 1000 | tf_op jit(solution)/shard_map/expert_grad/pallas_call | solution.py:700
  212.5 6.7 %expert_grad.9 = (f32[16,768,768]{2,1,0:T(8,128)}, f32[16,768,768]{2,1,0:T(8,128)}, f32[8,128]{1,0:T(8,128)}) custom-call(s32[3]{0:T(128)} %pad_add_fusion.refs_0_.at_ref, bf16[4,8,4,48,768]{4,3,2,1,0:T(8,128)(2,1)} %get-tuple-element.155.mine, ...), custom_call_target="tpu_custom_call", output_to_operand_aliasing={{0}: (3, {}), {1}: (4, {})} | custom-call | flops 1150000000 | bytes 1000 | tf_op jit(solution)/shard_map/expert_grad/pallas_call | solution.py:700
  227.1 6.7 %expert_grad.10 = (f32[16,768,768]{2,1,0:T(8,128)}, f32[16,768,768]{2,1,0:T(8,128)}, f32[8,128]{1,0:T(8,128)}) custom-call(s32[3]{0:T(128)} %pad_add_fusion.refs_0_.at_ref, bf16[4,8,4,48,768]{4,3,2,1,0:T(8,128)(2,1)} %get-tuple-element.155.mine, ...), custom_call_target="tpu_custom_call", output_to_operand_aliasing={{0}: (3, {}), {1}: (4, {})} | custom-call | flops 1150000000 | bytes 1000 | tf_op jit(solution)/shard_map/expert_grad/pallas_call | solution.py:700
  235.4 4.9 %back.1 = (f32[256,768]{1,0:T(8,128)}, bf16[256,768]{1,0:T(8,128)(2,1)}, bf16[768,128]{1,0:T(8,128)(2,1)}) custom-call(s32[256,8]{1,0:T(8,128)} %prepare.1.refs_0_, bf16[256,768]{1,0:T(8,128)(2,1)} %bitcast.25, f32[256,768]{1,0:T(8,128)} %get-tuple-element.140.refs_2_.refs_1_, bf16[256,768]{1,0:T(8,128)(2,1)} %get-tuple-element.146.refs_1_.refs_3_, ...), custom_call_target="tpu_custom_call" | custom-call | flops 5750000128 | bytes 1000 | tf_op jit(solution)/shard_map/back/pallas_call | solution.py:48
  243.0 6.9 %expert_grad.11 = (f32[16,768,768]{2,1,0:T(8,128)}, f32[16,768,768]{2,1,0:T(8,128)}, f32[8,128]{1,0:T(8,128)}) custom-call(s32[3]{0:T(128)} %pad_add_fusion.refs_0_.at_ref, bf16[4,8,4,48,768]{4,3,2,1,0:T(8,128)(2,1)} %get-tuple-element.155.mine, ...), custom_call_target="tpu_custom_call", output_to_operand_aliasing={{0}: (3, {}), {1}: (4, {})} | custom-call | flops 1150000000 | bytes 1000 | tf_op jit(solution)/shard_map/expert_grad/pallas_call | solution.py:700
  249.9 10.6 %collective-permute-start.54 = (bf16[4,8,4,48,768]{4,3,2,1,0:T(8,128)(2,1)}, bf16[4,8,4,48,768]{4,3,2,1,0:T(8,128)(2,1)}, u32[]{:S(2)}, u32[]{:S(2)}) collective-permute-start(bf16[4,8,4,48,768]{4,3,2,1,0:T(8,128)(2,1)} %after.31.mine), channel_id=1, source_target_pairs={{0,1},{1,0},{2,3},{3,2},{4,5},{5,4},{6,7},{7,6},{8,9},{9,8},{10,11... | collective-permute-start | bytes 28311560 | tf_op jit(solution)/shard_map/ppermute | solution.py:80
  267.4 18.0 %attn_bwd.1 = (f32[4,8,128]{2,1,0:T(8,128)}, bf16[1024,576]{1,0:T(8,128)(2,1)}) custom-call(s32[3]{0:T(128)} %pad_add_fusion.refs_0_.at_ref, f32[32,128]{1,0:T(8,128)} %get-tuple-element.126.refs_1_, bf16[256,768]{1,0:T(8,128)(2,1)} %get-tuple-element.185.refs_2_.refs_4_, bf16[256,768]{1,0:T(8,128)(2,1)} %copy-done.41, bf16[256,768]{1,0:T(8,128)(2,1)} %copy-done.40, ...), custom_call_target="tpu_custom_call" | custom-call | flops 460000002048 | bytes 1000 | tf_op jit(solution)/shard_map/attn_bwd/pallas_call | solution.py:48
  285.5 7.4 %attn_grad.1 = (bf16[4,96,896]{2,1,0:T(8,128)(2,1)}, bf16[4,96,896]{2,1,0:T(8,128)(2,1)}, bf16[256,768]{1,0:T(8,128)(2,1)}, bf16[256,768]{1,0:T(8,128)(2,1)}, bf...) custom-call(s32[3]{0:T(128)} %pad_add_fusion.refs_0_.at_ref, bf16[1024,576]{1,0:T(8,128)(2,1)} %get-tuple-element.190.refs_1_, ...), custom_call_target="tpu_custom_call" | custom-call | flops 10350000128 | bytes 1000 | tf_op jit(solution)/shard_map/attn_grad/pallas_call | solution.py:48
  301.1 4.2 %give_back_y.1 = (bf16[192,768]{1,0:T(8,128)(2,1)}, bf16[192,768]{1,0:T(8,128)(2,1)}, bf16[192,768]{1,0:T(8,128)(2,1)}, bf16[192,768]{1,0:T(8,128)(2,1)}) custom-call(bf16[384,384]{1,0:T(8,128)(2,1)} %constant.17.clone.refs_0_, bf16[384,768]{1,0:T(8,128)(2,1)} %get-tuple-element.151.refs_1_, bf16[384,768]{1,0:T(8,128)(2,1)} %get-tuple-element.153.refs_2_, ...), custom_call_target="tpu_custom_call" | custom-call | flops 575000000 | bytes 1000 | tf_op jit(solution)/shard_map/give_back_y/pallas_call | solution.py:48
  307.7 6.8 %expert_grad.12 = (f32[16,768,768]{2,1,0:T(8,128)}, f32[16,768,768]{2,1,0:T(8,128)}, f32[8,128]{1,0:T(8,128)}) custom-call(s32[3]{0:T(128)} %pad_add_fusion.refs_0_.at_ref, bf16[4,8,4,48,768]{4,3,2,1,0:T(8,128)(2,1)} %after.31.mine, bf16[4,8,4,48,768]{4,3,2,1,0:T(8,128)(2,1)} %collective-permute-done.54.refs_3_.other, ...), custom_call_target="tpu_custom_call", output_to_operand_aliasing={{0}: (3, {}), {1}: (4, {})} | custom-call | flops 1150000000 | bytes 1000 | tf_op jit(solution)/shard_map/expert_grad/pallas_call | solution.py:700
  316.2 6.8 %expert_grad.13 = (f32[16,768,768]{2,1,0:T(8,128)}, f32[16,768,768]{2,1,0:T(8,128)}, f32[8,128]{1,0:T(8,128)}) custom-call(s32[3]{0:T(128)} %pad_add_fusion.refs_0_.at_ref, bf16[4,8,4,48,768]{4,3,2,1,0:T(8,128)(2,1)} %after.31.mine, bf16[4,8,4,48,768]{4,3,2,1,0:T(8,128)(2,1)} %collective-permute-done.54.refs_3_.other, ...), custom_call_target="tpu_custom_call", output_to_operand_aliasing={{0}: (3, {}), {1}: (4, {})} | custom-call | flops 1150000000 | bytes 1000 | tf_op jit(solution)/shard_map/expert_grad/pallas_call | solution.py:700
  335.0 7.0 %expert_grad.14 = (f32[16,768,768]{2,1,0:T(8,128)}, f32[16,768,768]{2,1,0:T(8,128)}, f32[8,128]{1,0:T(8,128)}) custom-call(s32[3]{0:T(128)} %pad_add_fusion.refs_0_.at_ref, bf16[4,8,4,48,768]{4,3,2,1,0:T(8,128)(2,1)} %after.31.mine, bf16[4,8,4,48,768]{4,3,2,1,0:T(8,128)(2,1)} %collective-permute-done.54.refs_3_.other, ...), custom_call_target="tpu_custom_call", output_to_operand_aliasing={{0}: (3, {}), {1}: (4, {})} | custom-call | flops 1150000000 | bytes 1000 | tf_op jit(solution)/shard_map/expert_grad/pallas_call | solution.py:700
  343.5 6.8 %expert_grad.15 = (f32[16,768,768]{2,1,0:T(8,128)}, f32[16,768,768]{2,1,0:T(8,128)}, f32[8,128]{1,0:T(8,128)}) custom-call(s32[3]{0:T(128)} %pad_add_fusion.refs_0_.at_ref, bf16[4,8,4,48,768]{4,3,2,1,0:T(8,128)(2,1)} %after.31.mine, bf16[4,8,4,48,768]{4,3,2,1,0:T(8,128)(2,1)} %collective-permute-done.54.refs_3_.other, ...), custom_call_target="tpu_custom_call", output_to_operand_aliasing={{0}: (3, {}), {1}: (4, {})} | custom-call | flops 1150000000 | bytes 1000 | tf_op jit(solution)/shard_map/expert_grad/pallas_call | solution.py:700
  (296 shorter events, 153.8 us)
Async XLA Ops:
  25.0 28.6 %collective-permute-start.12 = (bf16[192,768]{1,0:T(8,128)(2,1)}, bf16[192,768]{1,0:T(8,128)(2,1)S(1)}, u32[]{:S(2)}, u32[]{:S(2)}) collective-permute-start(bf16[192,768]{1,0:T(8,128)(2,1)} %after.21.refs_10_), channel_id=1, source_target_pairs={{0,24},{8,0},{16,8},{24,16},{1,25},{9,1},{17,9},{25,17},{2,26},{10... | collective-permute-start | bytes 884744 | tf_op jit(solution)/shard_map/ppermute | solution.py:76
  30.0 25.1 %collective-permute-start.11 = (bf16[192,768]{1,0:T(8,128)(2,1)}, bf16[192,768]{1,0:T(8,128)(2,1)S(1)}, u32[]{:S(2)}, u32[]{:S(2)}) collective-permute-start(bf16[192,768]{1,0:T(8,128)(2,1)} %after.20.refs_9_), channel_id=1, source_target_pairs={{0,16},{8,24},{16,0},{24,8},{1,17},{9,25},{17,1},{25,9},{2,18},{10... | collective-permute-start | bytes 884744 | tf_op jit(solution)/shard_map/ppermute | solution.py:76
  75.4 25.3 %collective-permute-start.23 = (bf16[768,768]{1,0:T(8,128)(2,1)}, bf16[768,768]{1,0:T(8,128)(2,1)S(1)}, u32[]{:S(2)}, u32[]{:S(2)}) collective-permute-start(bf16[768,768]{1,0:T(8,128)(2,1)} %after.25.g_own), channel_id=1, source_target_pairs={{0,2},{2,0},{4,6},{6,4},{1,3},{3,1},{5,7},{7,5},{8,10},{10,8},{12,... | collective-permute-start | bytes 3538952 | tf_op jit(solution)/shard_map/ppermute | solution.py:72
  76.6 26.8 %collective-permute-start.24 = (bf16[768,768]{1,0:T(8,128)(2,1)}, bf16[768,768]{1,0:T(8,128)(2,1)S(1)}, u32[]{:S(2)}, u32[]{:S(2)}) collective-permute-start(bf16[768,768]{1,0:T(8,128)(2,1)} %after.25.g_own), channel_id=1, source_target_pairs={{0,4},{2,6},{4,0},{6,2},{1,5},{3,7},{5,1},{7,3},{8,12},{10,14},{12... | collective-permute-start | bytes 3538952 | tf_op jit(solution)/shard_map/ppermute | solution.py:72
  100.7 37.0 %collective-permute-start.25 = (bf16[384,768]{1,0:T(8,128)(2,1)S(1)}, bf16[384,768]{1,0:T(8,128)(2,1)S(1)}, u32[]{:S(2)}, u32[]{:S(2)}) collective-permute-start(bf16[384,768]{1,0:T(8,128)(2,1)S(1)} %slice.28), channel_id=1, source_target_pairs={{0,4},{2,6},{4,0},{6,2},{1,5},{3,7},{5,1},{7,3},{8,12},{10,14},{12... | collective-permute-start | bytes 1769480 | tf_op jit(solution)/shard_map/ppermute | solution.py:72
  124.0 34.3 %collective-permute-start.32 = (bf16[384,768]{1,0:T(8,128)(2,1)}, bf16[384,768]{1,0:T(8,128)(2,1)}, u32[]{:S(2)}, u32[]{:S(2)}) collective-permute-start(bf16[384,768]{1,0:T(8,128)(2,1)} %slice.29), channel_id=1, source_target_pairs={{0,2},{2,0},{4,6},{6,4},{1,3},{3,1},{5,7},{7,5},{8,10},{10,8},{12,... | collective-permute-start | bytes 1769480 | tf_op jit(solution)/shard_map/ppermute | solution.py:72
  128.3 30.0 %collective-permute-start.31 = (bf16[384,768]{1,0:T(8,128)(2,1)}, bf16[384,768]{1,0:T(8,128)(2,1)}, u32[]{:S(2)}, u32[]{:S(2)}) collective-permute-start(bf16[384,768]{1,0:T(8,128)(2,1)} %order.3.refs_0_.own), channel_id=1, source_target_pairs={{0,6},{2,4},{4,2},{6,0},{1,7},{3,5},{5,3},{7,1},{8,14},{10,12},{12... | collective-permute-start | bytes 1769480 | tf_op jit(solution)/shard_map/ppermute | solution.py:72
  134.8 25.8 %collective-permute-start.30 = (bf16[384,768]{1,0:T(8,128)(2,1)}, bf16[384,768]{1,0:T(8,128)(2,1)}, u32[]{:S(2)}, u32[]{:S(2)}) collective-permute-start(bf16[384,768]{1,0:T(8,128)(2,1)} %order.3.refs_0_.own), channel_id=1, source_target_pairs={{0,4},{2,6},{4,0},{6,2},{1,5},{3,7},{5,1},{7,3},{8,12},{10,14},{12... | collective-permute-start | bytes 1769480 | tf_op jit(solution)/shard_map/ppermute | solution.py:72
  136.5 32.7 %collective-permute-start.29 = (bf16[384,768]{1,0:T(8,128)(2,1)}, bf16[384,768]{1,0:T(8,128)(2,1)}, u32[]{:S(2)}, u32[]{:S(2)}) collective-permute-start(bf16[384,768]{1,0:T(8,128)(2,1)} %order.3.refs_0_.own), channel_id=1, source_target_pairs={{0,2},{2,0},{4,6},{6,4},{1,3},{3,1},{5,7},{7,5},{8,10},{10,8},{12,... | collective-permute-start | bytes 1769480 | tf_op jit(solution)/shard_map/ppermute | solution.py:72
  157.9 31.3 %collective-permute-start.34 = (bf16[384,768]{1,0:T(8,128)(2,1)}, bf16[384,768]{1,0:T(8,128)(2,1)}, u32[]{:S(2)}, u32[]{:S(2)}) collective-permute-start(bf16[384,768]{1,0:T(8,128)(2,1)} %get-tuple-element.157), channel_id=1, source_target_pairs={{0,2},{2,0},{4,6},{6,4},{1,3},{3,1},{5,7},{7,5},{8,10},{10,8},{12,... | collective-permute-start | bytes 1769480 | tf_op jit(solution)/shard_map/ppermute | solution.py:72
  158.2 31.0 %collective-permute-start.35 = (bf16[384,768]{1,0:T(8,128)(2,1)}, bf16[384,768]{1,0:T(8,128)(2,1)}, u32[]{:S(2)}, u32[]{:S(2)}) collective-permute-start(bf16[384,768]{1,0:T(8,128)(2,1)} %get-tuple-element.158), channel_id=1, source_target_pairs={{0,4},{2,6},{4,0},{6,2},{1,5},{3,7},{5,1},{7,3},{8,12},{10,14},{12... | collective-permute-start | bytes 1769480 | tf_op jit(solution)/shard_map/ppermute | solution.py:72
  158.3 30.9 %collective-permute-start.36 = (bf16[384,768]{1,0:T(8,128)(2,1)}, bf16[384,768]{1,0:T(8,128)(2,1)}, u32[]{:S(2)}, u32[]{:S(2)}) collective-permute-start(bf16[384,768]{1,0:T(8,128)(2,1)} %get-tuple-element.159), channel_id=1, source_target_pairs={{0,6},{2,4},{4,2},{6,0},{1,7},{3,5},{5,3},{7,1},{8,14},{10,12},{12... | collective-permute-start | bytes 1769480 | tf_op jit(solution)/shard_map/ppermute | solution.py:72
  160.6 41.4 %collective-permute-start.33 = (bf16[4,8,4,48,768]{4,3,2,1,0:T(8,128)(2,1)}, bf16[4,8,4,48,768]{4,3,2,1,0:T(8,128)(2,1)}, u32[]{:S(2)}, u32[]{:S(2)}) collective-permute-start(bf16[4,8,4,48,768]{4,3,2,1,0:T(8,128)(2,1)} %get-tuple-element.155.mine), channel_id=1, source_target_pairs={{0,1},{1,0},{2,3},{3,2},{4,5},{5,4},{6,7},{7,6},{8,9},{9,8},{10,11... | collective-permute-start | bytes 28311560 | tf_op jit(solution)/shard_map/ppermute | solution.py:80
  189.2 30.0 %collective-permute-start.40 = (bf16[400,768]{1,0:T(8,128)(2,1)}, bf16[400,768]{1,0:T(8,128)(2,1)S(1)}, u32[]{:S(2)}, u32[]{:S(2)}) collective-permute-start(bf16[400,768]{1,0:T(8,128)(2,1)} %after.26), channel_id=1, source_target_pairs={{0,2},{2,0},{4,6},{6,4},{1,3},{3,1},{5,7},{7,5},{8,10},{10,8},{12,... | collective-permute-start | bytes 1843208 | tf_op jit(solution)/shard_map/ppermute | solution.py:72
  189.6 29.7 %collective-permute-start.41 = (bf16[400,768]{1,0:T(8,128)(2,1)}, bf16[400,768]{1,0:T(8,128)(2,1)S(1)}, u32[]{:S(2)}, u32[]{:S(2)}) collective-permute-start(bf16[400,768]{1,0:T(8,128)(2,1)} %after.27), channel_id=1, source_target_pairs={{0,4},{2,6},{4,0},{6,2},{1,5},{3,7},{5,1},{7,3},{8,12},{10,14},{12... | collective-permute-start | bytes 1843208 | tf_op jit(solution)/shard_map/ppermute | solution.py:72
  189.6 29.7 %collective-permute-start.42 = (bf16[400,768]{1,0:T(8,128)(2,1)}, bf16[400,768]{1,0:T(8,128)(2,1)S(1)}, u32[]{:S(2)}, u32[]{:S(2)}) collective-permute-start(bf16[400,768]{1,0:T(8,128)(2,1)} %after.28), channel_id=1, source_target_pairs={{0,6},{2,4},{4,2},{6,0},{1,7},{3,5},{5,3},{7,1},{8,14},{10,12},{12... | collective-permute-start | bytes 1843208 | tf_op jit(solution)/shard_map/ppermute | solution.py:72
  220.5 29.4 %collective-permute-start.43 = (bf16[2,384,768]{2,1,0:T(8,128)(2,1)}, bf16[2,384,768]{2,1,0:T(8,128)(2,1)S(1)}, u32[]{:S(2)}, u32[]{:S(2)}) collective-permute-start(bf16[2,384,768]{2,1,0:T(8,128)(2,1)} %after.29.refs_17_), channel_id=1, source_target_pairs={{0,2},{2,0},{4,6},{6,4},{1,3},{3,1},{5,7},{7,5},{8,10},{10,8},{12,... | collective-permute-start | bytes 3538952 | tf_op jit(solution)/shard_map/ppermute | solution.py:72
  221.9 38.7 %collective-permute-start.44 = (bf16[2,384,768]{2,1,0:T(8,128)(2,1)}, bf16[2,384,768]{2,1,0:T(8,128)(2,1)S(1)}, u32[]{:S(2)}, u32[]{:S(2)}) collective-permute-start(bf16[2,384,768]{2,1,0:T(8,128)(2,1)} %after.30.refs_18_), channel_id=1, source_target_pairs={{0,4},{2,6},{4,0},{6,2},{1,5},{3,7},{5,1},{7,3},{8,12},{10,14},{12... | collective-permute-start | bytes 3538952 | tf_op jit(solution)/shard_map/ppermute | solution.py:72
  240.3 25.3 %collective-permute-start.52 = (bf16[256,768]{1,0:T(8,128)(2,1)}, bf16[256,768]{1,0:T(8,128)(2,1)S(1)}, u32[]{:S(2)}, u32[]{:S(2)}) collective-permute-start(bf16[256,768]{1,0:T(8,128)(2,1)} %get-tuple-element.185.refs_2_.refs_4_), channel_id=1, source_target_pairs={{0,6},{2,4},{4,2},{6,0},{1,7},{3,5},{5,3},{7,1},{8,14},{10,12},{12... | collective-permute-start | bytes 1179656 | tf_op jit(solution)/shard_map/ppermute | solution.py:72
  249.9 47.2 %collective-permute-start.54 = (bf16[4,8,4,48,768]{4,3,2,1,0:T(8,128)(2,1)}, bf16[4,8,4,48,768]{4,3,2,1,0:T(8,128)(2,1)}, u32[]{:S(2)}, u32[]{:S(2)}) collective-permute-start(bf16[4,8,4,48,768]{4,3,2,1,0:T(8,128)(2,1)} %after.31.mine), channel_id=1, source_target_pairs={{0,1},{1,0},{2,3},{3,2},{4,5},{5,4},{6,7},{7,6},{8,9},{9,8},{10,11... | collective-permute-start | bytes 28311560 | tf_op jit(solution)/shard_map/ppermute | solution.py:80
  314.5 37.2 %collective-permute-start.55 = (bf16[192,768]{1,0:T(8,128)(2,1)S(1)}, bf16[192,768]{1,0:T(8,128)(2,1)S(1)}, u32[]{:S(2)}, u32[]{:S(2)}) collective-permute-start(bf16[192,768]{1,0:T(8,128)(2,1)S(1)} %copy-done.47), channel_id=1, source_target_pairs={{0,24},{8,0},{16,8},{24,16},{1,25},{9,1},{17,9},{25,17},{2,26},{10... | collective-permute-start | bytes 884744 | tf_op jit(solution)/shard_map/ppermute | solution.py:76
  314.9 36.8 %collective-permute-start.56 = (bf16[192,768]{1,0:T(8,128)(2,1)S(1)}, bf16[192,768]{1,0:T(8,128)(2,1)S(1)}, u32[]{:S(2)}, u32[]{:S(2)}) collective-permute-start(bf16[192,768]{1,0:T(8,128)(2,1)S(1)} %copy-done.46), channel_id=1, source_target_pairs={{0,16},{8,24},{16,0},{24,8},{1,17},{9,25},{17,1},{25,9},{2,18},{10... | collective-permute-start | bytes 884744 | tf_op jit(solution)/shard_map/ppermute | solution.py:76
  323.1 28.7 %collective-permute-start.57 = (bf16[192,768]{1,0:T(8,128)(2,1)S(1)}, bf16[192,768]{1,0:T(8,128)(2,1)S(1)}, u32[]{:S(2)}, u32[]{:S(2)}) collective-permute-start(bf16[192,768]{1,0:T(8,128)(2,1)S(1)} %copy-done.45), channel_id=1, source_target_pairs={{0,8},{8,16},{16,24},{24,0},{1,9},{9,17},{17,25},{25,1},{2,10},{10... | collective-permute-start | bytes 884744 | tf_op jit(solution)/shard_map/ppermute | solution.py:76
  327.6 28.2 %collective-permute-start.65 = (f32[96,896]{1,0:T(8,128)}, f32[96,896]{1,0:T(8,128)S(1)}, u32[]{:S(2)}, u32[]{:S(2)}) collective-permute-start(f32[96,896]{1,0:T(8,128)} %get-tuple-element.216.refs_2_.refs_1_), channel_id=1, source_target_pairs={{0,1},{1,0},{2,3},{3,2},{4,5},{5,4},{6,7},{7,6},{8,9},{9,8},{10,11... | collective-permute-start | bytes 1032200 | tf_op jit(solution)/shard_map/ppermute | solution.py:80
  (106 other events, 809.0 us)

commit v4 on v3

--- a/solution.py
+++ b/solution.py
@@ -32,7 +32,7 @@
 
 
 ANY = pl.BlockSpec(memory_space=pl.ANY)
-TIMES = {"attn_fwd": 13, "attn_bwd": 400, "attn_grad": 9, "project": 5, "moe": 300, "expert_grad": 1, "back": 5, "route": 4}
+TIMES = {"attn_fwd": 13, "attn_bwd": 400, "attn_grad": 9, "project": 5, "moe": 400, "expert_grad": 1, "back": 5, "route": 4}
 
 
 def cost(name):
@@ -909,7 +909,7 @@
     back_blocks = []
     mark = outs[0]
     if chunks == 2:
-        mark, back_blocks = give(0, False, (mark,))
+        mark, back_blocks = give(0, False, (mark, other_acts[0]))
     mark = expert_grads(1, mark)
     mark = expert_grads(1, mark, *back_blocks[1:])
     ready, blocks = give(chunks - 1, True, (mark,))
@@ -942,12 +942,12 @@
     else:
         given = call(functools.partial(give_back_kernel, size, False), "give_back_y", outs, (matrix, *y_terms), deps=(out_blocks[0],))
     y_blocks = [given[0]] + [to_expert(given[k], size - k, size) for k in range(1, size)]
-    grad_tokens = call(last_kernel, "last", [sd((count, width), f32)], (tok, dh, *terms, gains))[0]
     mark = expert_grads(1, out_blocks[0], given[0])
     mark = expert_grads(max(len(pending) - 2, 0), mark, *terms[1:])
     total, gain = call(functools.partial(total_kernel, size), "total", [sd(out_blocks[0].shape, f32), sd((half, 128), f32)],
                        (at, w_query, w_key, w_value, *shifted(out_blocks)), smem=1, deps=(mark, *terms[1:]))
     mark = expert_grads(1, total)
+    grad_tokens = call(last_kernel, "last", [sd((count, width), f32)], (tok, dh, *terms, gains), deps=(mark,))[0]
     gain = gain + to_tensor(gain, 1)
     mark = expert_grads(len(pending), mark, gain)
     gain = gain + to_tensor(gain, 2)

time: 364 us -> 364 us (level)
  waiting for transfers between devices: 43.5 us -> 51.2 us
  starting transfers between devices: 101 us -> 93.5 us
    ppermute x8, starting transfers between devices: 25.9 us -> 18.4 us  [to_core(): return lax.ppermute(a, 'rep', [(0, 1), (1, 0)])]
    ppermute x24, waiting for transfers between devices: 19 us -> 24.9 us  [to_expert(): lax.ppermute(a, 'expert', [(i, (i + shift) % size) for i in range(size)])]
  transfers between devices with their start and end apart: 68 -> 68, of which waited for: 10 -> 11; matrix products, arithmetic and copies ran while one was open for 1% -> 1% of each run, Pallas kernels for 52% -> 52%
where the time goes in v4:
time: 364 us; the launch traced here: 360 us
  Pallas kernels  192 us (53%)
  starting transfers between devices  93.5 us (26%)
  waiting for transfers between devices  51.2 us (14%)
  local copies, waits for them, and re-layouts  20.2 us (6%)
    pallas_call x23, Pallas kernels, call(): pl.pallas_call(body, out_shape=tuple(outs), in_specs=[SM] * smem + [VM] *...  98 us
    pallas_call x8, Pallas kernels, expert_grad(): pl.pallas_call(functools.partial(expert_grad_kernel, steps), grid=(part,...  54.4 us
    ppermute x24, starting transfers between devices, to_expert(): lax.ppermute(a, 'expert', [(i, (i + shift) % size) for i in range(size)])  39.5 us
    pallas_call x2, Pallas kernels, moe(): pl.pallas_call(functools.partial(moe_kernel, rows, part, first, last, len...  39.4 us
    ppermute x36, starting transfers between devices, to_tensor(): return lax.ppermute(a, 'tensor', [(i, i ^ flip) for i in range(4)])  35.6 us
    ppermute x36, waiting for transfers between devices, to_tensor(): return lax.ppermute(a, 'tensor', [(i, i ^ flip) for i in range(4)])  26.3 us
    ppermute x24, waiting for transfers between devices, to_expert(): lax.ppermute(a, 'expert', [(i, (i + shift) % size) for i in range(size)])  24.9 us
    ppermute x8, starting transfers between devices, to_core(): return lax.ppermute(a, 'rep', [(0, 1), (1, 0)])  18.4 us
  transfers between devices with their start and end apart: 68, of which 11 were waited for; matrix products, arithmetic and copies ran while one was open for 1% of the time, Pallas kernels for 52%

profile of v4, /device:TPU:1, one launch (start us, length us, event | category | flops | bytes accessed | tf_op | source)
XLA Modules:
  0.0 359.6 jit_solution(3580845261808712251)
XLA Ops:
  25.0 5.0 %collective-permute-start.12 = (bf16[192,768]{1,0:T(8,128)(2,1)}, bf16[192,768]{1,0:T(8,128)(2,1)S(1)}, u32[]{:S(2)}, u32[]{:S(2)}) collective-permute-start(bf16[192,768]{1,0:T(8,128)(2,1)} %after.21.refs_10_), channel_id=1, source_target_pairs={{0,24},{8,0},{16,8},{24,16},{1,25},{9,1},{17,9},{25,17},{2,26},{10... | collective-permute-start | bytes 884744 | tf_op jit(solution)/shard_map/ppermute | solution.py:76
  34.4 4.5 %project.1 = (bf16[1024,768]{1,0:T(8,128)(2,1)}, bf16[1024,576]{1,0:T(8,128)(2,1)}) custom-call(s32[3]{0:T(128)} %pad_add_fusion.refs_0_.at_ref, bf16[256,768]{1,0:T(8,128)(2,1)} %bitcast.21, bf16[256,768]{1,0:T(8,128)(2,1)} %copy-done.14, bf16[256,768]{1,0:T(8,128)(2,1)} %copy-done.13, bf16[128,768]{1,0:T(8,128)(2,1)} %copy-done.50, ...), custom_call_target="tpu_custom_call" | custom-call | flops 5750000128 | bytes 1000 | tf_op jit(solution)/shard_map/project/pallas_call | solution.py:48
  38.8 12.3 %attn_fwd.1 = (bf16[1024,192]{1,0:T(8,128)(2,1)}, f32[1024,3]{1,0:T(8,128)}, bf16[256,768]{1,0:T(8,128)(2,1)}, bf16[256,768]{1,0:T(8,128)(2,1)}, bf16[256,768]{1,0:T(8,128)(2,1)}, /*index=5*/bf16[256,768]{1,0:T(8,128)(2,1)}) custom-call(s32[3]{0:T(128)} %pad_add_fusion.refs_0_.at_ref, f32[32,128]{1,0:T(8,128)} %get-tuple-element.126.refs_1_, ...), custom_call_target="tpu_custom_call" | custom-call | flops 14949999616 | bytes 1000 | tf_op jit(solution)/shard_map/attn_fwd/pallas_call | solution.py:48
  60.3 8.7 %collective-permute-done.14.refs_0_ = bf16[256,768]{1,0:T(8,128)(2,1)S(1)} collective-permute-done((bf16[256,768]{1,0:T(8,128)(2,1)}, bf16[256,768]{1,0:T(8,128)(2,1)S(1)}, u32[]{:S(2)}, u32[]{:S(2)}) %collective-permute-start.14) | collective-permute-done | bytes 393248 | tf_op jit(solution)/shard_map/ppermute | solution.py:72
  84.8 9.3 %collective-permute-done.17.refs_3_ = bf16[112,768]{1,0:T(8,128)(2,1)S(1)} collective-permute-done((bf16[112,768]{1,0:T(8,128)(2,1)}, bf16[112,768]{1,0:T(8,128)(2,1)S(1)}, u32[]{:S(2)}, u32[]{:S(2)}) %collective-permute-start.17) | collective-permute-done | bytes 172064 | tf_op jit(solution)/shard_map/ppermute | solution.py:76
  108.8 6.9 %collective-permute-done.20.py.e_py = bf16[400,768]{1,0:T(8,128)(2,1)S(1)} collective-permute-done((bf16[400,768]{1,0:T(8,128)(2,1)}, bf16[400,768]{1,0:T(8,128)(2,1)S(1)}, u32[]{:S(2)}, u32[]{:S(2)}) %collective-permute-start.20) | collective-permute-done | bytes 614432 | tf_op jit(solution)/shard_map/ppermute | solution.py:72
  128.9 5.9 %collective-permute-done.21.d0 = bf16[192,768]{1,0:T(8,128)(2,1)S(1)} collective-permute-done((bf16[192,768]{1,0:T(8,128)(2,1)S(1)}, bf16[192,768]{1,0:T(8,128)(2,1)S(1)}, u32[]{:S(2)}, u32[]{:S(2)}) %collective-permute-start.21) | collective-permute-done | bytes 294944 | tf_op jit(solution)/shard_map/ppermute | solution.py:72
  138.5 19.4 %moe.2 = (bf16[384,768]{1,0:T(8,128)(2,1)}, bf16[384,768]{1,0:T(8,128)(2,1)}, bf16[384,768]{1,0:T(8,128)(2,1)}, bf16[384,768]{1,0:T(8,128)(2,1)}, bf16[384,768]{...) custom-call(s32[3]{0:T(128)} %pad_add_fusion.refs_0_.at_ref, ...), custom_call_target="tpu_custom_call" | custom-call | flops 460000002048 | bytes 1000 | tf_op jit(solution)/shard_map/moe/pallas_call | solution.py:658
  160.6 8.5 %collective-permute-start.33 = (bf16[4,8,4,48,768]{4,3,2,1,0:T(8,128)(2,1)}, bf16[4,8,4,48,768]{4,3,2,1,0:T(8,128)(2,1)}, u32[]{:S(2)}, u32[]{:S(2)}) collective-permute-start(bf16[4,8,4,48,768]{4,3,2,1,0:T(8,128)(2,1)} %get-tuple-element.155.mine), channel_id=1, source_target_pairs={{0,1},{1,0},{2,3},{3,2},{4,5},{5,4},{6,7},{7,6},{8,9},{9,8},{10,11... | collective-permute-start | bytes 28311560 | tf_op jit(solution)/shard_map/ppermute | solution.py:80
  169.2 20.0 %moe.3 = (bf16[400,768]{1,0:T(8,128)(2,1)}, bf16[400,768]{1,0:T(8,128)(2,1)}, bf16[400,768]{1,0:T(8,128)(2,1)}, bf16[400,768]{1,0:T(8,128)(2,1)}, bf16[384,768]{...) custom-call(s32[3]{0:T(128)} %pad_add_fusion.refs_0_.at_ref, ...), custom_call_target="tpu_custom_call" | custom-call | flops 460000002048 | bytes 1000 | tf_op jit(solution)/shard_map/moe/pallas_call | solution.py:658
  203.8 6.7 %expert_grad.8 = (f32[16,768,768]{2,1,0:T(8,128)}, f32[16,768,768]{2,1,0:T(8,128)}, f32[8,128]{1,0:T(8,128)}) custom-call(s32[3]{0:T(128)} %pad_add_fusion.refs_0_.at_ref, bf16[4,8,4,48,768]{4,3,2,1,0:T(8,128)(2,1)} %get-tuple-element.155.mine, bf16[4,8,4,48,768]{4,3,2,1,0:T(8,128)(2,1)} %collective-permute-done.33.refs_6_.other, ...), custom_call_target="tpu_custom_call" | custom-call | flops 1150000000 | bytes 1000 | tf_op jit(solution)/shard_map/expert_grad/pallas_call | solution.py:700
  211.2 6.7 %expert_grad.9 = (f32[16,768,768]{2,1,0:T(8,128)}, f32[16,768,768]{2,1,0:T(8,128)}, f32[8,128]{1,0:T(8,128)}) custom-call(s32[3]{0:T(128)} %pad_add_fusion.refs_0_.at_ref, bf16[4,8,4,48,768]{4,3,2,1,0:T(8,128)(2,1)} %get-tuple-element.155.mine, ...), custom_call_target="tpu_custom_call", output_to_operand_aliasing={{0}: (3, {}), {1}: (4, {})} | custom-call | flops 1150000000 | bytes 1000 | tf_op jit(solution)/shard_map/expert_grad/pallas_call | solution.py:700
  223.8 4.7 %collective-permute-start.45 = (bf16[112,768]{1,0:T(8,128)(2,1)}, bf16[112,768]{1,0:T(8,128)(2,1)S(1)}, u32[]{:S(2)}, u32[]{:S(2)}) collective-permute-start(bf16[112,768]{1,0:T(8,128)(2,1)} %get-tuple-element.181), channel_id=1, source_target_pairs={{0,24},{8,0},{16,8},{24,16},{1,25},{9,1},{17,9},{25,17},{2,26},{10... | collective-permute-start | bytes 516104 | tf_op jit(solution)/shard_map/ppermute | solution.py:76
  228.7 6.7 %expert_grad.10 = (f32[16,768,768]{2,1,0:T(8,128)}, f32[16,768,768]{2,1,0:T(8,128)}, f32[8,128]{1,0:T(8,128)}) custom-call(s32[3]{0:T(128)} %pad_add_fusion.refs_0_.at_ref, bf16[4,8,4,48,768]{4,3,2,1,0:T(8,128)(2,1)} %get-tuple-element.155.mine, ...), custom_call_target="tpu_custom_call", output_to_operand_aliasing={{0}: (3, {}), {1}: (4, {})} | custom-call | flops 1150000000 | bytes 1000 | tf_op jit(solution)/shard_map/expert_grad/pallas_call | solution.py:700
  235.5 7.0 %collective-permute-done.46.refs_14_ = bf16[112,768]{1,0:T(8,128)(2,1)S(1)} collective-permute-done((bf16[112,768]{1,0:T(8,128)(2,1)}, bf16[112,768]{1,0:T(8,128)(2,1)S(1)}, u32[]{:S(2)}, u32[]{:S(2)}) %collective-permute-start.46) | collective-permute-done | bytes 172064 | tf_op jit(solution)/shard_map/ppermute | solution.py:76
  243.2 4.9 %back.1 = (f32[256,768]{1,0:T(8,128)}, bf16[256,768]{1,0:T(8,128)(2,1)}, bf16[768,128]{1,0:T(8,128)(2,1)}) custom-call(s32[256,8]{1,0:T(8,128)} %prepare.1.refs_0_, bf16[256,768]{1,0:T(8,128)(2,1)} %bitcast.25, f32[256,768]{1,0:T(8,128)} %get-tuple-element.140.refs_2_.refs_1_, bf16[256,768]{1,0:T(8,128)(2,1)} %get-tuple-element.146.refs_1_.refs_3_, ...), custom_call_target="tpu_custom_call" | custom-call | flops 5750000128 | bytes 1000 | tf_op jit(solution)/shard_map/back/pallas_call | solution.py:48
  250.7 6.9 %expert_grad.11 = (f32[16,768,768]{2,1,0:T(8,128)}, f32[16,768,768]{2,1,0:T(8,128)}, f32[8,128]{1,0:T(8,128)}) custom-call(s32[3]{0:T(128)} %pad_add_fusion.refs_0_.at_ref, bf16[4,8,4,48,768]{4,3,2,1,0:T(8,128)(2,1)} %get-tuple-element.155.mine, ...), custom_call_target="tpu_custom_call", output_to_operand_aliasing={{0}: (3, {}), {1}: (4, {})} | custom-call | flops 1150000000 | bytes 1000 | tf_op jit(solution)/shard_map/expert_grad/pallas_call | solution.py:700
  269.5 18.0 %attn_bwd.1 = (f32[4,8,128]{2,1,0:T(8,128)}, bf16[1024,576]{1,0:T(8,128)(2,1)}) custom-call(s32[3]{0:T(128)} %pad_add_fusion.refs_0_.at_ref, f32[32,128]{1,0:T(8,128)} %get-tuple-element.126.refs_1_, bf16[256,768]{1,0:T(8,128)(2,1)} %get-tuple-element.185.refs_2_.refs_4_, bf16[256,768]{1,0:T(8,128)(2,1)} %copy-done.41, bf16[256,768]{1,0:T(8,128)(2,1)} %copy-done.40, ...), custom_call_target="tpu_custom_call" | custom-call | flops 460000002048 | bytes 1000 | tf_op jit(solution)/shard_map/attn_bwd/pallas_call | solution.py:48
  287.6 7.4 %attn_grad.1 = (bf16[4,96,896]{2,1,0:T(8,128)(2,1)}, bf16[4,96,896]{2,1,0:T(8,128)(2,1)}, bf16[256,768]{1,0:T(8,128)(2,1)}, bf16[256,768]{1,0:T(8,128)(2,1)}, bf...) custom-call(s32[3]{0:T(128)} %pad_add_fusion.refs_0_.at_ref, bf16[1024,576]{1,0:T(8,128)(2,1)} %get-tuple-element.190.refs_1_, ...), custom_call_target="tpu_custom_call" | custom-call | flops 10350000128 | bytes 1000 | tf_op jit(solution)/shard_map/attn_grad/pallas_call | solution.py:48
  304.0 4.2 %give_back_y.1 = (bf16[192,768]{1,0:T(8,128)(2,1)}, bf16[192,768]{1,0:T(8,128)(2,1)}, bf16[192,768]{1,0:T(8,128)(2,1)}, bf16[192,768]{1,0:T(8,128)(2,1)}) custom-call(bf16[384,384]{1,0:T(8,128)(2,1)} %constant.17.clone.refs_0_, bf16[384,768]{1,0:T(8,128)(2,1)} %get-tuple-element.151.refs_1_, bf16[384,768]{1,0:T(8,128)(2,1)} %get-tuple-element.153.refs_2_, ...), custom_call_target="tpu_custom_call" | custom-call | flops 575000000 | bytes 1000 | tf_op jit(solution)/shard_map/give_back_y/pallas_call | solution.py:48
  309.7 6.8 %expert_grad.12 = (f32[16,768,768]{2,1,0:T(8,128)}, f32[16,768,768]{2,1,0:T(8,128)}, f32[8,128]{1,0:T(8,128)}) custom-call(s32[3]{0:T(128)} %pad_add_fusion.refs_0_.at_ref, bf16[4,8,4,48,768]{4,3,2,1,0:T(8,128)(2,1)} %after.31.mine, bf16[4,8,4,48,768]{4,3,2,1,0:T(8,128)(2,1)} %collective-permute-done.54.refs_3_.other, ...), custom_call_target="tpu_custom_call", output_to_operand_aliasing={{0}: (3, {}), {1}: (4, {})} | custom-call | flops 1150000000 | bytes 1000 | tf_op jit(solution)/shard_map/expert_grad/pallas_call | solution.py:700
  317.8 6.8 %expert_grad.13 = (f32[16,768,768]{2,1,0:T(8,128)}, f32[16,768,768]{2,1,0:T(8,128)}, f32[8,128]{1,0:T(8,128)}) custom-call(s32[3]{0:T(128)} %pad_add_fusion.refs_0_.at_ref, bf16[4,8,4,48,768]{4,3,2,1,0:T(8,128)(2,1)} %after.31.mine, bf16[4,8,4,48,768]{4,3,2,1,0:T(8,128)(2,1)} %collective-permute-done.54.refs_3_.other, ...), custom_call_target="tpu_custom_call", output_to_operand_aliasing={{0}: (3, {}), {1}: (4, {})} | custom-call | flops 1150000000 | bytes 1000 | tf_op jit(solution)/shard_map/expert_grad/pallas_call | solution.py:700
  332.4 7.0 %expert_grad.14 = (f32[16,768,768]{2,1,0:T(8,128)}, f32[16,768,768]{2,1,0:T(8,128)}, f32[8,128]{1,0:T(8,128)}) custom-call(s32[3]{0:T(128)} %pad_add_fusion.refs_0_.at_ref, bf16[4,8,4,48,768]{4,3,2,1,0:T(8,128)(2,1)} %after.31.mine, bf16[4,8,4,48,768]{4,3,2,1,0:T(8,128)(2,1)} %collective-permute-done.54.refs_3_.other, ...), custom_call_target="tpu_custom_call", output_to_operand_aliasing={{0}: (3, {}), {1}: (4, {})} | custom-call | flops 1150000000 | bytes 1000 | tf_op jit(solution)/shard_map/expert_grad/pallas_call | solution.py:700
  343.5 6.8 %expert_grad.15 = (f32[16,768,768]{2,1,0:T(8,128)}, f32[16,768,768]{2,1,0:T(8,128)}, f32[8,128]{1,0:T(8,128)}) custom-call(s32[3]{0:T(128)} %pad_add_fusion.refs_0_.at_ref, bf16[4,8,4,48,768]{4,3,2,1,0:T(8,128)(2,1)} %after.31.mine, bf16[4,8,4,48,768]{4,3,2,1,0:T(8,128)(2,1)} %collective-permute-done.54.refs_3_.other, ...), custom_call_target="tpu_custom_call", output_to_operand_aliasing={{0}: (3, {}), {1}: (4, {})} | custom-call | flops 1150000000 | bytes 1000 | tf_op jit(solution)/shard_map/expert_grad/pallas_call | solution.py:700
  (296 shorter events, 156.9 us)
Async XLA Ops:
  25.0 28.6 %collective-permute-start.12 = (bf16[192,768]{1,0:T(8,128)(2,1)}, bf16[192,768]{1,0:T(8,128)(2,1)S(1)}, u32[]{:S(2)}, u32[]{:S(2)}) collective-permute-start(bf16[192,768]{1,0:T(8,128)(2,1)} %after.21.refs_10_), channel_id=1, source_target_pairs={{0,24},{8,0},{16,8},{24,16},{1,25},{9,1},{17,9},{25,17},{2,26},{10... | collective-permute-start | bytes 884744 | tf_op jit(solution)/shard_map/ppermute | solution.py:76
  30.0 25.1 %collective-permute-start.11 = (bf16[192,768]{1,0:T(8,128)(2,1)}, bf16[192,768]{1,0:T(8,128)(2,1)S(1)}, u32[]{:S(2)}, u32[]{:S(2)}) collective-permute-start(bf16[192,768]{1,0:T(8,128)(2,1)} %after.20.refs_9_), channel_id=1, source_target_pairs={{0,16},{8,24},{16,0},{24,8},{1,17},{9,25},{17,1},{25,9},{2,18},{10... | collective-permute-start | bytes 884744 | tf_op jit(solution)/shard_map/ppermute | solution.py:76
  30.0 25.1 %collective-permute-start.10 = (bf16[192,768]{1,0:T(8,128)(2,1)}, bf16[192,768]{1,0:T(8,128)(2,1)S(1)}, u32[]{:S(2)}, u32[]{:S(2)}) collective-permute-start(bf16[192,768]{1,0:T(8,128)(2,1)} %after.19.refs_8_), channel_id=1, source_target_pairs={{0,8},{8,16},{16,24},{24,0},{1,9},{9,17},{17,25},{25,1},{2,10},{10... | collective-permute-start | bytes 884744 | tf_op jit(solution)/shard_map/ppermute | solution.py:76
  75.4 25.3 %collective-permute-start.23 = (bf16[768,768]{1,0:T(8,128)(2,1)}, bf16[768,768]{1,0:T(8,128)(2,1)S(1)}, u32[]{:S(2)}, u32[]{:S(2)}) collective-permute-start(bf16[768,768]{1,0:T(8,128)(2,1)} %after.25.g_own), channel_id=1, source_target_pairs={{0,2},{2,0},{4,6},{6,4},{1,3},{3,1},{5,7},{7,5},{8,10},{10,8},{12,... | collective-permute-start | bytes 3538952 | tf_op jit(solution)/shard_map/ppermute | solution.py:72
  76.6 26.8 %collective-permute-start.24 = (bf16[768,768]{1,0:T(8,128)(2,1)}, bf16[768,768]{1,0:T(8,128)(2,1)S(1)}, u32[]{:S(2)}, u32[]{:S(2)}) collective-permute-start(bf16[768,768]{1,0:T(8,128)(2,1)} %after.25.g_own), channel_id=1, source_target_pairs={{0,4},{2,6},{4,0},{6,2},{1,5},{3,7},{5,1},{7,3},{8,12},{10,14},{12... | collective-permute-start | bytes 3538952 | tf_op jit(solution)/shard_map/ppermute | solution.py:72
  100.7 37.0 %collective-permute-start.25 = (bf16[384,768]{1,0:T(8,128)(2,1)S(1)}, bf16[384,768]{1,0:T(8,128)(2,1)S(1)}, u32[]{:S(2)}, u32[]{:S(2)}) collective-permute-start(bf16[384,768]{1,0:T(8,128)(2,1)S(1)} %slice.28), channel_id=1, source_target_pairs={{0,4},{2,6},{4,0},{6,2},{1,5},{3,7},{5,1},{7,3},{8,12},{10,14},{12... | collective-permute-start | bytes 1769480 | tf_op jit(solution)/shard_map/ppermute | solution.py:72
  124.0 34.3 %collective-permute-start.32 = (bf16[384,768]{1,0:T(8,128)(2,1)}, bf16[384,768]{1,0:T(8,128)(2,1)}, u32[]{:S(2)}, u32[]{:S(2)}) collective-permute-start(bf16[384,768]{1,0:T(8,128)(2,1)} %slice.29), channel_id=1, source_target_pairs={{0,2},{2,0},{4,6},{6,4},{1,3},{3,1},{5,7},{7,5},{8,10},{10,8},{12,... | collective-permute-start | bytes 1769480 | tf_op jit(solution)/shard_map/ppermute | solution.py:72
  128.3 30.0 %collective-permute-start.31 = (bf16[384,768]{1,0:T(8,128)(2,1)}, bf16[384,768]{1,0:T(8,128)(2,1)}, u32[]{:S(2)}, u32[]{:S(2)}) collective-permute-start(bf16[384,768]{1,0:T(8,128)(2,1)} %order.3.refs_0_.own), channel_id=1, source_target_pairs={{0,6},{2,4},{4,2},{6,0},{1,7},{3,5},{5,3},{7,1},{8,14},{10,12},{12... | collective-permute-start | bytes 1769480 | tf_op jit(solution)/shard_map/ppermute | solution.py:72
  134.8 25.8 %collective-permute-start.30 = (bf16[384,768]{1,0:T(8,128)(2,1)}, bf16[384,768]{1,0:T(8,128)(2,1)}, u32[]{:S(2)}, u32[]{:S(2)}) collective-permute-start(bf16[384,768]{1,0:T(8,128)(2,1)} %order.3.refs_0_.own), channel_id=1, source_target_pairs={{0,4},{2,6},{4,0},{6,2},{1,5},{3,7},{5,1},{7,3},{8,12},{10,14},{12... | collective-permute-start | bytes 1769480 | tf_op jit(solution)/shard_map/ppermute | solution.py:72
  136.5 32.7 %collective-permute-start.29 = (bf16[384,768]{1,0:T(8,128)(2,1)}, bf16[384,768]{1,0:T(8,128)(2,1)}, u32[]{:S(2)}, u32[]{:S(2)}) collective-permute-start(bf16[384,768]{1,0:T(8,128)(2,1)} %order.3.refs_0_.own), channel_id=1, source_target_pairs={{0,2},{2,0},{4,6},{6,4},{1,3},{3,1},{5,7},{7,5},{8,10},{10,8},{12,... | collective-permute-start | bytes 1769480 | tf_op jit(solution)/shard_map/ppermute | solution.py:72
  157.9 31.3 %collective-permute-start.34 = (bf16[384,768]{1,0:T(8,128)(2,1)}, bf16[384,768]{1,0:T(8,128)(2,1)}, u32[]{:S(2)}, u32[]{:S(2)}) collective-permute-start(bf16[384,768]{1,0:T(8,128)(2,1)} %get-tuple-element.157), channel_id=1, source_target_pairs={{0,2},{2,0},{4,6},{6,4},{1,3},{3,1},{5,7},{7,5},{8,10},{10,8},{12,... | collective-permute-start | bytes 1769480 | tf_op jit(solution)/shard_map/ppermute | solution.py:72
  158.2 31.0 %collective-permute-start.35 = (bf16[384,768]{1,0:T(8,128)(2,1)}, bf16[384,768]{1,0:T(8,128)(2,1)}, u32[]{:S(2)}, u32[]{:S(2)}) collective-permute-start(bf16[384,768]{1,0:T(8,128)(2,1)} %get-tuple-element.158), channel_id=1, source_target_pairs={{0,4},{2,6},{4,0},{6,2},{1,5},{3,7},{5,1},{7,3},{8,12},{10,14},{12... | collective-permute-start | bytes 1769480 | tf_op jit(solution)/shard_map/ppermute | solution.py:72
  158.3 30.9 %collective-permute-start.36 = (bf16[384,768]{1,0:T(8,128)(2,1)}, bf16[384,768]{1,0:T(8,128)(2,1)}, u32[]{:S(2)}, u32[]{:S(2)}) collective-permute-start(bf16[384,768]{1,0:T(8,128)(2,1)} %get-tuple-element.159), channel_id=1, source_target_pairs={{0,6},{2,4},{4,2},{6,0},{1,7},{3,5},{5,3},{7,1},{8,14},{10,12},{12... | collective-permute-start | bytes 1769480 | tf_op jit(solution)/shard_map/ppermute | solution.py:72
  160.6 31.3 %collective-permute-start.33 = (bf16[4,8,4,48,768]{4,3,2,1,0:T(8,128)(2,1)}, bf16[4,8,4,48,768]{4,3,2,1,0:T(8,128)(2,1)}, u32[]{:S(2)}, u32[]{:S(2)}) collective-permute-start(bf16[4,8,4,48,768]{4,3,2,1,0:T(8,128)(2,1)} %get-tuple-element.155.mine), channel_id=1, source_target_pairs={{0,1},{1,0},{2,3},{3,2},{4,5},{5,4},{6,7},{7,6},{8,9},{9,8},{10,11... | collective-permute-start | bytes 28311560 | tf_op jit(solution)/shard_map/ppermute | solution.py:80
  189.2 28.7 %collective-permute-start.42 = (bf16[400,768]{1,0:T(8,128)(2,1)}, bf16[400,768]{1,0:T(8,128)(2,1)S(1)}, u32[]{:S(2)}, u32[]{:S(2)}) collective-permute-start(bf16[400,768]{1,0:T(8,128)(2,1)} %after.28), channel_id=1, source_target_pairs={{0,6},{2,4},{4,2},{6,0},{1,7},{3,5},{5,3},{7,1},{8,14},{10,12},{12... | collective-permute-start | bytes 1843208 | tf_op jit(solution)/shard_map/ppermute | solution.py:72
  189.3 28.6 %collective-permute-start.41 = (bf16[400,768]{1,0:T(8,128)(2,1)}, bf16[400,768]{1,0:T(8,128)(2,1)S(1)}, u32[]{:S(2)}, u32[]{:S(2)}) collective-permute-start(bf16[400,768]{1,0:T(8,128)(2,1)} %after.27), channel_id=1, source_target_pairs={{0,4},{2,6},{4,0},{6,2},{1,5},{3,7},{5,1},{7,3},{8,12},{10,14},{12... | collective-permute-start | bytes 1843208 | tf_op jit(solution)/shard_map/ppermute | solution.py:72
  190.7 27.2 %collective-permute-start.40 = (bf16[400,768]{1,0:T(8,128)(2,1)}, bf16[400,768]{1,0:T(8,128)(2,1)S(1)}, u32[]{:S(2)}, u32[]{:S(2)}) collective-permute-start(bf16[400,768]{1,0:T(8,128)(2,1)} %after.26), channel_id=1, source_target_pairs={{0,2},{2,0},{4,6},{6,4},{1,3},{3,1},{5,7},{7,5},{8,10},{10,8},{12,... | collective-permute-start | bytes 1843208 | tf_op jit(solution)/shard_map/ppermute | solution.py:72
  219.2 38.5 %collective-permute-start.43 = (bf16[2,384,768]{2,1,0:T(8,128)(2,1)}, bf16[2,384,768]{2,1,0:T(8,128)(2,1)S(1)}, u32[]{:S(2)}, u32[]{:S(2)}) collective-permute-start(bf16[2,384,768]{2,1,0:T(8,128)(2,1)} %after.29.refs_17_), channel_id=1, source_target_pairs={{0,2},{2,0},{4,6},{6,4},{1,3},{3,1},{5,7},{7,5},{8,10},{10,8},{12,... | collective-permute-start | bytes 3538952 | tf_op jit(solution)/shard_map/ppermute | solution.py:72
  220.6 40.6 %collective-permute-start.44 = (bf16[2,384,768]{2,1,0:T(8,128)(2,1)}, bf16[2,384,768]{2,1,0:T(8,128)(2,1)S(1)}, u32[]{:S(2)}, u32[]{:S(2)}) collective-permute-start(bf16[2,384,768]{2,1,0:T(8,128)(2,1)} %after.30.refs_18_), channel_id=1, source_target_pairs={{0,4},{2,6},{4,0},{6,2},{1,5},{3,7},{5,1},{7,3},{8,12},{10,14},{12... | collective-permute-start | bytes 3538952 | tf_op jit(solution)/shard_map/ppermute | solution.py:72
  257.7 40.6 %collective-permute-start.54 = (bf16[4,8,4,48,768]{4,3,2,1,0:T(8,128)(2,1)}, bf16[4,8,4,48,768]{4,3,2,1,0:T(8,128)(2,1)}, u32[]{:S(2)}, u32[]{:S(2)}) collective-permute-start(bf16[4,8,4,48,768]{4,3,2,1,0:T(8,128)(2,1)} %after.31.mine), channel_id=1, source_target_pairs={{0,1},{1,0},{2,3},{3,2},{4,5},{5,4},{6,7},{7,6},{8,9},{9,8},{10,11... | collective-permute-start | bytes 28311560 | tf_op jit(solution)/shard_map/ppermute | solution.py:80
  316.5 35.2 %collective-permute-start.55 = (bf16[192,768]{1,0:T(8,128)(2,1)S(1)}, bf16[192,768]{1,0:T(8,128)(2,1)S(1)}, u32[]{:S(2)}, u32[]{:S(2)}) collective-permute-start(bf16[192,768]{1,0:T(8,128)(2,1)S(1)} %copy-done.47), channel_id=1, source_target_pairs={{0,24},{8,0},{16,8},{24,16},{1,25},{9,1},{17,9},{25,17},{2,26},{10... | collective-permute-start | bytes 884744 | tf_op jit(solution)/shard_map/ppermute | solution.py:76
  316.7 35.0 %collective-permute-start.56 = (bf16[192,768]{1,0:T(8,128)(2,1)S(1)}, bf16[192,768]{1,0:T(8,128)(2,1)S(1)}, u32[]{:S(2)}, u32[]{:S(2)}) collective-permute-start(bf16[192,768]{1,0:T(8,128)(2,1)S(1)} %copy-done.46), channel_id=1, source_target_pairs={{0,16},{8,24},{16,0},{24,8},{1,17},{9,25},{17,1},{25,9},{2,18},{10... | collective-permute-start | bytes 884744 | tf_op jit(solution)/shard_map/ppermute | solution.py:76
  324.7 27.1 %collective-permute-start.57 = (bf16[192,768]{1,0:T(8,128)(2,1)S(1)}, bf16[192,768]{1,0:T(8,128)(2,1)S(1)}, u32[]{:S(2)}, u32[]{:S(2)}) collective-permute-start(bf16[192,768]{1,0:T(8,128)(2,1)S(1)} %copy-done.45), channel_id=1, source_target_pairs={{0,8},{8,16},{16,24},{24,0},{1,9},{9,17},{17,25},{25,1},{2,10},{10... | collective-permute-start | bytes 884744 | tf_op jit(solution)/shard_map/ppermute | solution.py:76
  328.8 27.0 %collective-permute-start.65 = (f32[96,896]{1,0:T(8,128)}, f32[96,896]{1,0:T(8,128)S(1)}, u32[]{:S(2)}, u32[]{:S(2)}) collective-permute-start(f32[96,896]{1,0:T(8,128)} %get-tuple-element.216.refs_2_.refs_1_), channel_id=1, source_target_pairs={{0,1},{1,0},{2,3},{3,2},{4,5},{5,4},{6,7},{7,6},{8,9},{9,8},{10,11... | collective-permute-start | bytes 1032200 | tf_op jit(solution)/shard_map/ppermute | solution.py:80
  (106 other events, 812.2 us)

commit v5 on v3

--- a/solution.py
+++ b/solution.py
@@ -32,7 +32,7 @@
 
 
 ANY = pl.BlockSpec(memory_space=pl.ANY)
-TIMES = {"attn_fwd": 13, "attn_bwd": 400, "attn_grad": 9, "project": 5, "moe": 300, "expert_grad": 1, "back": 5, "route": 4}
+TIMES = {"attn_fwd": 13, "prepare": 30, "attn_bwd": 400, "attn_grad": 9, "project": 5, "moe": 300, "expert_grad": 1, "back": 5, "route": 4}
 
 
 def cost(name):

time: 364 us -> 364 us (level)
  starting transfers between devices: 101 us -> 87.8 us
  waiting for transfers between devices: 43.5 us -> 54.8 us
    ppermute x36, starting transfers between devices: 37.6 us -> 29 us  [to_tensor(): return lax.ppermute(a, 'tensor', [(i, i ^ flip) for i in range(4)])]
    ppermute x36, waiting for transfers between devices: 24.5 us -> 31.6 us  [to_tensor(): return lax.ppermute(a, 'tensor', [(i, i ^ flip) for i in range(4)])]
    ppermute x24, starting transfers between devices: 37.7 us -> 32.9 us  [to_expert(): lax.ppermute(a, 'expert', [(i, (i + shift) % size) for i in range(size)])]
    ppermute x24, waiting for transfers between devices: 19 us -> 23.2 us  [to_expert(): lax.ppermute(a, 'expert', [(i, (i + shift) % size) for i in range(size)])]
  transfers between devices with their start and end apart: 68 -> 68, of which waited for: 10 -> 13; matrix products, arithmetic and copies ran while one was open for 1% -> 1% of each run, Pallas kernels for 52% -> 51%
where the time goes in v5:
time: 364 us; the launch traced here: 359 us
  Pallas kernels  192 us (53%)
  starting transfers between devices  87.8 us (24%)
  waiting for transfers between devices  54.8 us (15%)
  local copies, waits for them, and re-layouts  21.4 us (6%)
    pallas_call x23, Pallas kernels, call(): pl.pallas_call(body, out_shape=tuple(outs), in_specs=[SM] * smem + [VM] *...  98 us
    pallas_call x8, Pallas kernels, expert_grad(): pl.pallas_call(functools.partial(expert_grad_kernel, steps), grid=(part,...  54.4 us
    pallas_call x2, Pallas kernels, moe(): pl.pallas_call(functools.partial(moe_kernel, rows, part, first, last, len...  39.4 us
    ppermute x24, starting transfers between devices, to_expert(): lax.ppermute(a, 'expert', [(i, (i + shift) % size) for i in range(size)])  32.9 us
    ppermute x36, waiting for transfers between devices, to_tensor(): return lax.ppermute(a, 'tensor', [(i, i ^ flip) for i in range(4)])  31.6 us
    ppermute x36, starting transfers between devices, to_tensor(): return lax.ppermute(a, 'tensor', [(i, i ^ flip) for i in range(4)])  29 us
    ppermute x8, starting transfers between devices, to_core(): return lax.ppermute(a, 'rep', [(0, 1), (1, 0)])  25.8 us
    ppermute x24, waiting for transfers between devices, to_expert(): lax.ppermute(a, 'expert', [(i, (i + shift) % size) for i in range(size)])  23.2 us
  transfers between devices with their start and end apart: 68, of which 13 were waited for; matrix products, arithmetic and copies ran while one was open for 1% of the time, Pallas kernels for 51%

profile of v5, /device:TPU:1, one launch (start us, length us, event | category | flops | bytes accessed | tf_op | source)
XLA Modules:
  0.0 358.7 jit_solution(3843308787986235814)
XLA Ops:
  3.3 4.2 %collective-permute-start.2 = (bf16[96,896]{1,0:T(8,128)(2,1)}, bf16[96,896]{1,0:T(8,128)(2,1)S(1)}, u32[]{:S(2)}, u32[]{:S(2)}) collective-permute-start(bf16[96,896]{1,0:T(8,128)(2,1)} %get-tuple-element.123.refs_3_.refs_1_), channel_id=1, source_target_pairs={{0,24},{8,0},{16,8},{24,16},{1,25},{9,1},{17,9},{25,17},{2,26},{10... | collective-permute-start | bytes 516104 | tf_op jit(solution)/shard_map/ppermute | solution.py:76
  36.3 4.5 %project.1 = (bf16[1024,768]{1,0:T(8,128)(2,1)}, bf16[1024,576]{1,0:T(8,128)(2,1)}) custom-call(s32[3]{0:T(128)} %pad_add_fusion.refs_0_.at_ref, bf16[256,768]{1,0:T(8,128)(2,1)} %bitcast.20, bf16[256,768]{1,0:T(8,128)(2,1)} %copy-done.14, bf16[256,768]{1,0:T(8,128)(2,1)} %copy-done.13, bf16[128,768]{1,0:T(8,128)(2,1)} %copy-done.50, ...), custom_call_target="tpu_custom_call" | custom-call | flops 5750000128 | bytes 1000 | tf_op jit(solution)/shard_map/project/pallas_call | solution.py:48
  40.7 12.3 %attn_fwd.1 = (bf16[1024,192]{1,0:T(8,128)(2,1)}, f32[1024,3]{1,0:T(8,128)}, bf16[256,768]{1,0:T(8,128)(2,1)}, bf16[256,768]{1,0:T(8,128)(2,1)}, bf16[256,768]{1,0:T(8,128)(2,1)}, /*index=5*/bf16[256,768]{1,0:T(8,128)(2,1)}) custom-call(s32[3]{0:T(128)} %pad_add_fusion.refs_0_.at_ref, f32[32,128]{1,0:T(8,128)} %get-tuple-element.126.refs_1_, ...), custom_call_target="tpu_custom_call" | custom-call | flops 14949999616 | bytes 1000 | tf_op jit(solution)/shard_map/attn_fwd/pallas_call | solution.py:48
  61.2 10.4 %collective-permute-done.14.refs_0_ = bf16[256,768]{1,0:T(8,128)(2,1)S(1)} collective-permute-done((bf16[256,768]{1,0:T(8,128)(2,1)}, bf16[256,768]{1,0:T(8,128)(2,1)S(1)}, u32[]{:S(2)}, u32[]{:S(2)}) %collective-permute-start.14) | collective-permute-done | bytes 393248 | tf_op jit(solution)/shard_map/ppermute | solution.py:72
  84.7 8.4 %collective-permute-done.17.refs_3_ = bf16[112,768]{1,0:T(8,128)(2,1)S(1)} collective-permute-done((bf16[112,768]{1,0:T(8,128)(2,1)}, bf16[112,768]{1,0:T(8,128)(2,1)S(1)}, u32[]{:S(2)}, u32[]{:S(2)}) %collective-permute-start.17) | collective-permute-done | bytes 172064 | tf_op jit(solution)/shard_map/ppermute | solution.py:76
  99.0 4.9 %collective-permute-done.23.refs_3_.g_px = bf16[768,768]{1,0:T(8,128)(2,1)S(1)} collective-permute-done((bf16[768,768]{1,0:T(8,128)(2,1)}, bf16[768,768]{1,0:T(8,128)(2,1)S(1)}, u32[]{:S(2)}, u32[]{:S(2)}) %collective-permute-start.23) | collective-permute-done | bytes 1179680 | tf_op jit(solution)/shard_map/ppermute | solution.py:72
  108.7 8.3 %collective-permute-done.20.py.e_py = bf16[400,768]{1,0:T(8,128)(2,1)S(1)} collective-permute-done((bf16[400,768]{1,0:T(8,128)(2,1)}, bf16[400,768]{1,0:T(8,128)(2,1)S(1)}, u32[]{:S(2)}, u32[]{:S(2)}) %collective-permute-start.20) | collective-permute-done | bytes 614432 | tf_op jit(solution)/shard_map/ppermute | solution.py:72
  130.9 6.9 %collective-permute-done.21.d0 = bf16[192,768]{1,0:T(8,128)(2,1)S(1)} collective-permute-done((bf16[192,768]{1,0:T(8,128)(2,1)S(1)}, bf16[192,768]{1,0:T(8,128)(2,1)S(1)}, u32[]{:S(2)}, u32[]{:S(2)}) %collective-permute-start.21) | collective-permute-done | bytes 294944 | tf_op jit(solution)/shard_map/ppermute | solution.py:72
  139.4 19.4 %moe.2 = (bf16[384,768]{1,0:T(8,128)(2,1)}, bf16[384,768]{1,0:T(8,128)(2,1)}, bf16[384,768]{1,0:T(8,128)(2,1)}, bf16[384,768]{1,0:T(8,128)(2,1)}, bf16[384,768]{...) custom-call(s32[3]{0:T(128)} %pad_add_fusion.refs_0_.at_ref, ...), custom_call_target="tpu_custom_call" | custom-call | flops 344999985152 | bytes 1000 | tf_op jit(solution)/shard_map/moe/pallas_call | solution.py:658
  161.5 8.2 %collective-permute-start.33 = (bf16[4,8,4,48,768]{4,3,2,1,0:T(8,128)(2,1)}, bf16[4,8,4,48,768]{4,3,2,1,0:T(8,128)(2,1)}, u32[]{:S(2)}, u32[]{:S(2)}) collective-permute-start(bf16[4,8,4,48,768]{4,3,2,1,0:T(8,128)(2,1)} %get-tuple-element.155.mine), channel_id=1, source_target_pairs={{0,1},{1,0},{2,3},{3,2},{4,5},{5,4},{6,7},{7,6},{8,9},{9,8},{10,11... | collective-permute-start | bytes 28311560 | tf_op jit(solution)/shard_map/ppermute | solution.py:80
  169.8 20.0 %moe.3 = (bf16[400,768]{1,0:T(8,128)(2,1)}, bf16[400,768]{1,0:T(8,128)(2,1)}, bf16[400,768]{1,0:T(8,128)(2,1)}, bf16[400,768]{1,0:T(8,128)(2,1)}, bf16[384,768]{...) custom-call(s32[3]{0:T(128)} %pad_add_fusion.refs_0_.at_ref, ...), custom_call_target="tpu_custom_call" | custom-call | flops 344999985152 | bytes 1000 | tf_op jit(solution)/shard_map/moe/pallas_call | solution.py:658
  204.8 6.7 %expert_grad.8 = (f32[16,768,768]{2,1,0:T(8,128)}, f32[16,768,768]{2,1,0:T(8,128)}, f32[8,128]{1,0:T(8,128)}) custom-call(s32[3]{0:T(128)} %pad_add_fusion.refs_0_.at_ref, bf16[4,8,4,48,768]{4,3,2,1,0:T(8,128)(2,1)} %get-tuple-element.155.mine, bf16[4,8,4,48,768]{4,3,2,1,0:T(8,128)(2,1)} %collective-permute-done.33.other, ...), custom_call_target="tpu_custom_call" | custom-call | flops 1150000000 | bytes 1000 | tf_op jit(solution)/shard_map/expert_grad/pallas_call | solution.py:700
  212.2 6.7 %expert_grad.9 = (f32[16,768,768]{2,1,0:T(8,128)}, f32[16,768,768]{2,1,0:T(8,128)}, f32[8,128]{1,0:T(8,128)}) custom-call(s32[3]{0:T(128)} %pad_add_fusion.refs_0_.at_ref, bf16[4,8,4,48,768]{4,3,2,1,0:T(8,128)(2,1)} %get-tuple-element.155.mine, ...), custom_call_target="tpu_custom_call", output_to_operand_aliasing={{0}: (3, {}), {1}: (4, {})} | custom-call | flops 1150000000 | bytes 1000 | tf_op jit(solution)/shard_map/expert_grad/pallas_call | solution.py:700
  228.9 6.7 %expert_grad.10 = (f32[16,768,768]{2,1,0:T(8,128)}, f32[16,768,768]{2,1,0:T(8,128)}, f32[8,128]{1,0:T(8,128)}) custom-call(s32[3]{0:T(128)} %pad_add_fusion.refs_0_.at_ref, bf16[4,8,4,48,768]{4,3,2,1,0:T(8,128)(2,1)} %get-tuple-element.155.mine, ...), custom_call_target="tpu_custom_call", output_to_operand_aliasing={{0}: (3, {}), {1}: (4, {})} | custom-call | flops 1150000000 | bytes 1000 | tf_op jit(solution)/shard_map/expert_grad/pallas_call | solution.py:700
  237.2 4.9 %back.1 = (f32[256,768]{1,0:T(8,128)}, bf16[256,768]{1,0:T(8,128)(2,1)}, bf16[768,128]{1,0:T(8,128)(2,1)}) custom-call(s32[256,8]{1,0:T(8,128)} %prepare.1.refs_0_, bf16[256,768]{1,0:T(8,128)(2,1)} %bitcast.25, f32[256,768]{1,0:T(8,128)} %get-tuple-element.140.refs_2_.refs_1_, bf16[256,768]{1,0:T(8,128)(2,1)} %get-tuple-element.146.refs_1_.refs_3_, ...), custom_call_target="tpu_custom_call" | custom-call | flops 5750000128 | bytes 1000 | tf_op jit(solution)/shard_map/back/pallas_call | solution.py:48
  244.7 6.9 %expert_grad.11 = (f32[16,768,768]{2,1,0:T(8,128)}, f32[16,768,768]{2,1,0:T(8,128)}, f32[8,128]{1,0:T(8,128)}) custom-call(s32[3]{0:T(128)} %pad_add_fusion.refs_0_.at_ref, bf16[4,8,4,48,768]{4,3,2,1,0:T(8,128)(2,1)} %get-tuple-element.155.mine, ...), custom_call_target="tpu_custom_call", output_to_operand_aliasing={{0}: (3, {}), {1}: (4, {})} | custom-call | flops 1150000000 | bytes 1000 | tf_op jit(solution)/shard_map/expert_grad/pallas_call | solution.py:700
  251.7 8.5 %collective-permute-start.54 = (bf16[4,8,4,48,768]{4,3,2,1,0:T(8,128)(2,1)}, bf16[4,8,4,48,768]{4,3,2,1,0:T(8,128)(2,1)}, u32[]{:S(2)}, u32[]{:S(2)}) collective-permute-start(bf16[4,8,4,48,768]{4,3,2,1,0:T(8,128)(2,1)} %after.31.mine), channel_id=1, source_target_pairs={{0,1},{1,0},{2,3},{3,2},{4,5},{5,4},{6,7},{7,6},{8,9},{9,8},{10,11... | collective-permute-start | bytes 28311560 | tf_op jit(solution)/shard_map/ppermute | solution.py:80
  266.0 18.0 %attn_bwd.1 = (f32[4,8,128]{2,1,0:T(8,128)}, bf16[1024,576]{1,0:T(8,128)(2,1)}) custom-call(s32[3]{0:T(128)} %pad_add_fusion.refs_0_.at_ref, f32[32,128]{1,0:T(8,128)} %get-tuple-element.126.refs_1_, bf16[256,768]{1,0:T(8,128)(2,1)} %get-tuple-element.185.refs_2_.refs_4_, bf16[256,768]{1,0:T(8,128)(2,1)} %copy-done.41, bf16[256,768]{1,0:T(8,128)(2,1)} %copy-done.40, ...), custom_call_target="tpu_custom_call" | custom-call | flops 460000002048 | bytes 1000 | tf_op jit(solution)/shard_map/attn_bwd/pallas_call | solution.py:48
  284.1 7.4 %attn_grad.1 = (bf16[4,96,896]{2,1,0:T(8,128)(2,1)}, bf16[4,96,896]{2,1,0:T(8,128)(2,1)}, bf16[256,768]{1,0:T(8,128)(2,1)}, bf16[256,768]{1,0:T(8,128)(2,1)}, bf...) custom-call(s32[3]{0:T(128)} %pad_add_fusion.refs_0_.at_ref, bf16[1024,576]{1,0:T(8,128)(2,1)} %get-tuple-element.190.refs_1_, ...), custom_call_target="tpu_custom_call" | custom-call | flops 10350000128 | bytes 1000 | tf_op jit(solution)/shard_map/attn_grad/pallas_call | solution.py:48
  301.0 4.2 %give_back_y.1 = (bf16[192,768]{1,0:T(8,128)(2,1)}, bf16[192,768]{1,0:T(8,128)(2,1)}, bf16[192,768]{1,0:T(8,128)(2,1)}, bf16[192,768]{1,0:T(8,128)(2,1)}) custom-call(bf16[384,384]{1,0:T(8,128)(2,1)} %constant.17.clone.refs_0_, bf16[384,768]{1,0:T(8,128)(2,1)} %get-tuple-element.151.refs_1_, bf16[384,768]{1,0:T(8,128)(2,1)} %get-tuple-element.153.refs_2_, ...), custom_call_target="tpu_custom_call" | custom-call | flops 575000000 | bytes 1000 | tf_op jit(solution)/shard_map/give_back_y/pallas_call | solution.py:48
  308.5 6.8 %expert_grad.12 = (f32[16,768,768]{2,1,0:T(8,128)}, f32[16,768,768]{2,1,0:T(8,128)}, f32[8,128]{1,0:T(8,128)}) custom-call(s32[3]{0:T(128)} %pad_add_fusion.refs_0_.at_ref, bf16[4,8,4,48,768]{4,3,2,1,0:T(8,128)(2,1)} %after.31.mine, bf16[4,8,4,48,768]{4,3,2,1,0:T(8,128)(2,1)} %collective-permute-done.54.refs_3_.other, ...), custom_call_target="tpu_custom_call", output_to_operand_aliasing={{0}: (3, {}), {1}: (4, {})} | custom-call | flops 1150000000 | bytes 1000 | tf_op jit(solution)/shard_map/expert_grad/pallas_call | solution.py:700
  317.1 6.8 %expert_grad.13 = (f32[16,768,768]{2,1,0:T(8,128)}, f32[16,768,768]{2,1,0:T(8,128)}, f32[8,128]{1,0:T(8,128)}) custom-call(s32[3]{0:T(128)} %pad_add_fusion.refs_0_.at_ref, bf16[4,8,4,48,768]{4,3,2,1,0:T(8,128)(2,1)} %after.31.mine, bf16[4,8,4,48,768]{4,3,2,1,0:T(8,128)(2,1)} %collective-permute-done.54.refs_3_.other, ...), custom_call_target="tpu_custom_call", output_to_operand_aliasing={{0}: (3, {}), {1}: (4, {})} | custom-call | flops 1150000000 | bytes 1000 | tf_op jit(solution)/shard_map/expert_grad/pallas_call | solution.py:700
  335.3 7.0 %expert_grad.14 = (f32[16,768,768]{2,1,0:T(8,128)}, f32[16,768,768]{2,1,0:T(8,128)}, f32[8,128]{1,0:T(8,128)}) custom-call(s32[3]{0:T(128)} %pad_add_fusion.refs_0_.at_ref, bf16[4,8,4,48,768]{4,3,2,1,0:T(8,128)(2,1)} %after.31.mine, bf16[4,8,4,48,768]{4,3,2,1,0:T(8,128)(2,1)} %collective-permute-done.54.refs_3_.other, ...), custom_call_target="tpu_custom_call", output_to_operand_aliasing={{0}: (3, {}), {1}: (4, {})} | custom-call | flops 1150000000 | bytes 1000 | tf_op jit(solution)/shard_map/expert_grad/pallas_call | solution.py:700
  342.9 6.7 %expert_grad.15 = (f32[16,768,768]{2,1,0:T(8,128)}, f32[16,768,768]{2,1,0:T(8,128)}, f32[8,128]{1,0:T(8,128)}) custom-call(s32[3]{0:T(128)} %pad_add_fusion.refs_0_.at_ref, bf16[4,8,4,48,768]{4,3,2,1,0:T(8,128)(2,1)} %after.31.mine, bf16[4,8,4,48,768]{4,3,2,1,0:T(8,128)(2,1)} %collective-permute-done.54.refs_3_.other, ...), custom_call_target="tpu_custom_call", output_to_operand_aliasing={{0}: (3, {}), {1}: (4, {})} | custom-call | flops 1150000000 | bytes 1000 | tf_op jit(solution)/shard_map/expert_grad/pallas_call | solution.py:700
  (296 shorter events, 152.3 us)
Async XLA Ops:
  27.2 27.3 %collective-permute-start.12 = (bf16[192,768]{1,0:T(8,128)(2,1)}, bf16[192,768]{1,0:T(8,128)(2,1)S(1)}, u32[]{:S(2)}, u32[]{:S(2)}) collective-permute-start(bf16[192,768]{1,0:T(8,128)(2,1)} %after.21.refs_10_), channel_id=1, source_target_pairs={{0,24},{8,0},{16,8},{24,16},{1,25},{9,1},{17,9},{25,17},{2,26},{10... | collective-permute-start | bytes 884744 | tf_op jit(solution)/shard_map/ppermute | solution.py:76
  27.9 29.1 %collective-permute-start.11 = (bf16[192,768]{1,0:T(8,128)(2,1)}, bf16[192,768]{1,0:T(8,128)(2,1)S(1)}, u32[]{:S(2)}, u32[]{:S(2)}) collective-permute-start(bf16[192,768]{1,0:T(8,128)(2,1)} %after.20.refs_9_), channel_id=1, source_target_pairs={{0,16},{8,24},{16,0},{24,8},{1,17},{9,25},{17,1},{25,9},{2,18},{10... | collective-permute-start | bytes 884744 | tf_op jit(solution)/shard_map/ppermute | solution.py:76
  31.0 25.9 %collective-permute-start.10 = (bf16[192,768]{1,0:T(8,128)(2,1)}, bf16[192,768]{1,0:T(8,128)(2,1)S(1)}, u32[]{:S(2)}, u32[]{:S(2)}) collective-permute-start(bf16[192,768]{1,0:T(8,128)(2,1)} %after.19.refs_8_), channel_id=1, source_target_pairs={{0,8},{8,16},{16,24},{24,0},{1,9},{9,17},{17,25},{25,1},{2,10},{10... | collective-permute-start | bytes 884744 | tf_op jit(solution)/shard_map/ppermute | solution.py:76
  77.9 26.0 %collective-permute-start.23 = (bf16[768,768]{1,0:T(8,128)(2,1)}, bf16[768,768]{1,0:T(8,128)(2,1)S(1)}, u32[]{:S(2)}, u32[]{:S(2)}) collective-permute-start(bf16[768,768]{1,0:T(8,128)(2,1)} %after.25.g_own), channel_id=1, source_target_pairs={{0,2},{2,0},{4,6},{6,4},{1,3},{3,1},{5,7},{7,5},{8,10},{10,8},{12,... | collective-permute-start | bytes 3538952 | tf_op jit(solution)/shard_map/ppermute | solution.py:72
  78.2 25.9 %collective-permute-start.24 = (bf16[768,768]{1,0:T(8,128)(2,1)}, bf16[768,768]{1,0:T(8,128)(2,1)S(1)}, u32[]{:S(2)}, u32[]{:S(2)}) collective-permute-start(bf16[768,768]{1,0:T(8,128)(2,1)} %after.25.g_own), channel_id=1, source_target_pairs={{0,4},{2,6},{4,0},{6,2},{1,5},{3,7},{5,1},{7,3},{8,12},{10,14},{12... | collective-permute-start | bytes 3538952 | tf_op jit(solution)/shard_map/ppermute | solution.py:72
  104.0 34.6 %collective-permute-start.25 = (bf16[384,768]{1,0:T(8,128)(2,1)S(1)}, bf16[384,768]{1,0:T(8,128)(2,1)S(1)}, u32[]{:S(2)}, u32[]{:S(2)}) collective-permute-start(bf16[384,768]{1,0:T(8,128)(2,1)S(1)} %slice.28), channel_id=1, source_target_pairs={{0,4},{2,6},{4,0},{6,2},{1,5},{3,7},{5,1},{7,3},{8,12},{10,14},{12... | collective-permute-start | bytes 1769480 | tf_op jit(solution)/shard_map/ppermute | solution.py:72
  125.2 34.4 %collective-permute-start.32 = (bf16[384,768]{1,0:T(8,128)(2,1)}, bf16[384,768]{1,0:T(8,128)(2,1)}, u32[]{:S(2)}, u32[]{:S(2)}) collective-permute-start(bf16[384,768]{1,0:T(8,128)(2,1)} %slice.29), channel_id=1, source_target_pairs={{0,2},{2,0},{4,6},{6,4},{1,3},{3,1},{5,7},{7,5},{8,10},{10,8},{12,... | collective-permute-start | bytes 1769480 | tf_op jit(solution)/shard_map/ppermute | solution.py:72
  128.6 32.4 %collective-permute-start.31 = (bf16[384,768]{1,0:T(8,128)(2,1)}, bf16[384,768]{1,0:T(8,128)(2,1)}, u32[]{:S(2)}, u32[]{:S(2)}) collective-permute-start(bf16[384,768]{1,0:T(8,128)(2,1)} %order.3.refs_0_.own), channel_id=1, source_target_pairs={{0,6},{2,4},{4,2},{6,0},{1,7},{3,5},{5,3},{7,1},{8,14},{10,12},{12... | collective-permute-start | bytes 1769480 | tf_op jit(solution)/shard_map/ppermute | solution.py:72
  137.8 32.0 %collective-permute-start.29 = (bf16[384,768]{1,0:T(8,128)(2,1)}, bf16[384,768]{1,0:T(8,128)(2,1)}, u32[]{:S(2)}, u32[]{:S(2)}) collective-permute-start(bf16[384,768]{1,0:T(8,128)(2,1)} %order.3.refs_0_.own), channel_id=1, source_target_pairs={{0,2},{2,0},{4,6},{6,4},{1,3},{3,1},{5,7},{7,5},{8,10},{10,8},{12,... | collective-permute-start | bytes 1769480 | tf_op jit(solution)/shard_map/ppermute | solution.py:72
  158.8 31.0 %collective-permute-start.34 = (bf16[384,768]{1,0:T(8,128)(2,1)}, bf16[384,768]{1,0:T(8,128)(2,1)}, u32[]{:S(2)}, u32[]{:S(2)}) collective-permute-start(bf16[384,768]{1,0:T(8,128)(2,1)} %get-tuple-element.157), channel_id=1, source_target_pairs={{0,2},{2,0},{4,6},{6,4},{1,3},{3,1},{5,7},{7,5},{8,10},{10,8},{12,... | collective-permute-start | bytes 1769480 | tf_op jit(solution)/shard_map/ppermute | solution.py:72
  159.7 30.2 %collective-permute-start.35 = (bf16[384,768]{1,0:T(8,128)(2,1)}, bf16[384,768]{1,0:T(8,128)(2,1)}, u32[]{:S(2)}, u32[]{:S(2)}) collective-permute-start(bf16[384,768]{1,0:T(8,128)(2,1)} %get-tuple-element.158), channel_id=1, source_target_pairs={{0,4},{2,6},{4,0},{6,2},{1,5},{3,7},{5,1},{7,3},{8,12},{10,14},{12... | collective-permute-start | bytes 1769480 | tf_op jit(solution)/shard_map/ppermute | solution.py:72
  161.1 28.8 %collective-permute-start.36 = (bf16[384,768]{1,0:T(8,128)(2,1)}, bf16[384,768]{1,0:T(8,128)(2,1)}, u32[]{:S(2)}, u32[]{:S(2)}) collective-permute-start(bf16[384,768]{1,0:T(8,128)(2,1)} %get-tuple-element.159), channel_id=1, source_target_pairs={{0,6},{2,4},{4,2},{6,0},{1,7},{3,5},{5,3},{7,1},{8,14},{10,12},{12... | collective-permute-start | bytes 1769480 | tf_op jit(solution)/shard_map/ppermute | solution.py:72
  161.5 40.2 %collective-permute-start.33 = (bf16[4,8,4,48,768]{4,3,2,1,0:T(8,128)(2,1)}, bf16[4,8,4,48,768]{4,3,2,1,0:T(8,128)(2,1)}, u32[]{:S(2)}, u32[]{:S(2)}) collective-permute-start(bf16[4,8,4,48,768]{4,3,2,1,0:T(8,128)(2,1)} %get-tuple-element.155.mine), channel_id=1, source_target_pairs={{0,1},{1,0},{2,3},{3,2},{4,5},{5,4},{6,7},{7,6},{8,9},{9,8},{10,11... | collective-permute-start | bytes 28311560 | tf_op jit(solution)/shard_map/ppermute | solution.py:80
  189.9 29.1 %collective-permute-start.40 = (bf16[400,768]{1,0:T(8,128)(2,1)}, bf16[400,768]{1,0:T(8,128)(2,1)S(1)}, u32[]{:S(2)}, u32[]{:S(2)}) collective-permute-start(bf16[400,768]{1,0:T(8,128)(2,1)} %after.26), channel_id=1, source_target_pairs={{0,2},{2,0},{4,6},{6,4},{1,3},{3,1},{5,7},{7,5},{8,10},{10,8},{12,... | collective-permute-start | bytes 1843208 | tf_op jit(solution)/shard_map/ppermute | solution.py:72
  190.7 28.2 %collective-permute-start.41 = (bf16[400,768]{1,0:T(8,128)(2,1)}, bf16[400,768]{1,0:T(8,128)(2,1)S(1)}, u32[]{:S(2)}, u32[]{:S(2)}) collective-permute-start(bf16[400,768]{1,0:T(8,128)(2,1)} %after.27), channel_id=1, source_target_pairs={{0,4},{2,6},{4,0},{6,2},{1,5},{3,7},{5,1},{7,3},{8,12},{10,14},{12... | collective-permute-start | bytes 1843208 | tf_op jit(solution)/shard_map/ppermute | solution.py:72
  192.4 26.6 %collective-permute-start.42 = (bf16[400,768]{1,0:T(8,128)(2,1)}, bf16[400,768]{1,0:T(8,128)(2,1)S(1)}, u32[]{:S(2)}, u32[]{:S(2)}) collective-permute-start(bf16[400,768]{1,0:T(8,128)(2,1)} %after.28), channel_id=1, source_target_pairs={{0,6},{2,4},{4,2},{6,0},{1,7},{3,5},{5,3},{7,1},{8,14},{10,12},{12... | collective-permute-start | bytes 1843208 | tf_op jit(solution)/shard_map/ppermute | solution.py:72
  220.2 31.4 %collective-permute-start.43 = (bf16[2,384,768]{2,1,0:T(8,128)(2,1)}, bf16[2,384,768]{2,1,0:T(8,128)(2,1)S(1)}, u32[]{:S(2)}, u32[]{:S(2)}) collective-permute-start(bf16[2,384,768]{2,1,0:T(8,128)(2,1)} %after.29.refs_17_), channel_id=1, source_target_pairs={{0,2},{2,0},{4,6},{6,4},{1,3},{3,1},{5,7},{7,5},{8,10},{10,8},{12,... | collective-permute-start | bytes 3538952 | tf_op jit(solution)/shard_map/ppermute | solution.py:72
  220.9 39.2 %collective-permute-start.44 = (bf16[2,384,768]{2,1,0:T(8,128)(2,1)}, bf16[2,384,768]{2,1,0:T(8,128)(2,1)S(1)}, u32[]{:S(2)}, u32[]{:S(2)}) collective-permute-start(bf16[2,384,768]{2,1,0:T(8,128)(2,1)} %after.30.refs_18_), channel_id=1, source_target_pairs={{0,4},{2,6},{4,0},{6,2},{1,5},{3,7},{5,1},{7,3},{8,12},{10,14},{12... | collective-permute-start | bytes 3538952 | tf_op jit(solution)/shard_map/ppermute | solution.py:72
  251.7 46.3 %collective-permute-start.54 = (bf16[4,8,4,48,768]{4,3,2,1,0:T(8,128)(2,1)}, bf16[4,8,4,48,768]{4,3,2,1,0:T(8,128)(2,1)}, u32[]{:S(2)}, u32[]{:S(2)}) collective-permute-start(bf16[4,8,4,48,768]{4,3,2,1,0:T(8,128)(2,1)} %after.31.mine), channel_id=1, source_target_pairs={{0,1},{1,0},{2,3},{3,2},{4,5},{5,4},{6,7},{7,6},{8,9},{9,8},{10,11... | collective-permute-start | bytes 28311560 | tf_op jit(solution)/shard_map/ppermute | solution.py:80
  301.0 24.3 %collective-permute-start.62 = (bf16[96,896]{1,0:T(8,128)(2,1)}, bf16[96,896]{1,0:T(8,128)(2,1)S(1)}, u32[]{:S(2)}, u32[]{:S(2)}) collective-permute-start(bf16[96,896]{1,0:T(8,128)(2,1)} %get-tuple-element.213), channel_id=1, source_target_pairs={{0,16},{8,24},{16,0},{24,8},{1,17},{9,25},{17,1},{25,9},{2,18},{10... | collective-permute-start | bytes 516104 | tf_op jit(solution)/shard_map/ppermute | solution.py:76
  315.4 35.4 %collective-permute-start.55 = (bf16[192,768]{1,0:T(8,128)(2,1)S(1)}, bf16[192,768]{1,0:T(8,128)(2,1)S(1)}, u32[]{:S(2)}, u32[]{:S(2)}) collective-permute-start(bf16[192,768]{1,0:T(8,128)(2,1)S(1)} %copy-done.47), channel_id=1, source_target_pairs={{0,24},{8,0},{16,8},{24,16},{1,25},{9,1},{17,9},{25,17},{2,26},{10... | collective-permute-start | bytes 884744 | tf_op jit(solution)/shard_map/ppermute | solution.py:76
  315.7 35.1 %collective-permute-start.56 = (bf16[192,768]{1,0:T(8,128)(2,1)S(1)}, bf16[192,768]{1,0:T(8,128)(2,1)S(1)}, u32[]{:S(2)}, u32[]{:S(2)}) collective-permute-start(bf16[192,768]{1,0:T(8,128)(2,1)S(1)} %copy-done.46), channel_id=1, source_target_pairs={{0,16},{8,24},{16,0},{24,8},{1,17},{9,25},{17,1},{25,9},{2,18},{10... | collective-permute-start | bytes 884744 | tf_op jit(solution)/shard_map/ppermute | solution.py:76
  323.9 26.9 %collective-permute-start.57 = (bf16[192,768]{1,0:T(8,128)(2,1)S(1)}, bf16[192,768]{1,0:T(8,128)(2,1)S(1)}, u32[]{:S(2)}, u32[]{:S(2)}) collective-permute-start(bf16[192,768]{1,0:T(8,128)(2,1)S(1)} %copy-done.45), channel_id=1, source_target_pairs={{0,8},{8,16},{16,24},{24,0},{1,9},{9,17},{17,25},{25,1},{2,10},{10... | collective-permute-start | bytes 884744 | tf_op jit(solution)/shard_map/ppermute | solution.py:76
  328.4 26.5 %collective-permute-start.65 = (f32[96,896]{1,0:T(8,128)}, f32[96,896]{1,0:T(8,128)S(1)}, u32[]{:S(2)}, u32[]{:S(2)}) collective-permute-start(f32[96,896]{1,0:T(8,128)} %get-tuple-element.216.refs_2_.refs_1_), channel_id=1, source_target_pairs={{0,1},{1,0},{2,3},{3,2},{4,5},{5,4},{6,7},{7,6},{8,9},{9,8},{10,11... | collective-permute-start | bytes 1032200 | tf_op jit(solution)/shard_map/ppermute | solution.py:80
  (106 other events, 807.8 us)
